TPU v7x, 256 devices: a whole 4x4x8 slice. The times are simulated.
256 devices in a mesh: node: 16 (over y, z_lo), local: 16 (over z_hi, x, core).
Axes of the slice: x: 4, y: 4, z: 8 (z_hi: 2, z_lo: 4; z = z_hi * 4 + z_lo), core: 2. Of those that a mesh axis runs over, the one named last changes fastest.
Arguments:
- hidden: bfloat16 [6144, 11264], P('node', 'local'), may hold values from -6 to 6
- codes: bfloat16 [11264, 8192], P('local', 'node'), may hold values from -127 to 127, as said below
- scales: float32 [11264, 32], P('local', 'node'), may hold values from 4e-05 to 0.0004
- upstream: bfloat16 [6144, 8192], P('node', 'local'), may hold values from -6 to 6
Outputs:
- mixed: bfloat16 [6144, 8192], P('node', 'local')
- hidden_grad: bfloat16 [6144, 11264], P('node', 'local')
- weight_grad: float32 [11264, 8192], P('local', 'node')
Inputs may be any that keep to these rules, and one draw needn't show every extreme that they name: codes are whole numbers.
All inputs are finite; a program needn't handle non-finite values.
Results may differ from a plain program's by a relative error of at most 0.023.
Values may be sent and summed in bfloat16 or wider, within the bound.
No kernel may reach another device: no remote copies, remote signals or barrier semaphores. Data moves between devices by JAX's collectives and lax.ppermute only.
A program may use at most 128 MiB of HBM per device.

v0:
```python
import math

import jax
import jax.numpy as jnp
from jax import lax
from jax.sharding import PartitionSpec as P

BLOCK = 256


def on_whole(array, axis, dim, block):
    whole = lax.all_gather(array, axis, axis=dim, tiled=True)
    return block(whole, jnp.int32(0))


def dequantize(code_block, scale_block):
    return (code_block.astype(jnp.float32) * jnp.repeat(scale_block, BLOCK, axis=1)).astype(
        jnp.bfloat16
    )


def local(hidden, codes, scales, upstream):
    node_count = lax.axis_size("node")
    tok_rows = hidden.shape[0]
    factor = 1.0 / math.sqrt(tok_rows * node_count)
    cot_rows = lax.all_gather(upstream, "local", axis=1, tiled=True)

    def expand(pieces):
        return dequantize(pieces[0], pieces[1])

    weight_full = on_whole(
        (codes, scales.astype(jnp.bfloat16)),
        "node",
        1,
        lambda piece, start: expand((piece[0], piece[1].astype(jnp.float32))),
    )
    terms = jnp.dot(hidden, weight_full, preferred_element_type=jnp.float32)
    hidden_grad = lax.dot_general(
        cot_rows, weight_full, (((1,), (1,)), ((), ())), preferred_element_type=jnp.float32
    ).astype(jnp.bfloat16)
    local_grad = (
        lax.dot_general(
            hidden, cot_rows, (((0,), (0,)), ((), ())), preferred_element_type=jnp.float32
        )
        * factor
    )
    local_grad = lax.optimization_barrier(local_grad.astype(jnp.bfloat16)).astype(jnp.float32)
    weight_grad = lax.psum_scatter(
        local_grad.astype(jnp.bfloat16), "node", scatter_dimension=1, tiled=True
    ).astype(jnp.float32)
    mixed = lax.psum_scatter(terms.astype(jnp.bfloat16), "local", scatter_dimension=1, tiled=True)
    return (mixed, hidden_grad, weight_grad)


def solution(mesh):
    return jax.shard_map(
        local,
        mesh=mesh,
        in_specs=(P("node", "local"), P("local", "node"), P("local", "node"), P("node", "local")),
        out_specs=(P("node", "local"), P("node", "local"), P("local", "node")),
        check_vma=False,
    )
```

profile of v0, /device:TPU:1, one launch (start us, length us, event | category | flops | bytes accessed | tf_op | source)
XLA Modules:
  0.0 740.3 jit_solution(383713853099810855)
XLA Ops:
  7.2 0.0 copy-start
  7.2 0.0 all-gather.4.cloned.1.call-start
  7.2 0.7 all-gather.4.cloned.1.call-update
  7.9 0.0 all-gather.6.cloned.1.call-start
  8.0 0.7 all-gather.6.cloned.1.call-update
  8.7 0.0 reduce-scatter.3.cloned.1.call-start
  8.7 0.7 convert_bitcast_fusion
  9.4 39.8 %all-gather = bf16[16,2,704]{2,1,0:T(2,128)(2,1)S(1)} all-gather(bf16[1,2,704]{2,1,0:T(2,128)(2,1)S(1)} %convert_bitcast_fusion), channel_id=1, replica_groups=mesh['node'=16,'local'=16] {'node'}, dimensions={0}, use_global_device_ids=true | all-gather | bytes 47872 | tf_op jit(solution)/shard_map/all_gather | solution.py:12
  49.2 0.2 copy.9
  49.4 3.6 broadcast_in_dim.3
  53.0 23.6 %copy.11 = f32[88,8,32,256]{3,1,2,0:T(8,128)} copy(f32[88,8,32,256]{3,2,1,0:T(8,128)S(1)} %bitcast.17) | data formatting | bytes 46137344
  76.5 188.2 %all-gather.4.cloned.1.call-done = bf16[704,8192]{1,0:T(8,128)(2,1)} async-done(((bf16[704,512]{1,0:T(8,128)(2,1)}), bf16[704,8192]{1,0:T(8,128)(2,1)}) %all-gather.4.cloned.1.call-update) | async-done | bytes 11534352 | tf_op jit(solution)/shard_map/all_gather | solution.py:12
  264.7 0.0 copy-done
  264.7 17.0 %fusion = bf16[384,8192]{0,1:T(8,128)(2,1)} fusion(bf16[384,704]{0,1:T(8,128)(2,1)S(1)} %copy-done, f32[704,8192]{1,0:T(8,128)} %bitcast.15, bf16[704,8192]{1,0:T(8,128)(2,1)} %all-gather.4.cloned.1.call-done), kind=kOutput, calls=%fused_computation.3 | convolution fusion | flops 4449632256 | bytes 41435136 | tf_op jit(solution)/shard_map/dot_general | solution.py:37
  281.7 0.0 reduce-scatter.3.cloned.1.call-update
  281.7 0.2 reduce-scatter.5.cloned.1.call-start
  282.0 79.9 %all-gather.6.cloned.1.call-done = bf16[384,8192]{1,0:T(8,128)(2,1)} async-done(((bf16[384,512]{1,0:T(8,128)(2,1)}), bf16[384,8192]{1,0:T(8,128)(2,1)}) %all-gather.6.cloned.1.call-update) | async-done | bytes 6291472 | tf_op jit(solution)/shard_map/all_gather | solution.py:26
  361.9 11.7 %multiply_convert_fusion = bf16[704,8192]{1,0:T(8,128)(2,1)} fusion(bf16[384,704]{0,1:T(8,128)(2,1)S(1)} %copy-done, bf16[384,8192]{1,0:T(8,128)(2,1)} %all-gather.6.cloned.1.call-done), kind=kOutput, calls=%fused_computation | convolution fusion | flops 4440719360 | bytes 18366464 | tf_op jit(solution)/shard_map/dot_general | solution.py:42
  373.5 0.0 reduce-scatter.5.cloned.1.call-update
  373.6 19.5 %fusion.1 = bf16[384,704]{0,1:T(8,128)(2,1)} fusion(bf16[384,8192]{1,0:T(8,128)(2,1)} %all-gather.6.cloned.1.call-done, f32[704,8192]{1,0:T(8,128)} %bitcast.16, bf16[704,8192]{1,0:T(8,128)(2,1)} %all-gather.4.cloned.1.call-done), kind=kOutput, calls=%fused_computation.5 | convolution fusion | flops 4446756864 | bytes 41435136 | tf_op jit(solution)/shard_map/dot_general | solution.py:38
  393.1 87.7 %reduce-scatter.3.cloned.1.call-done = bf16[384,512]{0,1:T(8,128)(2,1)} async-done(((bf16[384,8192]{0,1:T(8,128)(2,1)}), bf16[384,512]{0,1:T(8,128)(2,1)}) %reduce-scatter.3.cloned.1.call-update) | async-done | bytes 393232 | tf_op jit(solution)/shard_map/reduce_scatter | solution.py:51
  480.8 1.9 copy.10
  482.7 248.7 %reduce-scatter.5.cloned.1.call-done = bf16[704,512]{1,0:T(8,128)(2,1)} async-done(((bf16[704,8192]{1,0:T(8,128)(2,1)}), bf16[704,512]{1,0:T(8,128)(2,1)}) %reduce-scatter.5.cloned.1.call-update) | async-done | bytes 720912 | tf_op jit(solution)/shard_map/reduce_scatter | solution.py:48
  731.4 2.4 convert_element_type.41
  (1 shorter events, 0.0 us)
Async XLA Ops:
  7.2 257.6 %copy-start = (bf16[384,704]{0,1:T(8,128)(2,1)S(1)}, bf16[384,704]{0,1:T(8,128)(2,1)}, u32[]{:S(2)}) copy-start(bf16[384,704]{0,1:T(8,128)(2,1)} %param.4) | copy-start | bytes 1622020
  7.2 257.6 %all-gather.4.cloned.1.call-start = ((), (), s32[]{:S(2)}) async-start(), calls=%async_computation.2 | async-start | bytes 12255232 | tf_op jit(solution)/shard_map/all_gather | solution.py:12
  7.9 354.0 %all-gather.6.cloned.1.call-start = ((), (), s32[]{:S(2)}) async-start(), calls=%async_computation.4 | async-start | bytes 6684672 | tf_op jit(solution)/shard_map/all_gather | solution.py:26
  8.7 472.1 %reduce-scatter.3.cloned.1.call-start = ((), (), s32[]{:S(2)}) async-start(), calls=%async_computation.3 | async-start | bytes 6684672 | tf_op jit(solution)/shard_map/reduce_scatter | solution.py:51
  281.7 449.6 %reduce-scatter.5.cloned.1.call-start = ((), (), s32[]{:S(2)}) async-start(), calls=%async_computation.5 | async-start | bytes 12255232 | tf_op jit(solution)/shard_map/reduce_scatter | solution.py:48
Sparse Core Ops, SparseCore 0:
  9.8 254.8 all-gather.3
  267.3 94.5 all-gather.5
  366.3 114.3 reduce-scatter.2
  483.2 248.1 reduce-scatter.4
where the time goes:
time: 741 us; the launch traced here: 740 us
  waiting for transfers between devices  606 us (82%)
  matrix products  48.1 us (6%)
  blocking collectives  39.8 us (5%)
  local copies, waits for them, and re-layouts  29.2 us (4%)
  between operations  13.8 us (2%)
    reduce_scatter x1, waiting for transfers between devices, local(): lax.psum_scatter(local_grad.astype(jnp.bfloat16), 'node', scatter_dimensi...  249 us
    all_gather x1, waiting for transfers between devices, on_whole(): whole = lax.all_gather(array, axis, axis=dim, tiled=True)  188 us
    reduce_scatter x1, waiting for transfers between devices, local(): lax.psum_scatter(terms.astype(jnp.bfloat16), 'local', scatter_dimension=1...  87.7 us
    all_gather x1, waiting for transfers between devices, local(): cot_rows = lax.all_gather(upstream, 'local', axis=1, tiled=True)  79.9 us
    all_gather x1, blocking collectives, on_whole(): whole = lax.all_gather(array, axis, axis=dim, tiled=True)  39.8 us
    unnamed x4, local copies, waits for them, and re-layouts  25.5 us
    dot_general x1, matrix products, local(): lax.dot_general(cot_rows, weight_full, (((1,), (1,)), ((), ())), preferre...  19.5 us
    dot_general x1, matrix products, local(): terms = jnp.dot(hidden, weight_full, preferred_element_type=jnp.float32)  17 us
  transfers between devices with their start and end apart: 4, of which 4 were waited for; matrix products, arithmetic and copies ran while one was open for 11% of the time, Pallas kernels for 0%

commit v1 on v0

v1 whole, which is shorter than its diff:
```python
import functools
import math

import jax
import jax.numpy as jnp
from jax import lax
from jax.experimental import pallas as pl
from jax.experimental.pallas import tpu as pltpu
from jax.sharding import Mesh, PartitionSpec as P
import numpy as np

BLOCK = 256
AXES = ("y", "zl", "zh", "x", "c")
DIMS = (4, 4, 2, 4, 2)
VMEM_LIMIT = 50 * 1024 * 1024


def permute(array, target):
    pairs = []
    for index, source in enumerate(np.ndindex(*DIMS)):
        pairs.append((index, int(np.ravel_multi_index(target(*source), DIMS))))
    return lax.ppermute(array, AXES, pairs)


def inverse(target):
    table = {target(*source): source for source in np.ndindex(*DIMS)}
    return lambda *place: table[place]


def along_y(shift):
    return lambda y, zl, zh, x, c: ((y + shift) % 4, zl, zh, x, c)


def along_zl(shift):
    return lambda y, zl, zh, x, c: (y, (zl + shift) % 4, zh, x, c)


def to_plane(other_half):
    def target(y, zl, zh, x, c):
        column = zh * 8 + x * 2 + c
        plane, row = column % 4, column // 4
        return (y, plane, zh ^ other_half, ((row % 2) * 2 + plane // 2 + zl // 2) % 4, zl % 2)

    return target


def slot_of(r, k):
    y, zl, zh = (lax.axis_index(name) for name in ("y", "zl", "zh"))
    tokens = lax.rem(zl - r + 4, 4)
    row = lax.rem(y + k, 4)
    x = lax.rem(lax.rem(row, 2) * 2 + zl // 2 + tokens // 2, 4)
    other_half = jnp.where(row // 2 == zh, 0, 1)
    return (x * 2 + lax.rem(tokens, 2)) * 2 + other_half


def mixed_kernel(h0, h1, h2, h3, w0, w1, w2, w3, out, hs, ws, ob, h_sem, w_sem, o_sem):
    hidden, weights = (h0, h1, h2, h3), (w0, w1, w2, w3)
    for i in range(4):
        pltpu.make_async_copy(hidden[i], hs.at[i], h_sem.at[i]).start()
        pltpu.make_async_copy(weights[i], ws.at[i], w_sem.at[i]).start()
    for i in range(4):
        pltpu.make_async_copy(weights[i], ws.at[i], w_sem.at[i]).wait()
        pltpu.make_async_copy(hidden[i], hs.at[i], h_sem.at[i]).wait()

    def rows(r, _):
        block = hs[r].T

        def columns(k, _):
            ob[r * 4 + k] = jnp.dot(block, ws[k], preferred_element_type=jnp.float32).astype(jnp.bfloat16)
            pltpu.make_async_copy(ob.at[r * 4 + k], out.at[slot_of(r, k)], o_sem.at[r * 4 + k]).start()
            return 0

        return lax.fori_loop(0, 4, columns, 0)

    lax.fori_loop(0, 4, rows, 0)

    def finish(i, _):
        pltpu.make_async_copy(ob.at[i], out.at[i], o_sem.at[i]).wait()
        return 0

    lax.fori_loop(0, 16, finish, 0)


def weight_kernel(factor, h0, h1, h2, h3, u, o0, o1, o2, o3, hs, us, own, ob, h_sem, u_sem, o_sem):
    hidden, outs = (h0, h1, h2, h3), (o0, o1, o2, o3)
    t, d = us.shape[0] // 4, us.shape[1] // 4

    def piece(r, k):
        return pltpu.make_async_copy(
            u.at[slot_of(r, k)], us.at[pl.ds(r * t, t), pl.ds(k * d, d)], u_sem.at[r * 4 + k]
        )

    for i in range(4):
        pltpu.make_async_copy(hidden[i], hs.at[:, pl.ds(i * t, t)], h_sem.at[i]).start()
    for k in range(4):
        for r in range(4):
            piece(r, k).start()
    for i in range(4):
        pltpu.make_async_copy(hidden[i], hs.at[:, pl.ds(i * t, t)], h_sem.at[i]).wait()
    for k in (1, 2, 3, 0):
        for r in range(4):
            piece(r, k).wait()
        total = jnp.dot(hs[...], us[:, k * d : (k + 1) * d], preferred_element_type=jnp.float32) * factor
        if k == 0:
            own[...] = total
            pltpu.make_async_copy(own, outs[0], o_sem.at[0]).start()
        else:
            ob[k - 1] = total.astype(jnp.bfloat16)
            pltpu.make_async_copy(ob.at[k - 1], outs[k], o_sem.at[k]).start()
    pltpu.make_async_copy(own, outs[0], o_sem.at[0]).wait()
    for k in range(1, 4):
        pltpu.make_async_copy(ob.at[k - 1], outs[k], o_sem.at[k]).wait()


def hidden_kernel(w0, w1, w2, w3, u, o0, o1, o2, o3, ws, us, own, ob, w_sem, u_sem, o_sem):
    weights, outs = (w0, w1, w2, w3), (o0, o1, o2, o3)
    t, d = us.shape[0] // 4, us.shape[1] // 4

    def piece(r, k):
        return pltpu.make_async_copy(
            u.at[slot_of(r, k)], us.at[pl.ds(r * t, t), pl.ds(k * d, d)], u_sem.at[r * 4 + k]
        )

    for i in range(4):
        pltpu.make_async_copy(weights[i], ws.at[:, pl.ds(i * d, d)], w_sem.at[i]).start()
    for r in range(4):
        for k in range(4):
            piece(r, k).start()
    for i in range(4):
        pltpu.make_async_copy(weights[i], ws.at[:, pl.ds(i * d, d)], w_sem.at[i]).wait()
    for r in (1, 2, 3, 0):
        for k in range(4):
            piece(r, k).wait()
        total = lax.dot_general(
            ws[...], us[r * t : (r + 1) * t, :], (((1,), (1,)), ((), ())), preferred_element_type=jnp.float32
        )
        if r == 0:
            own[...] = total
            pltpu.make_async_copy(own, outs[0], o_sem.at[0]).start()
        else:
            ob[r - 1] = total.astype(jnp.bfloat16)
            pltpu.make_async_copy(ob.at[r - 1], outs[r], o_sem.at[r]).start()
    pltpu.make_async_copy(own, outs[0], o_sem.at[0]).wait()
    for r in range(1, 4):
        pltpu.make_async_copy(ob.at[r - 1], outs[r], o_sem.at[r]).wait()


def call(kernel, inputs, outputs, scratch, flops, name):
    moved = sum(v.size * v.dtype.itemsize for v in (*inputs, *outputs))
    return pl.pallas_call(
        kernel,
        out_shape=outputs,
        in_specs=[pl.BlockSpec(memory_space=pl.ANY)] * len(inputs),
        out_specs=[pl.BlockSpec(memory_space=pl.ANY)] * len(outputs),
        scratch_shapes=scratch,
        compiler_params=pltpu.CompilerParams(vmem_limit_bytes=VMEM_LIMIT),
        cost_estimate=pl.CostEstimate(flops=flops, bytes_accessed=moved, transcendentals=0),
        name=name,
    )(*inputs)


def local(hidden, codes, scales, upstream):
    t, f = hidden.shape
    d = codes.shape[1]
    factor = 1.0 / math.sqrt(t * 16)
    bf16, f32 = jnp.bfloat16, jnp.float32
    sem = pltpu.SemaphoreType.DMA
    shape = jax.ShapeDtypeStruct
    flops = 2 * f * 4 * t * 4 * d

    first = permute(upstream, to_plane(0))
    second = permute(upstream, to_plane(1))
    weight = (codes.astype(f32) * jnp.repeat(scales, BLOCK, axis=1)).astype(bf16)
    weights = [weight] + [permute(weight, along_y(-k)) for k in (1, 2, 3)]
    turned = hidden.T
    hiddens = [turned] + [permute(turned, along_zl(r)) for r in (1, 2, 3)]
    cots = lax.all_gather(jnp.stack([first, second]), ("x", "c"), axis=0, tiled=True)

    (terms,) = call(
        mixed_kernel,
        [*hiddens, *weights],
        [shape((16, t, d), bf16)],
        [
            pltpu.VMEM((4, f, t), bf16),
            pltpu.VMEM((4, f, d), bf16),
            pltpu.VMEM((16, t, d), bf16),
            sem((4,)),
            sem((4,)),
            sem((16,)),
        ],
        flops,
        "mixed_terms",
    )
    sums = lax.psum_scatter(terms, ("x", "c"), scatter_dimension=0, tiled=True)

    grads = call(
        functools.partial(weight_kernel, factor),
        [*hiddens, cots],
        [shape((f, d), f32)] + [shape((f, d), bf16)] * 3,
        [
            pltpu.VMEM((f, 4 * t), bf16),
            pltpu.VMEM((4 * t, 4 * d), bf16),
            pltpu.VMEM((f, d), f32),
            pltpu.VMEM((3, f, d), bf16),
            sem((4,)),
            sem((16,)),
            sem((4,)),
        ],
        flops,
        "weight_terms",
    )
    weight_parts = [permute(grads[k], along_y(k)) for k in (1, 2, 3)]
    backs = call(
        hidden_kernel,
        [*weights, cots],
        [shape((f, t), f32)] + [shape((f, t), bf16)] * 3,
        [
            pltpu.VMEM((f, 4 * d), bf16),
            pltpu.VMEM((4 * t, 4 * d), bf16),
            pltpu.VMEM((f, t), f32),
            pltpu.VMEM((3, f, t), bf16),
            sem((4,)),
            sem((16,)),
            sem((4,)),
        ],
        flops,
        "hidden_terms",
    )
    hidden_parts = [permute(backs[r], along_zl(-r)) for r in (1, 2, 3)]

    near = permute(sums[0], inverse(to_plane(0)))
    far = permute(sums[1], inverse(to_plane(1)))
    mixed = (near.astype(f32) + far.astype(f32)).astype(bf16)
    weight_grad = grads[0] + sum(part.astype(f32) for part in weight_parts)
    hidden_grad = (backs[0] + sum(part.astype(f32) for part in hidden_parts)).astype(bf16).T
    return (mixed, hidden_grad, weight_grad)


def solution(mesh):
    fine = Mesh(mesh.devices.reshape(DIMS), AXES)
    node, columns = ("y", "zl"), ("zh", "x", "c")
    return jax.shard_map(
        local,
        mesh=fine,
        in_specs=(P(node, columns), P(columns, node), P(columns, node), P(node, columns)),
        out_specs=(P(node, columns), P(node, columns), P(columns, node)),
        check_vma=False,
    )
```

time: 741 us -> 213 us (0.29)
  waiting for transfers between devices: 606 us -> 79.7 us
  starting transfers between devices: 0.34 us -> 71.3 us
  matrix products: 48.1 us -> 0 us
  blocking collectives: 39.8 us -> 0 us
  Pallas kernels: 0 us -> 31.7 us
  local copies, waits for them, and re-layouts: 29.2 us -> 7.77 us
    reduce_scatter x2 -> x1, waiting for transfers between devices: 336 us -> 28 us  [local(): sums = lax.psum_scatter(terms, ('x', 'c'), scatter_dimension=0, tiled=True)]
    all_gather x2 -> x1, waiting for transfers between devices: 268 us -> 0.02 us  [local(): lax.all_gather(jnp.stack([first, second]), ('x', 'c'), axis=0, tiled=True)]
    ppermute x0 -> x16, starting transfers between devices: none -> 71.2 us  [permute(): return lax.ppermute(array, AXES, pairs)]
    ppermute x0 -> x16, waiting for transfers between devices: none -> 51.7 us  [permute(): return lax.ppermute(array, AXES, pairs)]
    dot_general x3 -> x0, matrix products: 48.1 us -> none  [the longest x1 19.5 us: local(): lax.dot_general(cot_rows, weight_full, (((1,), (1,)), ((), ())), preferre...]
    all_gather x1 -> x0, blocking collectives: 39.8 us -> none  [on_whole(): whole = lax.all_gather(array, axis, axis=dim, tiled=True)]
    pallas_call x0 -> x3, Pallas kernels: none -> 31.7 us  [call(): pl.pallas_call(kernel, out_shape=outputs, in_specs=[pl.BlockSpec(memory_s...]
    unnamed x4 -> x26, local copies, waits for them, and re-layouts: 25.5 us -> 5.69 us
  transfers between devices with their start and end apart: 4 -> 18, of which waited for: 4 -> 7; matrix products, arithmetic and copies ran while one was open for 11% -> 4% of each run, Pallas kernels for 0% -> 15%
where the time goes in v1:
time: 213 us; the launch traced here: 212 us
  waiting for transfers between devices  79.7 us (37%)
  starting transfers between devices  71.3 us (33%)
  Pallas kernels  31.7 us (15%)
  between operations  14.3 us (7%)
  local copies, waits for them, and re-layouts  7.77 us (4%)
  other arithmetic  7.38 us (3%)
    ppermute x16, starting transfers between devices, permute(): return lax.ppermute(array, AXES, pairs)  71.2 us
    ppermute x16, waiting for transfers between devices, permute(): return lax.ppermute(array, AXES, pairs)  51.7 us
    pallas_call x3, Pallas kernels, call(): pl.pallas_call(kernel, out_shape=outputs, in_specs=[pl.BlockSpec(memory_s...  31.7 us
    reduce_scatter x1, waiting for transfers between devices, local(): sums = lax.psum_scatter(terms, ('x', 'c'), scatter_dimension=0, tiled=True)  28 us
    unnamed x26, local copies, waits for them, and re-layouts  5.69 us
  transfers between devices with their start and end apart: 18, of which 7 were waited for; matrix products, arithmetic and copies ran while one was open for 4% of the time, Pallas kernels for 15%

profile of v1, /device:TPU:1, one launch (start us, length us, event | category | flops | bytes accessed | tf_op | source)
XLA Modules:
  0.0 212.1 jit_solution(3623807633268191350)
XLA Ops:
  7.2 0.0 copy-start.2
  7.2 0.0 copy-start.10
  7.2 0.0 all-gather.2.cloned.1.call-start
  7.2 7.9 %collective-permute-start.9 = (bf16[384,512]{1,0:T(8,128)(2,1)}, bf16[384,512]{1,0:T(8,128)(2,1)S(1)}, u32[]{:S(2)}, u32[]{:S(2)}) collective-permute-start(bf16[384,512]{1,0:T(8,128)(2,1)} %param.7), channel_id=1, source_target_pairs={{0,8},{1,24},{2,42},{3,58},{4,12},{5,28},{6,46},{7,62},{8,0},{9,16... | collective-permute-start | bytes 1179656 | tf_op jit(solution)/shard_map/ppermute | solution.py:22
  15.2 2.3 %collective-permute-start.8 = (bf16[384,512]{1,0:T(8,128)(2,1)}, bf16[384,512]{1,0:T(8,128)(2,1)S(1)}, u32[]{:S(2)}, u32[]{:S(2)}) collective-permute-start(bf16[384,512]{1,0:T(8,128)(2,1)} %param.7), channel_id=1, source_target_pairs={{0,0},{1,16},{2,34},{3,50},{4,4},{5,20},{6,38},{7,54},{8,8},{9,24}... | collective-permute-start | bytes 1179656 | tf_op jit(solution)/shard_map/ppermute | solution.py:22
  17.5 7.7 %collective-permute-done.9 = bf16[384,512]{1,0:T(8,128)(2,1)S(1)} collective-permute-done((bf16[384,512]{1,0:T(8,128)(2,1)}, bf16[384,512]{1,0:T(8,128)(2,1)S(1)}, u32[]{:S(2)}, u32[]{:S(2)}) %collective-permute-start.9) | collective-permute-done | bytes 393248 | tf_op jit(solution)/shard_map/ppermute | solution.py:22
  25.2 1.0 collective-permute-done.8
  26.3 0.9 pad_maximum_fusion
  27.2 0.0 all-gather.2.cloned.1.call-update
  27.2 0.0 reduce-scatter.2.cloned.1.call-start
  27.3 0.0 copy-done.2
  27.3 0.1 collective-permute-start
  27.4 0.0 copy-done.10
  27.4 0.2 copy.8
  27.6 0.9 broadcast_in_dim.3
  28.5 0.0 copy-start.9
  28.5 0.1 copy.9
  28.6 1.0 copy-done.9
  29.6 0.3 multiply_convert_fusion.w0
  29.9 2.8 %collective-permute-start.3 = (bf16[704,512]{1,0:T(8,128)(2,1)S(1)}, bf16[704,512]{1,0:T(8,128)(2,1)S(1)}, u32[]{:S(2)}, u32[]{:S(2)}) collective-permute-start(bf16[704,512]{1,0:T(8,128)(2,1)S(1)} %multiply_convert_fusion.w0), channel_id=1, source_target_pairs={{0,192},{1,193},{2,194},{3,195},{4,196},{5,197},{6,198},{7,199},{8... | collective-permute-start | bytes 2162696 | tf_op jit(solution)/shard_map/ppermute | solution.py:22
  32.7 0.4 collective-permute-start.4
  33.0 0.7 collective-permute-start.5
  33.7 16.7 %collective-permute-start.1 = (bf16[704,384]{1,0:T(8,128)(2,1)S(1)}, bf16[704,384]{1,0:T(8,128)(2,1)S(1)}, u32[]{:S(2)}, u32[]{:S(2)}) collective-permute-start(bf16[704,384]{1,0:T(8,128)(2,1)S(1)} %bitcast.12), channel_id=1, source_target_pairs={{0,32},{1,33},{2,34},{3,35},{4,36},{5,37},{6,38},{7,39},{8,40},{9,... | collective-permute-start | bytes 1622024 | tf_op jit(solution)/shard_map/ppermute | solution.py:22
  50.4 5.6 %collective-permute-done.h1 = bf16[704,384]{1,0:T(8,128)(2,1)S(1)} collective-permute-done((bf16[704,384]{1,0:T(8,128)(2,1)S(1)}, bf16[704,384]{1,0:T(8,128)(2,1)S(1)}, u32[]{:S(2)}, u32[]{:S(2)}) %collective-permute-start) | collective-permute-done | bytes 540704 | tf_op jit(solution)/shard_map/ppermute | solution.py:22
  56.0 1.1 collective-permute-start.2
  57.1 22.7 %collective-permute-done.1.h2 = bf16[704,384]{1,0:T(8,128)(2,1)S(1)} collective-permute-done((bf16[704,384]{1,0:T(8,128)(2,1)S(1)}, bf16[704,384]{1,0:T(8,128)(2,1)S(1)}, u32[]{:S(2)}, u32[]{:S(2)}) %collective-permute-start.1) | collective-permute-done | bytes 540704 | tf_op jit(solution)/shard_map/ppermute | solution.py:22
  79.8 10.9 %collective-permute-done.2.h3 = bf16[704,384]{1,0:T(8,128)(2,1)S(1)} collective-permute-done((bf16[704,384]{1,0:T(8,128)(2,1)S(1)}, bf16[704,384]{1,0:T(8,128)(2,1)S(1)}, u32[]{:S(2)}, u32[]{:S(2)}) %collective-permute-start.2) | collective-permute-done | bytes 540704 | tf_op jit(solution)/shard_map/ppermute | solution.py:22
  90.8 0.0 collective-permute-done.3.w1
  90.8 0.0 collective-permute-done.4.w2
  90.8 0.0 collective-permute-done.5.w3
  90.8 0.9 copy-done
  91.7 0.9 copy-done.11
  92.5 11.5 %mixed_terms.1 = bf16[16,384,512]{2,1,0:T(8,128)(2,1)} custom-call(bf16[704,384]{1,0:T(8,128)(2,1)S(1)} %bitcast.14, bf16[704,384]{1,0:T(8,128)(2,1)S(1)} %collective-permute-done.h1, bf16[704,384]{1,0:T(8,128)(2,1)S(1)} %collective-permute-done.1.h2, bf16[704,384]{1,0:T(8,128)(2,1)S(1)} %collective-permute-done.2.h3, ...), custom_call_target="tpu_custom_call" | custom-call | flops 4429185024 | bytes 11337728 | tf_op jit(solution)/shard_map/mixed_terms/pallas_call | solution.py:150
  104.0 0.0 copy-start.3
  104.1 0.8 copy-done.3
  104.9 0.8 copy-done.5
  105.7 0.0 reduce-scatter.2.cloned.1.call-update
  105.7 0.0 all-gather.2.cloned.1.call-done.u
  105.7 1.1 copy-done.1
  106.8 10.9 %hidden_terms.1 = (f32[704,384]{1,0:T(8,128)}, bf16[704,384]{1,0:T(8,128)(2,1)}, bf16[704,384]{1,0:T(8,128)(2,1)}, bf16[704,384]{1,0:T(8,128)(2,1)S(1)}) custom-call(bf16[704,512]{1,0:T(8,128)(2,1)S(1)} %multiply_convert_fusion.w0, bf16[704,512]{1,0:T(8,128)(2,1)S(1)} %collective-permute-done.3.w1, bf16[704,512]{1,0:T(8,128)(2,1)S(1)} %copy-done.1, ...), custom_call_target="tpu_custom_call" | custom-call | flops 4429185024 | bytes 11878400 | tf_op jit(solution)/shard_map/hidden_terms/pallas_call | solution.py:150
  117.7 0.3 collective-permute-start.12
  118.0 0.7 collective-permute-start.11
  118.7 2.5 %collective-permute-start.10 = (bf16[704,384]{1,0:T(8,128)(2,1)}, bf16[704,384]{1,0:T(8,128)(2,1)}, u32[]{:S(2)}, u32[]{:S(2)}) collective-permute-start(bf16[704,384]{1,0:T(8,128)(2,1)} %get-tuple-element.12), channel_id=1, source_target_pairs={{0,48},{1,49},{2,50},{3,51},{4,52},{5,53},{6,54},{7,55},{8,56},{9,... | collective-permute-start | bytes 1622024 | tf_op jit(solution)/shard_map/ppermute | solution.py:22
  121.2 9.2 %weight_terms.1 = (f32[704,512]{1,0:T(8,128)}, bf16[704,512]{1,0:T(8,128)(2,1)S(1)}, bf16[704,512]{1,0:T(8,128)(2,1)S(1)}, bf16[704,512]{1,0:T(8,128)(2,1)}) custom-call(bf16[704,384]{1,0:T(8,128)(2,1)S(1)} %bitcast.15, bf16[704,384]{1,0:T(8,128)(2,1)S(1)} %collective-permute-done.h1, bf16[704,384]{1,0:T(8,128)(2,1)S(1)} %copy-done.4, ...), custom_call_target="tpu_custom_call" | custom-call | flops 4429185024 | bytes 12058624 | tf_op jit(solution)/shard_map/weight_terms/pallas_call | solution.py:150
  130.5 2.8 %collective-permute-start.15 = (bf16[704,512]{1,0:T(8,128)(2,1)}, bf16[704,512]{1,0:T(8,128)(2,1)S(1)}, u32[]{:S(2)}, u32[]{:S(2)}) collective-permute-start(bf16[704,512]{1,0:T(8,128)(2,1)} %get-tuple-element.18), channel_id=1, source_target_pairs={{0,192},{1,193},{2,194},{3,195},{4,196},{5,197},{6,198},{7,199},{8... | collective-permute-start | bytes 2162696 | tf_op jit(solution)/shard_map/ppermute | solution.py:22
  133.3 0.4 collective-permute-start.14
  133.7 0.0 collective-permute-done.12
  133.7 0.7 collective-permute-start.13
  134.3 28.0 %reduce-scatter.2.cloned.1.call-done = bf16[2,384,512]{2,1,0:T(8,128)(2,1)} async-done(((bf16[16,384,512]{2,1,0:T(8,128)(2,1)}), bf16[2,384,512]{2,1,0:T(8,128)(2,1)}) %reduce-scatter.2.cloned.1.call-update) | async-done | bytes 786448 | tf_op jit(solution)/shard_map/reduce_scatter | solution.py:194
  162.3 1.2 slice_bitcast_fusion.1
  163.5 0.0 collective-permute-done.11
  163.5 30.0 %collective-permute-start.7 = (bf16[384,512]{1,0:T(8,128)(2,1)S(1)}, bf16[384,512]{1,0:T(8,128)(2,1)S(1)}, u32[]{:S(2)}, u32[]{:S(2)}) collective-permute-start(bf16[384,512]{1,0:T(8,128)(2,1)S(1)} %get-tuple-element.20), channel_id=1, source_target_pairs={{0,8},{1,24},{2,40},{3,56},{4,12},{5,28},{6,44},{7,60},{8,0},{9,16... | collective-permute-start | bytes 1179656 | tf_op jit(solution)/shard_map/ppermute | solution.py:22
  193.4 0.0 collective-permute-done.10
  193.4 1.9 collective-permute-start.6
  195.4 0.0 copy-start.7
  195.4 2.5 %fusion = bf16[384,704]{0,1:T(8,128)(2,1)} fusion(f32[704,384]{1,0:T(8,128)S(1)} %copy-done.8, bf16[704,384]{1,0:T(8,128)(2,1)} %collective-permute-done.12, bf16[704,384]{1,0:T(8,128)(2,1)} %collective-permute-done.11, bf16[704,384]{1,0:T(8,128)(2,1)} %collective-permute-done.10), kind=kLoop, calls=%fused_computation.5 | loop fusion | flops 1892352 | bytes 3244032 | tf_op jit(solution)/shard_map/transpose | solution.py:235
  197.9 0.0 collective-permute-done.15
  197.9 0.0 collective-permute-done.14
  197.9 0.0 collective-permute-done.13
  197.9 0.0 copy-done.7
  197.9 2.8 %add_add_fusion = f32[704,512]{1,0:T(8,128)} fusion(f32[704,512]{1,0:T(8,128)S(1)} %copy-done.7, bf16[704,512]{1,0:T(8,128)(2,1)S(1)} %collective-permute-done.15, bf16[704,512]{1,0:T(8,128)(2,1)} %collective-permute-done.14, bf16[704,512]{1,0:T(8,128)(2,1)} %collective-permute-done.13), kind=kLoop, calls=%fused_computation | loop fusion | flops 2162688 | bytes 5046272 | tf_op jit(solution)/shard_map/add | solution.py:234
  200.7 0.0 collective-permute-done.7
  200.7 3.7 %collective-permute-done.6 = bf16[384,512]{1,0:T(8,128)(2,1)S(1)} collective-permute-done((bf16[384,512]{1,0:T(8,128)(2,1)S(1)}, bf16[384,512]{1,0:T(8,128)(2,1)S(1)}, u32[]{:S(2)}, u32[]{:S(2)}) %collective-permute-start.6) | collective-permute-done | bytes 393248 | tf_op jit(solution)/shard_map/ppermute | solution.py:22
  204.4 0.8 add_convert_fusion.1
  (10 shorter events, 0.0 us)
Async XLA Ops:
  7.2 20.1 %copy-start.2 = (bf16[384,704]{0,1:T(8,128)(2,1)S(1)}, bf16[384,704]{0,1:T(8,128)(2,1)}, u32[]{:S(2)}) copy-start(bf16[384,704]{0,1:T(8,128)(2,1)} %param.4) | copy-start | bytes 1622020
  7.2 20.2 %copy-start.10 = (f32[704,2]{0,1:T(2,128)S(1)}, f32[704,2]{0,1:T(2,128)}, u32[]{:S(2)}) copy-start(f32[704,2]{0,1:T(2,128)} %param.6) | copy-start | bytes 16900
  7.2 98.5 %all-gather.2.cloned.1.call-start = ((), (), s32[]{:S(2)}) async-start(), calls=%async_computation.2 | async-start | bytes 7077888 | tf_op jit(solution)/shard_map/all_gather | solution.py:177
  7.2 18.0 %collective-permute-start.9 = (bf16[384,512]{1,0:T(8,128)(2,1)}, bf16[384,512]{1,0:T(8,128)(2,1)S(1)}, u32[]{:S(2)}, u32[]{:S(2)}) collective-permute-start(bf16[384,512]{1,0:T(8,128)(2,1)} %param.7), channel_id=1, source_target_pairs={{0,8},{1,24},{2,42},{3,58},{4,12},{5,28},{6,46},{7,62},{8,0},{9,16... | collective-permute-start | bytes 1179656 | tf_op jit(solution)/shard_map/ppermute | solution.py:22
  15.2 11.1 %collective-permute-start.8 = (bf16[384,512]{1,0:T(8,128)(2,1)}, bf16[384,512]{1,0:T(8,128)(2,1)S(1)}, u32[]{:S(2)}, u32[]{:S(2)}) collective-permute-start(bf16[384,512]{1,0:T(8,128)(2,1)} %param.7), channel_id=1, source_target_pairs={{0,0},{1,16},{2,34},{3,50},{4,4},{5,20},{6,38},{7,54},{8,8},{9,24}... | collective-permute-start | bytes 1179656 | tf_op jit(solution)/shard_map/ppermute | solution.py:22
  27.2 135.1 %reduce-scatter.2.cloned.1.call-start = ((), (), s32[]{:S(2)}) async-start(), calls=%async_computation.1 | async-start | bytes 7077888 | tf_op jit(solution)/shard_map/reduce_scatter | solution.py:194
  27.3 28.7 %collective-permute-start = (bf16[704,384]{1,0:T(8,128)(2,1)S(1)}, bf16[704,384]{1,0:T(8,128)(2,1)S(1)}, u32[]{:S(2)}, u32[]{:S(2)}) collective-permute-start(bf16[704,384]{1,0:T(8,128)(2,1)S(1)} %bitcast.11), channel_id=1, source_target_pairs={{0,16},{1,17},{2,18},{3,19},{4,20},{5,21},{6,22},{7,23},{8,24},{9,... | collective-permute-start | bytes 1622024 | tf_op jit(solution)/shard_map/ppermute | solution.py:22
  28.5 1.1 copy-start.9
  29.9 60.9 %collective-permute-start.3 = (bf16[704,512]{1,0:T(8,128)(2,1)S(1)}, bf16[704,512]{1,0:T(8,128)(2,1)S(1)}, u32[]{:S(2)}, u32[]{:S(2)}) collective-permute-start(bf16[704,512]{1,0:T(8,128)(2,1)S(1)} %multiply_convert_fusion.w0), channel_id=1, source_target_pairs={{0,192},{1,193},{2,194},{3,195},{4,196},{5,197},{6,198},{7,199},{8... | collective-permute-start | bytes 2162696 | tf_op jit(solution)/shard_map/ppermute | solution.py:22
  32.7 58.1 %collective-permute-start.4 = (bf16[704,512]{1,0:T(8,128)(2,1)S(1)}, bf16[704,512]{1,0:T(8,128)(2,1)S(1)}, u32[]{:S(2)}, u32[]{:S(2)}) collective-permute-start(bf16[704,512]{1,0:T(8,128)(2,1)S(1)} %multiply_convert_fusion.w0), channel_id=1, source_target_pairs={{0,128},{1,129},{2,130},{3,131},{4,132},{5,133},{6,134},{7,135},{8... | collective-permute-start | bytes 2162696 | tf_op jit(solution)/shard_map/ppermute | solution.py:22
  33.0 57.7 %collective-permute-start.5 = (bf16[704,512]{1,0:T(8,128)(2,1)S(1)}, bf16[704,512]{1,0:T(8,128)(2,1)S(1)}, u32[]{:S(2)}, u32[]{:S(2)}) collective-permute-start(bf16[704,512]{1,0:T(8,128)(2,1)S(1)} %multiply_convert_fusion.w0), channel_id=1, source_target_pairs={{0,64},{1,65},{2,66},{3,67},{4,68},{5,69},{6,70},{7,71},{8,72},{9,... | collective-permute-start | bytes 2162696 | tf_op jit(solution)/shard_map/ppermute | solution.py:22
  33.7 46.1 %collective-permute-start.1 = (bf16[704,384]{1,0:T(8,128)(2,1)S(1)}, bf16[704,384]{1,0:T(8,128)(2,1)S(1)}, u32[]{:S(2)}, u32[]{:S(2)}) collective-permute-start(bf16[704,384]{1,0:T(8,128)(2,1)S(1)} %bitcast.12), channel_id=1, source_target_pairs={{0,32},{1,33},{2,34},{3,35},{4,36},{5,37},{6,38},{7,39},{8,40},{9,... | collective-permute-start | bytes 1622024 | tf_op jit(solution)/shard_map/ppermute | solution.py:22
  56.0 34.7 %collective-permute-start.2 = (bf16[704,384]{1,0:T(8,128)(2,1)S(1)}, bf16[704,384]{1,0:T(8,128)(2,1)S(1)}, u32[]{:S(2)}, u32[]{:S(2)}) collective-permute-start(bf16[704,384]{1,0:T(8,128)(2,1)S(1)} %bitcast.13), channel_id=1, source_target_pairs={{0,48},{1,49},{2,50},{3,51},{4,52},{5,53},{6,54},{7,55},{8,56},{9,... | collective-permute-start | bytes 1622024 | tf_op jit(solution)/shard_map/ppermute | solution.py:22
  90.8 0.9 copy-start
  91.7 0.9 copy-start.11
  104.0 0.8 copy-start.3
  104.9 0.8 copy-start.5
  105.7 1.1 copy-start.1
  106.8 14.5 %copy-start.4 = (bf16[704,384]{1,0:T(8,128)(2,1)S(1)}, bf16[704,384]{1,0:T(8,128)(2,1)}, u32[]{:S(2)}) copy-start(bf16[704,384]{1,0:T(8,128)(2,1)} %copy-done.3) | copy-start | bytes 1622020
  106.8 14.5 %copy-start.6 = (bf16[704,384]{1,0:T(8,128)(2,1)S(1)}, bf16[704,384]{1,0:T(8,128)(2,1)}, u32[]{:S(2)}) copy-start(bf16[704,384]{1,0:T(8,128)(2,1)} %copy-done.5) | copy-start | bytes 1622020
  117.7 16.0 %collective-permute-start.12 = (bf16[704,384]{1,0:T(8,128)(2,1)S(1)}, bf16[704,384]{1,0:T(8,128)(2,1)}, u32[]{:S(2)}, u32[]{:S(2)}) collective-permute-start(bf16[704,384]{1,0:T(8,128)(2,1)S(1)} %get-tuple-element.14), channel_id=1, source_target_pairs={{0,16},{1,17},{2,18},{3,19},{4,20},{5,21},{6,22},{7,23},{8,24},{9,... | collective-permute-start | bytes 1622024 | tf_op jit(solution)/shard_map/ppermute | solution.py:22
  118.0 45.5 %collective-permute-start.11 = (bf16[704,384]{1,0:T(8,128)(2,1)}, bf16[704,384]{1,0:T(8,128)(2,1)}, u32[]{:S(2)}, u32[]{:S(2)}) collective-permute-start(bf16[704,384]{1,0:T(8,128)(2,1)} %get-tuple-element.13), channel_id=1, source_target_pairs={{0,32},{1,33},{2,34},{3,35},{4,36},{5,37},{6,38},{7,39},{8,40},{9,... | collective-permute-start | bytes 1622024 | tf_op jit(solution)/shard_map/ppermute | solution.py:22
  118.7 74.8 %collective-permute-start.10 = (bf16[704,384]{1,0:T(8,128)(2,1)}, bf16[704,384]{1,0:T(8,128)(2,1)}, u32[]{:S(2)}, u32[]{:S(2)}) collective-permute-start(bf16[704,384]{1,0:T(8,128)(2,1)} %get-tuple-element.12), channel_id=1, source_target_pairs={{0,48},{1,49},{2,50},{3,51},{4,52},{5,53},{6,54},{7,55},{8,56},{9,... | collective-permute-start | bytes 1622024 | tf_op jit(solution)/shard_map/ppermute | solution.py:22
  130.5 64.9 %copy-start.8 = (f32[704,384]{1,0:T(8,128)S(1)}, f32[704,384]{1,0:T(8,128)}, u32[]{:S(2)}) copy-start(f32[704,384]{1,0:T(8,128)} %get-tuple-element.11) | copy-start | bytes 3244036
  130.5 67.4 %collective-permute-start.15 = (bf16[704,512]{1,0:T(8,128)(2,1)}, bf16[704,512]{1,0:T(8,128)(2,1)S(1)}, u32[]{:S(2)}, u32[]{:S(2)}) collective-permute-start(bf16[704,512]{1,0:T(8,128)(2,1)} %get-tuple-element.18), channel_id=1, source_target_pairs={{0,192},{1,193},{2,194},{3,195},{4,196},{5,197},{6,198},{7,199},{8... | collective-permute-start | bytes 2162696 | tf_op jit(solution)/shard_map/ppermute | solution.py:22
  133.3 64.6 %collective-permute-start.14 = (bf16[704,512]{1,0:T(8,128)(2,1)S(1)}, bf16[704,512]{1,0:T(8,128)(2,1)}, u32[]{:S(2)}, u32[]{:S(2)}) collective-permute-start(bf16[704,512]{1,0:T(8,128)(2,1)S(1)} %get-tuple-element.17), channel_id=1, source_target_pairs={{0,128},{1,129},{2,130},{3,131},{4,132},{5,133},{6,134},{7,135},{8... | collective-permute-start | bytes 2162696 | tf_op jit(solution)/shard_map/ppermute | solution.py:22
  133.7 64.2 %collective-permute-start.13 = (bf16[704,512]{1,0:T(8,128)(2,1)S(1)}, bf16[704,512]{1,0:T(8,128)(2,1)}, u32[]{:S(2)}, u32[]{:S(2)}) collective-permute-start(bf16[704,512]{1,0:T(8,128)(2,1)S(1)} %get-tuple-element.16), channel_id=1, source_target_pairs={{0,64},{1,65},{2,66},{3,67},{4,68},{5,69},{6,70},{7,71},{8,72},{9,... | collective-permute-start | bytes 2162696 | tf_op jit(solution)/shard_map/ppermute | solution.py:22
  163.5 37.2 %collective-permute-start.7 = (bf16[384,512]{1,0:T(8,128)(2,1)S(1)}, bf16[384,512]{1,0:T(8,128)(2,1)S(1)}, u32[]{:S(2)}, u32[]{:S(2)}) collective-permute-start(bf16[384,512]{1,0:T(8,128)(2,1)S(1)} %get-tuple-element.20), channel_id=1, source_target_pairs={{0,8},{1,24},{2,40},{3,56},{4,12},{5,28},{6,44},{7,60},{8,0},{9,16... | collective-permute-start | bytes 1179656 | tf_op jit(solution)/shard_map/ppermute | solution.py:22
  193.4 10.9 %collective-permute-start.6 = (bf16[384,512]{1,0:T(8,128)(2,1)S(1)}, bf16[384,512]{1,0:T(8,128)(2,1)S(1)}, u32[]{:S(2)}, u32[]{:S(2)}) collective-permute-start(bf16[384,512]{1,0:T(8,128)(2,1)S(1)} %get-tuple-element.19), channel_id=1, source_target_pairs={{0,0},{1,16},{2,32},{3,48},{4,4},{5,20},{6,36},{7,52},{8,8},{9,24}... | collective-permute-start | bytes 1179656 | tf_op jit(solution)/shard_map/ppermute | solution.py:22
  195.4 2.5 %copy-start.7 = (f32[704,512]{1,0:T(8,128)S(1)}, f32[704,512]{1,0:T(8,128)}, u32[]{:S(2)}) copy-start(f32[704,512]{1,0:T(8,128)} %get-tuple-element.15) | copy-start | bytes 4325380
Sparse Core Ops, SparseCore 0:
  27.4 71.8 all-gather.1
  105.8 56.4 reduce-scatter.1

commit v2 on v0

v2 whole, which is shorter than its diff:
```python
import functools
import math

import jax
import jax.numpy as jnp
from jax import lax
from jax.experimental import pallas as pl
from jax.experimental.pallas import tpu as pltpu
from jax.sharding import Mesh, PartitionSpec as P
import numpy as np

BLOCK = 256
AXES = ("y", "zl", "zh", "x", "c")
DIMS = (4, 4, 2, 4, 2)
VMEM_LIMIT = 50 * 1024 * 1024
bf16, f32 = jnp.bfloat16, jnp.float32

ORDERS = ((1, 3), (3, 1))


def permute(array, target):
    pairs = []
    for index, source in enumerate(np.ndindex(*DIMS)):
        place = target(*source)
        if place is not None:
            pairs.append((index, int(np.ravel_multi_index(place, DIMS))))
    return lax.ppermute(array, AXES, pairs)


def inverse(target):
    table = {target(*source): source for source in np.ndindex(*DIMS)}
    return lambda *place: table[place]


def partner(axis, mask):
    position = AXES.index(axis)

    def target(*place):
        return tuple(v ^ mask if i == position else v for i, v in enumerate(place))

    return target


def to_plane(kind):
    def target(y, zl, zh, x, c):
        column = zh * 8 + x * 2 + c
        plane, p, q = column % 4, column // 8, column // 4 % 2
        r = plane ^ zl
        return (y, plane, p ^ kind, 2 * (r // 2 ^ plane % 2 ^ plane // 2 ^ p) + (q ^ kind), r % 2)

    return target


def from_plane(kind, part):
    back = inverse(to_plane(kind))

    def target(y, zl, zh, x, c):
        if x // 2 ^ zl % 2 ^ zl // 2 ^ zh ^ kind != part:
            return None
        return back(y, zl, zh, x, c)

    return target


def place_of(kind, other, s):
    y, zl, zh, x, c = (lax.axis_index(name) for name in AXES)
    x, p = x ^ s, zh ^ kind
    r = 2 * ((x // 2) ^ (zl % 2) ^ (zl // 2) ^ p) + (c ^ other)
    return r, y ^ (2 * p + ((x % 2) ^ kind))


def step_for(part, k):
    y, zl, zh, x = (lax.axis_index(name) for name in ("y", "zl", "zh", "x"))
    p, q = (y ^ k) // 2, (y ^ k) % 2
    return x ^ (2 * (part ^ (zl % 2) ^ (zl // 2) ^ p) + (q ^ p ^ zh))


def gathered(own, near, rest, m, half, order):
    if m == 0:
        rows = own.shape[0] // 2
        return own.at[half * rows : (half + 1) * rows]
    if m == order[0]:
        return near
    return rest.at[0 if m == order[1] else 1]


def halves(refs, m):
    own, near0, rest0, near1, rest1 = refs
    return (
        gathered(own, near0, rest0, m, 0, ORDERS[0]),
        gathered(own, near1, rest1, m, 1, ORDERS[1]),
    )


def whole(refs, m):
    pair, rest = refs
    return (pair.at[0], pair.at[1], rest.at[1], rest.at[0])[m]


def upstream_copies(refs, us, u_sem, start):
    t, d = us.shape[0] // 4, us.shape[1] // 4
    for kind, (a, b) in enumerate(ORDERS):
        own, near, rest, pair, far = refs[5 * kind : 5 * kind + 5]
        pieces = (
            (own, 0, 0), (near, 0, a), (rest.at[0], 0, b), (rest.at[1], 0, 2),
            (pair.at[0], 1, 0), (pair.at[1], 1, a), (far.at[0], 1, b), (far.at[1], 1, 2),
        )
        for piece, other, s in pieces:
            r, k = place_of(kind, other, s)
            rows = pl.ds(pl.multiple_of(r * t, t), t)
            columns = pl.ds(pl.multiple_of(k * d, d), d)
            pltpu.make_async_copy(piece, us.at[rows, columns], u_sem.at[r * 4 + k]).start()


def wait_upstream(refs, us, u_sem, r, k):
    t, d = us.shape[0] // 4, us.shape[1] // 4
    place = us.at[r * t : (r + 1) * t, k * d : (k + 1) * d]
    pltpu.make_async_copy(refs[0], place, u_sem.at[r * 4 + k]).wait()


def mixed_kernel(part, *refs):
    hidden, weights = refs[:5], refs[5:7]
    send, keep, hs, ws, ob, h_sem, w_sem, o_sem = refs[7:]
    half, d = hs.shape[1] // 2, ob.shape[3]
    copies = []
    for m in range(4):
        place = ws.at[:, m * d : (m + 1) * d]
        copies.append(pltpu.make_async_copy(whole(weights, m), place, w_sem.at[m]))
    for m in range(2):
        for i, piece in enumerate(halves(hidden, 2 * part + m)):
            place = hs.at[m, i * half : (i + 1) * half]
            copies.append(pltpu.make_async_copy(piece, place, h_sem.at[2 * m + i]))
    for copy in copies:
        copy.start()
    for copy in copies:
        copy.wait()
    core = lax.axis_index("c")
    a, b = ORDERS[part]
    for i, out in enumerate((send, keep)):
        block = hs[core if i else 1 - core].T
        terms = jnp.dot(block, ws[...], preferred_element_type=f32).astype(bf16)
        for k in range(4):
            s = step_for(part, k)
            slot = jnp.where(s == 0, 0, jnp.where(s == b, 1, jnp.where(s == a, 2, 3)))
            ob[i, slot] = terms[:, k * d : (k + 1) * d]
        pltpu.make_async_copy(ob.at[i], out, o_sem.at[i]).start()
    for i, out in enumerate((send, keep)):
        pltpu.make_async_copy(ob.at[i], out, o_sem.at[i]).wait()


def give_out(total, m, orders, outs, own, ob, o_sem):
    half = total.shape[0] // 2
    copies = []
    for i, (a, b) in enumerate(orders):
        rows = slice(i * half, (i + 1) * half)
        mine, mid, send = outs[3 * i : 3 * i + 3]
        if m == 0:
            own[rows] = total[rows]
            copies.append(pltpu.make_async_copy(own.at[rows], mine, o_sem.at[m, i]))
        else:
            ob[m - 1, rows] = total[rows].astype(bf16)
            out = mid if m == b else send.at[0 if m == a else 1]
            copies.append(pltpu.make_async_copy(ob.at[m - 1, rows], out, o_sem.at[m, i]))
    for copy in copies:
        copy.start()
    return copies


def weight_kernel(factor, orders, *refs):
    hidden, cots, outs = refs[:5], refs[5:15], refs[15:21]
    hs, us, own, ob, h_sem, u_sem, o_sem = refs[21:]
    t, d = us.shape[0] // 4, us.shape[1] // 4
    half = hs.shape[0] // 2
    copies = []
    for m in range(4):
        for i, piece in enumerate(halves(hidden, m)):
            place = hs.at[i * half : (i + 1) * half, m * t : (m + 1) * t]
            copies.append(pltpu.make_async_copy(piece, place, h_sem.at[2 * m + i]))
    for copy in copies:
        copy.start()
    upstream_copies(cots, us, u_sem, True)
    for copy in copies:
        copy.wait()
    copies = []
    for k in (2, 1, 3, 0):
        for r in range(4):
            wait_upstream(cots, us, u_sem, r, k)
        total = jnp.dot(hs[...], us[:, k * d : (k + 1) * d], preferred_element_type=f32) * factor
        copies += give_out(total, k, orders, outs, own, ob, o_sem)
    for copy in copies:
        copy.wait()


def hidden_kernel(orders, *refs):
    weights, cots, outs = refs[:2], refs[2:12], refs[12:18]
    ws, us, own, ob, w_sem, u_sem, o_sem = refs[18:]
    t, d = us.shape[0] // 4, us.shape[1] // 4
    copies = []
    for m in range(4):
        place = ws.at[:, m * d : (m + 1) * d]
        copies.append(pltpu.make_async_copy(whole(weights, m), place, w_sem.at[m]))
    for copy in copies:
        copy.start()
    upstream_copies(cots, us, u_sem, True)
    for copy in copies:
        copy.wait()
    copies = []
    for r in (2, 1, 3, 0):
        for k in range(4):
            wait_upstream(cots, us, u_sem, r, k)
        total = lax.dot_general(
            ws[...], us[r * t : (r + 1) * t, :], (((1,), (1,)), ((), ())), preferred_element_type=f32
        )
        copies += give_out(total, r, orders, outs, own, ob, o_sem)
    for copy in copies:
        copy.wait()


def call(kernel, inputs, outputs, scratch, flops, name):
    moved = sum(v.size * v.dtype.itemsize for v in (*inputs, *outputs))
    return pl.pallas_call(
        kernel,
        out_shape=outputs,
        in_specs=[pl.BlockSpec(memory_space=pltpu.HBM)] * len(inputs),
        out_specs=[pl.BlockSpec(memory_space=pltpu.HBM)] * len(outputs),
        scratch_shapes=scratch,
        compiler_params=pltpu.CompilerParams(vmem_limit_bytes=VMEM_LIMIT),
        cost_estimate=pl.CostEstimate(flops=flops, bytes_accessed=moved, transcendentals=0),
        name=name,
    )(*inputs)


def after(value, *others):
    return lax.optimization_barrier((value, *others))[0]


def finish(parts, axis, order, first):
    mine, mid, _ = parts
    mid = (mid.astype(f32) + first[1].astype(f32)).astype(bf16)
    second = permute(mid, partner(axis, order[1]))
    return mine + first[0].astype(f32) + second.astype(f32)


def local(hidden, codes, scales, upstream):
    t, f = hidden.shape
    d = codes.shape[1]
    half = f // 2
    factor = 1.0 / math.sqrt(t * 16)
    sem = pltpu.SemaphoreType.DMA
    shape = jax.ShapeDtypeStruct
    flops = 2 * f * 4 * t * 4 * d

    owns = [permute(upstream, to_plane(kind)) for kind in (0, 1)]
    weight = (codes.astype(f32) * jnp.repeat(scales, BLOCK, axis=1)).astype(bf16)
    w_near = [permute(v, partner("y", 1)) for v in (weight[:half], weight[half:])]
    turned = after(hidden.T, *owns)
    h_own = [turned[:half], turned[half:]]
    h_near = [permute(v, partner("zl", a)) for v, (a, _) in zip(h_own, ORDERS)]
    u_near = [permute(v, partner("x", a)) for v, (a, _) in zip(owns, ORDERS)]
    h_rest = [
        permute(jnp.stack(pair), partner("zl", b)) for *pair, (_, b) in zip(h_own, h_near, ORDERS)
    ]
    u_pair = [jnp.stack(pair) for pair in zip(owns, u_near)]
    u_rest = [permute(pair, partner("x", b)) for pair, (_, b) in zip(u_pair, ORDERS)]
    w_pair = jnp.concatenate([weight, *w_near]).reshape(2, f, d)
    weights = [w_pair, permute(w_pair, partner("y", 3))]
    hiddens = [turned, h_near[0], h_rest[0], h_near[1], h_rest[1]]
    cots = []
    for kind in range(2):
        cots += [owns[kind], u_near[kind], u_rest[kind]]
        cots += [permute(v, partner("c", 1)) for v in (u_pair[kind], u_rest[kind])]

    def mixed_terms(part, *before):
        return call(
            functools.partial(mixed_kernel, part),
            [after(hiddens[0], *before), *hiddens[1:], *weights],
            [shape((4, t, d), bf16)] * 2,
            [
                pltpu.VMEM((2, f, t), bf16),
                pltpu.VMEM((f, 4 * d), bf16),
                pltpu.VMEM((2, 4, t, d), bf16),
                sem((4,)),
                sem((4,)),
                sem((2,)),
            ],
            flops // 2,
            "mixed_terms",
        )

    def give(part, keep, got):
        share = (keep[2:].astype(f32) + got[2:].astype(f32)).astype(bf16)
        return share, permute(share, partner("x", ORDERS[part][0]))

    def take(part, keep, got, first, *before):
        mid = (keep[1].astype(f32) + got[1].astype(f32) + first[1].astype(f32)).astype(bf16)
        second = permute(after(mid, *before), partner("x", ORDERS[part][1]))
        total = keep[0].astype(f32) + got[0].astype(f32) + first[0].astype(f32) + second.astype(f32)
        return second, [permute(total.astype(bf16), from_plane(kind, part)) for kind in (0, 1)]

    send0, keep0 = mixed_terms(0, *u_rest)
    got0 = permute(send0, partner("c", 1))
    share0, first0 = give(0, keep0, got0)
    send1, keep1 = mixed_terms(1, send0)
    got1 = permute(send1, partner("c", 1))
    share1, first1 = give(1, keep1, got1)
    orders = ORDERS[::-1]
    backs = call(
        functools.partial(hidden_kernel, orders),
        [after(weights[0], send1, share0), *weights[1:], *cots],
        [shape((half, t), f32), shape((half, t), bf16), shape((2, half, t), bf16)] * 2,
        [
            pltpu.VMEM((f, 4 * d), bf16),
            pltpu.VMEM((4 * t, 4 * d), bf16),
            pltpu.VMEM((f, t), f32),
            pltpu.VMEM((3, f, t), bf16),
            sem((4,)),
            sem((16,)),
            sem((4, 2)),
        ],
        flops,
        "hidden_terms",
    )
    sent = [permute(backs[3 * i + 2], partner("zl", orders[i][0])) for i in range(2)]
    grads = call(
        functools.partial(weight_kernel, factor, orders),
        [after(hiddens[0], backs[2], share1), *hiddens[1:], *cots],
        [shape((half, d), f32), shape((half, d), bf16), shape((2, half, d), bf16)] * 2,
        [
            pltpu.VMEM((f, 4 * t), bf16),
            pltpu.VMEM((4 * t, 4 * d), bf16),
            pltpu.VMEM((f, d), f32),
            pltpu.VMEM((3, f, d), bf16),
            sem((8,)),
            sem((16,)),
            sem((4, 2)),
        ],
        flops,
        "weight_terms",
    )
    first0, first1, *sent = lax.optimization_barrier((first0, first1, *sent, grads[2]))[:4]
    second0, ends = take(0, keep0, got0, first0)
    back = [finish(backs[3 * i : 3 * i + 3], "zl", orders[i], sent[i]) for i in range(2)]
    second1, more = take(1, keep1, got1, first1)
    ends += more
    grad = []
    for i in range(2):
        send = after(grads[3 * i + 2], first0, first1, *sent)
        first = permute(send, partner("y", orders[i][0]))
        grad.append(finish(grads[3 * i : 3 * i + 3], "y", orders[i], first))
    mixed = sum(v.astype(f32) for v in ends).astype(bf16)
    hidden_grad = jnp.concatenate(back).astype(bf16).T
    return (mixed, hidden_grad, jnp.concatenate(grad))


def solution(mesh):
    fine = Mesh(mesh.devices.reshape(DIMS), AXES)
    node, columns = ("y", "zl"), ("zh", "x", "c")
    return jax.shard_map(
        local,
        mesh=fine,
        in_specs=(P(node, columns), P(columns, node), P(columns, node), P(node, columns)),
        out_specs=(P(node, columns), P(node, columns), P(columns, node)),
        check_vma=False,
    )
```

time: 741 us -> 194 us (0.26)
  waiting for transfers between devices: 606 us -> 82.9 us
  starting transfers between devices: 0.34 us -> 58.9 us
  matrix products: 48.1 us -> 0 us
  blocking collectives: 39.8 us -> 0 us
  Pallas kernels: 0 us -> 30.6 us
  local copies, waits for them, and re-layouts: 29.2 us -> 5.99 us
  between operations: 13.8 us -> 1.05 us
  other arithmetic: 3.1 us -> 11.5 us
    reduce_scatter x2 -> x0, waiting for transfers between devices: 336 us -> none  [the longest x1 249 us: local(): lax.psum_scatter(local_grad.astype(jnp.bfloat16), 'node', scatter_dimensi...]
    all_gather x2 -> x0, waiting for transfers between devices: 268 us -> none  [the longest x1 188 us: on_whole(): whole = lax.all_gather(array, axis, axis=dim, tiled=True)]
    ppermute x0 -> x35, waiting for transfers between devices: none -> 82.9 us  [permute(): return lax.ppermute(array, AXES, pairs)]
    ppermute x0 -> x35, starting transfers between devices: none -> 58.9 us  [permute(): return lax.ppermute(array, AXES, pairs)]
    dot_general x3 -> x0, matrix products: 48.1 us -> none  [the longest x1 19.5 us: local(): lax.dot_general(cot_rows, weight_full, (((1,), (1,)), ((), ())), preferre...]
    all_gather x1 -> x0, blocking collectives: 39.8 us -> none  [on_whole(): whole = lax.all_gather(array, axis, axis=dim, tiled=True)]
    pallas_call x0 -> x4, Pallas kernels: none -> 30.6 us  [call(): pl.pallas_call(kernel, out_shape=outputs, in_specs=[pl.BlockSpec(memory_s...]
    unnamed x4 -> x40, local copies, waits for them, and re-layouts: 25.5 us -> 4.94 us
  transfers between devices with their start and end apart: 4 -> 35, of which waited for: 4 -> 14; matrix products, arithmetic and copies ran while one was open for 11% -> 6% of each run, Pallas kernels for 0% -> 13%
where the time goes in v2:
time: 194 us; the launch traced here: 191 us
  waiting for transfers between devices  82.9 us (43%)
  starting transfers between devices  58.9 us (30%)
  Pallas kernels  30.6 us (16%)
  other arithmetic  11.5 us (6%)
  local copies, waits for them, and re-layouts  5.99 us (3%)
    ppermute x35, waiting for transfers between devices, permute(): return lax.ppermute(array, AXES, pairs)  82.9 us
    ppermute x35, starting transfers between devices, permute(): return lax.ppermute(array, AXES, pairs)  58.9 us
    pallas_call x4, Pallas kernels, call(): pl.pallas_call(kernel, out_shape=outputs, in_specs=[pl.BlockSpec(memory_s...  30.6 us
    unnamed x40, local copies, waits for them, and re-layouts  4.94 us
  transfers between devices with their start and end apart: 35, of which 14 were waited for; matrix products, arithmetic and copies ran while one was open for 6% of the time, Pallas kernels for 13%

profile of v2, /device:TPU:1, one launch (start us, length us, event | category | flops | bytes accessed | tf_op | source)
XLA Modules:
  0.0 191.0 jit_solution(17595240848674536333)
XLA Ops:
  0.6 9.6 %collective-permute-start.1 = (bf16[384,512]{1,0:T(8,128)(2,1)}, bf16[384,512]{1,0:T(8,128)(2,1)S(1)}, u32[]{:S(2)}, u32[]{:S(2)}) collective-permute-start(bf16[384,512]{1,0:T(8,128)(2,1)} %param.7), channel_id=1, source_target_pairs={{0,10},{1,31},{2,42},{3,63},{4,8},{5,29},{6,40},{7,61},{8,6},{9,19... | collective-permute-start | bytes 1179656 | tf_op jit(solution)/shard_map/ppermute | solution.py:27
  10.2 0.9 copy.7
  11.1 0.9 broadcast_in_dim.3
  12.0 0.1 copy.8
  12.1 1.0 copy-done.9
  13.1 0.2 multiply_convert_fusion
  13.4 1.4 collective-permute-start.10
  14.8 0.2 collective-permute-start.11
  15.0 3.9 %collective-permute-start = (bf16[384,512]{1,0:T(8,128)(2,1)S(1)}, bf16[384,512]{1,0:T(8,128)(2,1)S(1)}, u32[]{:S(2)}, u32[]{:S(2)}) collective-permute-start(bf16[384,512]{1,0:T(8,128)(2,1)S(1)} %copy-done.18), channel_id=1, source_target_pairs={{0,0},{1,21},{2,32},{3,53},{4,2},{5,23},{6,34},{7,55},{8,12},{9,25... | collective-permute-start | bytes 1179656 | tf_op jit(solution)/shard_map/ppermute | solution.py:27
  18.9 17.9 %collective-permute-done.1.refs_7_.refs_10_ = bf16[384,512]{1,0:T(8,128)(2,1)S(1)} collective-permute-done((bf16[384,512]{1,0:T(8,128)(2,1)}, bf16[384,512]{1,0:T(8,128)(2,1)S(1)}, u32[]{:S(2)}, u32[]{:S(2)}) %collective-permute-start.1) | collective-permute-done | bytes 393248 | tf_op jit(solution)/shard_map/ppermute | solution.py:27
  37.0 2.8 %collective-permute-start.12 = (bf16[2,704,512]{2,1,0:T(8,128)(2,1)S(1)}, bf16[2,704,512]{2,1,0:T(8,128)(2,1)S(1)}, u32[]{:S(2)}, u32[]{:S(2)}) collective-permute-start(bf16[2,704,512]{2,1,0:T(8,128)(2,1)S(1)} %bitcast.60), channel_id=1, source_target_pairs={{0,192},{1,193},{2,194},{3,195},{4,196},{5,197},{6,198},{7,199},{8... | collective-permute-start | bytes 4325384 | tf_op jit(solution)/shard_map/ppermute | solution.py:27
  40.0 2.3 %collective-permute-start.8 = (bf16[352,384]{1,0:T(8,128)(2,1)S(1)}, bf16[352,384]{1,0:T(8,128)(2,1)S(1)}, u32[]{:S(2)}, u32[]{:S(2)}) collective-permute-start(bf16[352,384]{1,0:T(8,128)(2,1)S(1)} %get-tuple-element.61), channel_id=1, source_target_pairs={{0,48},{1,49},{2,50},{3,51},{4,52},{5,53},{6,54},{7,55},{8,56},{9,... | collective-permute-start | bytes 811016 | tf_op jit(solution)/shard_map/ppermute | solution.py:27
  42.3 3.9 %collective-permute-done.4.refs_8_.refs_11_ = bf16[384,512]{1,0:T(8,128)(2,1)S(1)} collective-permute-done((bf16[384,512]{1,0:T(8,128)(2,1)S(1)}, bf16[384,512]{1,0:T(8,128)(2,1)S(1)}, u32[]{:S(2)}, u32[]{:S(2)}) %collective-permute-start.4) | collective-permute-done | bytes 393248 | tf_op jit(solution)/shard_map/ppermute | solution.py:27
  46.3 0.7 collective-permute-start.5
  47.0 3.5 %collective-permute-done.2.refs_3_.refs_6_ = bf16[384,512]{1,0:T(8,128)(2,1)S(1)} collective-permute-done((bf16[384,512]{1,0:T(8,128)(2,1)S(1)}, bf16[384,512]{1,0:T(8,128)(2,1)S(1)}, u32[]{:S(2)}, u32[]{:S(2)}) %collective-permute-start.2) | collective-permute-done | bytes 393248 | tf_op jit(solution)/shard_map/ppermute | solution.py:27
  50.5 1.5 collective-permute-start.3
  52.3 15.0 %collective-permute-done.5.refs_9_.refs_12_ = bf16[2,384,512]{2,1,0:T(8,128)(2,1)S(1)} collective-permute-done((bf16[2,384,512]{2,1,0:T(8,128)(2,1)S(1)}, bf16[2,384,512]{2,1,0:T(8,128)(2,1)S(1)}, u32[]{:S(2)}, u32[]{:S(2)}) %collective-permute-start.5) | collective-permute-done | bytes 786464 | tf_op jit(solution)/shard_map/ppermute | solution.py:27
  67.3 2.2 %collective-permute-done.3.refs_4_.refs_7_ = bf16[2,384,512]{2,1,0:T(8,128)(2,1)S(1)} collective-permute-done((bf16[2,384,512]{2,1,0:T(8,128)(2,1)S(1)}, bf16[2,384,512]{2,1,0:T(8,128)(2,1)S(1)}, u32[]{:S(2)}, u32[]{:S(2)}) %collective-permute-start.3) | collective-permute-done | bytes 786464 | tf_op jit(solution)/shard_map/ppermute | solution.py:27
  69.6 4.9 %collective-permute-done.9.refs_4_ = bf16[2,352,384]{2,1,0:T(8,128)(2,1)S(1)} collective-permute-done((bf16[2,352,384]{2,1,0:T(8,128)(2,1)S(1)}, bf16[2,352,384]{2,1,0:T(8,128)(2,1)S(1)}, u32[]{:S(2)}, u32[]{:S(2)}) %collective-permute-start.9) | collective-permute-done | bytes 540704 | tf_op jit(solution)/shard_map/ppermute | solution.py:27
  74.5 1.1 copy-done.10
  75.6 5.4 %mixed_terms.2 = (bf16[4,384,512]{2,1,0:T(8,128)(2,1)}, bf16[4,384,512]{2,1,0:T(8,128)(2,1)}) custom-call(bf16[704,384]{1,0:T(8,128)(2,1)S(1)} %bitcast.65, bf16[352,384]{1,0:T(8,128)(2,1)S(1)} %collective-permute-done.6.refs_1_, bf16[2,352,384]{2,1,0:T(8,128)(2,1)S(1)} %collective-permute-done.7.refs_2_, ...), custom_call_target="tpu_custom_call" | custom-call | flops 2214592512 | bytes 8192000 | tf_op jit(solution)/shard_map/mixed_terms/pallas_call | solution.py:221
  81.1 4.6 %collective-permute-start.13 = (bf16[4,384,512]{2,1,0:T(8,128)(2,1)}, bf16[4,384,512]{2,1,0:T(8,128)(2,1)S(1)}, u32[]{:S(2)}, u32[]{:S(2)}) collective-permute-start(bf16[4,384,512]{2,1,0:T(8,128)(2,1)} %get-tuple-element.33), channel_id=1, source_target_pairs={{0,1},{1,0},{2,3},{3,2},{4,5},{5,4},{6,7},{7,6},{8,9},{9,8},{10,11... | collective-permute-start | bytes 4718600 | tf_op jit(solution)/shard_map/ppermute | solution.py:27
  85.7 5.5 %mixed_terms.3 = (bf16[4,384,512]{2,1,0:T(8,128)(2,1)}, bf16[4,384,512]{2,1,0:T(8,128)(2,1)}) custom-call(bf16[704,384]{1,0:T(8,128)(2,1)S(1)} %bitcast.66, bf16[352,384]{1,0:T(8,128)(2,1)S(1)} %collective-permute-done.6.refs_1_, bf16[2,352,384]{2,1,0:T(8,128)(2,1)S(1)} %collective-permute-done.7.refs_2_, ...), custom_call_target="tpu_custom_call" | custom-call | flops 2214592512 | bytes 8192000 | tf_op jit(solution)/shard_map/mixed_terms/pallas_call | solution.py:221
  91.2 0.1 collective-permute-start.15
  91.3 0.5 collective-permute-start.19
  91.8 0.1 collective-permute-start.17
  91.9 0.4 collective-permute-start.20
  92.3 0.1 collective-permute-start.18
  92.4 1.1 add_convert_fusion.1
  93.5 2.8 %collective-permute-done.15 = bf16[4,384,512]{2,1,0:T(8,128)(2,1)S(1)} collective-permute-done((bf16[4,384,512]{2,1,0:T(8,128)(2,1)}, bf16[4,384,512]{2,1,0:T(8,128)(2,1)S(1)}, u32[]{:S(2)}, u32[]{:S(2)}) %collective-permute-start.15) | collective-permute-done | bytes 1572896 | tf_op jit(solution)/shard_map/ppermute | solution.py:27
  96.3 2.1 %collective-permute-start.14 = (bf16[2,384,512]{2,1,0:T(8,128)(2,1)}, bf16[2,384,512]{2,1,0:T(8,128)(2,1)}, u32[]{:S(2)}, u32[]{:S(2)}) collective-permute-start(bf16[2,384,512]{2,1,0:T(8,128)(2,1)} %add_convert_fusion.1), channel_id=1, source_target_pairs={{0,2},{1,3},{2,0},{3,1},{4,6},{5,7},{6,4},{7,5},{8,10},{9,11},{10,... | collective-permute-start | bytes 2359304 | tf_op jit(solution)/shard_map/ppermute | solution.py:27
  98.3 1.1 add_convert_fusion
  99.4 3.9 %collective-permute-start.16 = (bf16[2,384,512]{2,1,0:T(8,128)(2,1)}, bf16[2,384,512]{2,1,0:T(8,128)(2,1)S(1)}, u32[]{:S(2)}, u32[]{:S(2)}) collective-permute-start(bf16[2,384,512]{2,1,0:T(8,128)(2,1)} %add_convert_fusion), channel_id=1, source_target_pairs={{0,6},{1,7},{2,4},{3,5},{4,2},{5,3},{6,0},{7,1},{8,14},{9,15},{10,... | collective-permute-start | bytes 2359304 | tf_op jit(solution)/shard_map/ppermute | solution.py:27
  103.4 0.9 copy-done.14
  104.3 0.9 copy-done.15
  105.2 10.3 %hidden_terms.1 = (f32[352,384]{1,0:T(8,128)S(1)}, bf16[352,384]{1,0:T(8,128)(2,1)S(1)}, bf16[2,352,384]{2,1,0:T(8,128)(2,1)S(1)}, f32[352,384]{1,0:T(8,128)S(1)...) custom-call(bf16[2,704,512]{2,1,0:T(8,128)(2,1)} %bitcast.63, bf16[2,704,512]{2,1,0:T(8,128)(2,1)} %copy-done.10, ...), custom_call_target="tpu_custom_call" | custom-call | flops 4429185024 | bytes 11878400 | tf_op jit(solution)/shard_map/hidden_terms/pallas_call | solution.py:221
  115.5 1.7 collective-permute-start.22
  117.1 0.1 collective-permute-start.21
  117.3 9.4 %weight_terms.1 = (f32[352,512]{1,0:T(8,128)}, bf16[352,512]{1,0:T(8,128)(2,1)S(1)}, bf16[2,352,512]{2,1,0:T(8,128)(2,1)}, f32[352,512]{1,0:T(8,128)}, bf16[352,...) custom-call(bf16[704,384]{1,0:T(8,128)(2,1)S(1)} %bitcast.67, bf16[352,384]{1,0:T(8,128)(2,1)S(1)} %collective-permute-done.6.refs_1_, ...), custom_call_target="tpu_custom_call" | custom-call | flops 4429185024 | bytes 12058624 | tf_op jit(solution)/shard_map/weight_terms/pallas_call | solution.py:221
  126.7 3.1 %collective-permute-done.22 = bf16[2,352,384]{2,1,0:T(8,128)(2,1)} collective-permute-done((bf16[2,352,384]{2,1,0:T(8,128)(2,1)}, bf16[2,352,384]{2,1,0:T(8,128)(2,1)}, u32[]{:S(2)}, u32[]{:S(2)}) %collective-permute-start.22) | collective-permute-done | bytes 540704 | tf_op jit(solution)/shard_map/ppermute | solution.py:27
  129.8 11.6 %collective-permute-done.21 = bf16[2,352,384]{2,1,0:T(8,128)(2,1)S(1)} collective-permute-done((bf16[2,352,384]{2,1,0:T(8,128)(2,1)S(1)}, bf16[2,352,384]{2,1,0:T(8,128)(2,1)S(1)}, u32[]{:S(2)}, u32[]{:S(2)}) %collective-permute-start.21) | collective-permute-done | bytes 540704 | tf_op jit(solution)/shard_map/ppermute | solution.py:27
  141.4 1.2 fusion.6
  142.6 3.0 %collective-permute-start.30 = (bf16[352,384]{1,0:T(8,128)(2,1)S(1)}, bf16[352,384]{1,0:T(8,128)(2,1)S(1)}, u32[]{:S(2)}, u32[]{:S(2)}) collective-permute-start(bf16[352,384]{1,0:T(8,128)(2,1)S(1)} %fusion.6), channel_id=1, source_target_pairs={{0,48},{1,49},{2,50},{3,51},{4,52},{5,53},{6,54},{7,55},{8,56},{9,... | collective-permute-start | bytes 811016 | tf_op jit(solution)/shard_map/ppermute | solution.py:27
  145.8 1.2 fusion.12
  147.1 0.2 fusion.13
  147.4 1.3 collective-permute-start.23
  148.7 2.9 %collective-permute-done.30 = bf16[352,384]{1,0:T(8,128)(2,1)S(1)} collective-permute-done((bf16[352,384]{1,0:T(8,128)(2,1)S(1)}, bf16[352,384]{1,0:T(8,128)(2,1)S(1)}, u32[]{:S(2)}, u32[]{:S(2)}) %collective-permute-start.30) | collective-permute-done | bytes 270368 | tf_op jit(solution)/shard_map/ppermute | solution.py:27
  151.7 1.1 fusion.8
  152.8 6.0 %collective-permute-done.29 = bf16[352,384]{1,0:T(8,128)(2,1)S(1)} collective-permute-done((bf16[352,384]{1,0:T(8,128)(2,1)S(1)}, bf16[352,384]{1,0:T(8,128)(2,1)S(1)}, u32[]{:S(2)}, u32[]{:S(2)}) %collective-permute-start.29) | collective-permute-done | bytes 270368 | tf_op jit(solution)/shard_map/ppermute | solution.py:27
  158.9 0.9 maximum_bitcast_fusion
  159.7 0.2 fusion
  159.9 6.2 %collective-permute-start.28 = (bf16[384,512]{1,0:T(8,128)(2,1)S(1)}, bf16[384,512]{1,0:T(8,128)(2,1)S(1)}, u32[]{:S(2)}, u32[]{:S(2)}) collective-permute-start(bf16[384,512]{1,0:T(8,128)(2,1)S(1)} %fusion), channel_id=1, source_target_pairs={{0,44},{1,60},{2,40},{3,56},{12,36},{13,52},{14,32},{15,48},{20,61... | collective-permute-start | bytes 1179656 | tf_op jit(solution)/shard_map/ppermute | solution.py:27
  166.2 0.7 collective-permute-start.27
  166.9 1.2 fusion.1
  168.1 1.3 collective-permute-start.25
  169.4 9.5 %collective-permute-start.24 = (bf16[384,512]{1,0:T(8,128)(2,1)S(1)}, bf16[384,512]{1,0:T(8,128)(2,1)S(1)}, u32[]{:S(2)}, u32[]{:S(2)}) collective-permute-start(bf16[384,512]{1,0:T(8,128)(2,1)S(1)} %fusion.1), channel_id=1, source_target_pairs={{0,0},{1,16},{2,4},{3,20},{12,8},{13,24},{14,12},{15,28},{20,17},{... | collective-permute-start | bytes 1179656 | tf_op jit(solution)/shard_map/ppermute | solution.py:27
  179.2 0.3 collective-permute-start.34
  179.5 5.2 %collective-permute-done.25 = bf16[384,512]{1,0:T(8,128)(2,1)S(1)} collective-permute-done((bf16[384,512]{1,0:T(8,128)(2,1)S(1)}, bf16[384,512]{1,0:T(8,128)(2,1)S(1)}, u32[]{:S(2)}, u32[]{:S(2)}) %collective-permute-start.25) | collective-permute-done | bytes 393248 | tf_op jit(solution)/shard_map/ppermute | solution.py:27
  184.8 1.2 collective-permute-done.24
  185.9 0.9 add_convert_fusion.2
  186.9 0.1 fusion.5
  187.0 2.6 %collective-permute-done.34 = bf16[352,512]{1,0:T(8,128)(2,1)S(1)} collective-permute-done((bf16[352,512]{1,0:T(8,128)(2,1)S(1)}, bf16[352,512]{1,0:T(8,128)(2,1)S(1)}, u32[]{:S(2)}, u32[]{:S(2)}) %collective-permute-start.34) | collective-permute-done | bytes 360480 | tf_op jit(solution)/shard_map/ppermute | solution.py:27
  189.6 0.1 fusion.3
  189.8 1.2 pad_maximum_fusion.1
  (76 shorter events, 1.6 us)
Async XLA Ops:
  0.6 36.2 %collective-permute-start.1 = (bf16[384,512]{1,0:T(8,128)(2,1)}, bf16[384,512]{1,0:T(8,128)(2,1)S(1)}, u32[]{:S(2)}, u32[]{:S(2)}) collective-permute-start(bf16[384,512]{1,0:T(8,128)(2,1)} %param.7), channel_id=1, source_target_pairs={{0,10},{1,31},{2,42},{3,63},{4,8},{5,29},{6,40},{7,61},{8,6},{9,19... | collective-permute-start | bytes 1179656 | tf_op jit(solution)/shard_map/ppermute | solution.py:27
  12.0 1.1 copy-start.9
  13.1 1.9 copy-start.18
  13.4 26.4 %copy-start.1 = (bf16[384,704]{0,1:T(8,128)(2,1)S(1)}, bf16[384,704]{0,1:T(8,128)(2,1)}, u32[]{:S(2)}) copy-start(bf16[384,704]{0,1:T(8,128)(2,1)} %param.4) | copy-start | bytes 1622020
  13.4 23.4 %collective-permute-start.10 = (bf16[352,512]{1,0:T(8,128)(2,1)S(1)}, bf16[352,512]{1,0:T(8,128)(2,1)S(1)}, u32[]{:S(2)}, u32[]{:S(2)}) collective-permute-start(bf16[352,512]{1,0:T(8,128)(2,1)S(1)} %get-tuple-element.57), channel_id=1, source_target_pairs={{0,64},{1,65},{2,66},{3,67},{4,68},{5,69},{6,70},{7,71},{8,72},{9,... | collective-permute-start | bytes 1081352 | tf_op jit(solution)/shard_map/ppermute | solution.py:27
  14.8 22.0 %collective-permute-start.11 = (bf16[352,512]{1,0:T(8,128)(2,1)S(1)}, bf16[352,512]{1,0:T(8,128)(2,1)S(1)}, u32[]{:S(2)}, u32[]{:S(2)}) collective-permute-start(bf16[352,512]{1,0:T(8,128)(2,1)S(1)} %get-tuple-element.58), channel_id=1, source_target_pairs={{0,64},{1,65},{2,66},{3,67},{4,68},{5,69},{6,70},{7,71},{8,72},{9,... | collective-permute-start | bytes 1081352 | tf_op jit(solution)/shard_map/ppermute | solution.py:27
  15.0 24.8 %collective-permute-start = (bf16[384,512]{1,0:T(8,128)(2,1)S(1)}, bf16[384,512]{1,0:T(8,128)(2,1)S(1)}, u32[]{:S(2)}, u32[]{:S(2)}) collective-permute-start(bf16[384,512]{1,0:T(8,128)(2,1)S(1)} %copy-done.18), channel_id=1, source_target_pairs={{0,0},{1,21},{2,32},{3,53},{4,2},{5,23},{6,34},{7,55},{8,12},{9,25... | collective-permute-start | bytes 1179656 | tf_op jit(solution)/shard_map/ppermute | solution.py:27
  36.8 9.4 %collective-permute-start.4 = (bf16[384,512]{1,0:T(8,128)(2,1)S(1)}, bf16[384,512]{1,0:T(8,128)(2,1)S(1)}, u32[]{:S(2)}, u32[]{:S(2)}) collective-permute-start(bf16[384,512]{1,0:T(8,128)(2,1)S(1)} %collective-permute-done.1.refs_7_.refs_10_), channel_id=1, source_target_pairs={{0,6},{1,7},{2,4},{3,5},{4,2},{5,3},{6,0},{7,1},{8,14},{9,15},{10,... | collective-permute-start | bytes 1179656 | tf_op jit(solution)/shard_map/ppermute | solution.py:27
  36.9 48.8 %copy-start = (bf16[1408,512]{1,0:T(8,128)(2,1)}, bf16[1408,512]{1,0:T(8,128)(2,1)S(1)}, u32[]{:S(2)}) copy-start(bf16[1408,512]{1,0:T(8,128)(2,1)S(1)} %pad_maximum_fusion) | copy-start | bytes 4325380
  37.0 37.6 %collective-permute-start.12 = (bf16[2,704,512]{2,1,0:T(8,128)(2,1)S(1)}, bf16[2,704,512]{2,1,0:T(8,128)(2,1)S(1)}, u32[]{:S(2)}, u32[]{:S(2)}) collective-permute-start(bf16[2,704,512]{2,1,0:T(8,128)(2,1)S(1)} %bitcast.60), channel_id=1, source_target_pairs={{0,192},{1,193},{2,194},{3,195},{4,196},{5,197},{6,198},{7,199},{8... | collective-permute-start | bytes 4325384 | tf_op jit(solution)/shard_map/ppermute | solution.py:27
  39.8 10.7 %collective-permute-start.2 = (bf16[384,512]{1,0:T(8,128)(2,1)S(1)}, bf16[384,512]{1,0:T(8,128)(2,1)S(1)}, u32[]{:S(2)}, u32[]{:S(2)}) collective-permute-start(bf16[384,512]{1,0:T(8,128)(2,1)S(1)} %collective-permute-done.refs_2_.refs_5_), channel_id=1, source_target_pairs={{0,2},{1,3},{2,0},{3,1},{4,6},{5,7},{6,4},{7,5},{8,10},{9,11},{10,... | collective-permute-start | bytes 1179656 | tf_op jit(solution)/shard_map/ppermute | solution.py:27
  39.9 12.1 %collective-permute-start.6 = (bf16[352,384]{1,0:T(8,128)(2,1)S(1)}, bf16[352,384]{1,0:T(8,128)(2,1)S(1)}, u32[]{:S(2)}, u32[]{:S(2)}) collective-permute-start(bf16[352,384]{1,0:T(8,128)(2,1)S(1)} %get-tuple-element.62), channel_id=1, source_target_pairs={{0,16},{1,17},{2,18},{3,19},{4,20},{5,21},{6,22},{7,23},{8,24},{9,... | collective-permute-start | bytes 811016 | tf_op jit(solution)/shard_map/ppermute | solution.py:27
  40.0 12.2 %collective-permute-start.8 = (bf16[352,384]{1,0:T(8,128)(2,1)S(1)}, bf16[352,384]{1,0:T(8,128)(2,1)S(1)}, u32[]{:S(2)}, u32[]{:S(2)}) collective-permute-start(bf16[352,384]{1,0:T(8,128)(2,1)S(1)} %get-tuple-element.61), channel_id=1, source_target_pairs={{0,48},{1,49},{2,50},{3,51},{4,52},{5,53},{6,54},{7,55},{8,56},{9,... | collective-permute-start | bytes 811016 | tf_op jit(solution)/shard_map/ppermute | solution.py:27
  46.3 21.0 %collective-permute-start.5 = (bf16[2,384,512]{2,1,0:T(8,128)(2,1)S(1)}, bf16[2,384,512]{2,1,0:T(8,128)(2,1)S(1)}, u32[]{:S(2)}, u32[]{:S(2)}) collective-permute-start(bf16[2,384,512]{2,1,0:T(8,128)(2,1)S(1)} %pad_maximum_fusion.3), channel_id=1, source_target_pairs={{0,2},{1,3},{2,0},{3,1},{4,6},{5,7},{6,4},{7,5},{8,10},{9,11},{10,... | collective-permute-start | bytes 2359304 | tf_op jit(solution)/shard_map/ppermute | solution.py:27
  50.5 19.0 %collective-permute-start.3 = (bf16[2,384,512]{2,1,0:T(8,128)(2,1)S(1)}, bf16[2,384,512]{2,1,0:T(8,128)(2,1)S(1)}, u32[]{:S(2)}, u32[]{:S(2)}) collective-permute-start(bf16[2,384,512]{2,1,0:T(8,128)(2,1)S(1)} %pad_maximum_fusion.2), channel_id=1, source_target_pairs={{0,6},{1,7},{2,4},{3,5},{4,2},{5,3},{6,0},{7,1},{8,14},{9,15},{10,... | collective-permute-start | bytes 2359304 | tf_op jit(solution)/shard_map/ppermute | solution.py:27
  52.1 17.5 %collective-permute-start.7 = (bf16[2,352,384]{2,1,0:T(8,128)(2,1)S(1)}, bf16[2,352,384]{2,1,0:T(8,128)(2,1)S(1)}, u32[]{:S(2)}, u32[]{:S(2)}) collective-permute-start(bf16[2,352,384]{2,1,0:T(8,128)(2,1)S(1)} %pad_maximum_fusion.4), channel_id=1, source_target_pairs={{0,48},{1,49},{2,50},{3,51},{4,52},{5,53},{6,54},{7,55},{8,56},{9,... | collective-permute-start | bytes 1622024 | tf_op jit(solution)/shard_map/ppermute | solution.py:27
  52.2 22.3 %collective-permute-start.9 = (bf16[2,352,384]{2,1,0:T(8,128)(2,1)S(1)}, bf16[2,352,384]{2,1,0:T(8,128)(2,1)S(1)}, u32[]{:S(2)}, u32[]{:S(2)}) collective-permute-start(bf16[2,352,384]{2,1,0:T(8,128)(2,1)S(1)} %pad_maximum_fusion.5), channel_id=1, source_target_pairs={{0,16},{1,17},{2,18},{3,19},{4,20},{5,21},{6,22},{7,23},{8,24},{9,... | collective-permute-start | bytes 1622024 | tf_op jit(solution)/shard_map/ppermute | solution.py:27
  67.3 24.6 %copy-start.11 = (bf16[2,384,512]{2,1,0:T(8,128)(2,1)}, bf16[2,384,512]{2,1,0:T(8,128)(2,1)S(1)}, u32[]{:S(2)}) copy-start(bf16[2,384,512]{2,1,0:T(8,128)(2,1)S(1)} %collective-permute-done.5.refs_9_.refs_12_) | copy-start | bytes 2359300
  69.6 22.7 %copy-start.12 = (bf16[2,384,512]{2,1,0:T(8,128)(2,1)}, bf16[2,384,512]{2,1,0:T(8,128)(2,1)S(1)}, u32[]{:S(2)}) copy-start(bf16[2,384,512]{2,1,0:T(8,128)(2,1)S(1)} %collective-permute-done.3.refs_4_.refs_7_) | copy-start | bytes 2359300
  74.5 11.2 %copy-start.2 = (bf16[2,352,384]{2,1,0:T(8,128)(2,1)}, bf16[2,352,384]{2,1,0:T(8,128)(2,1)S(1)}, u32[]{:S(2)}) copy-start(bf16[2,352,384]{2,1,0:T(8,128)(2,1)S(1)} %collective-permute-done.9.refs_4_) | copy-start | bytes 1622020
  74.5 1.1 copy-start.10
  81.1 11.3 %copy-start.3 = (bf16[4,384,512]{2,1,0:T(8,128)(2,1)S(1)}, bf16[4,384,512]{2,1,0:T(8,128)(2,1)}, u32[]{:S(2)}) copy-start(bf16[4,384,512]{2,1,0:T(8,128)(2,1)} %get-tuple-element.32) | copy-start | bytes 4718596
  81.1 11.2 %collective-permute-start.13 = (bf16[4,384,512]{2,1,0:T(8,128)(2,1)}, bf16[4,384,512]{2,1,0:T(8,128)(2,1)S(1)}, u32[]{:S(2)}, u32[]{:S(2)}) collective-permute-start(bf16[4,384,512]{2,1,0:T(8,128)(2,1)} %get-tuple-element.33), channel_id=1, source_target_pairs={{0,1},{1,0},{2,3},{3,2},{4,5},{5,4},{6,7},{7,6},{8,9},{9,8},{10,11... | collective-permute-start | bytes 4718600 | tf_op jit(solution)/shard_map/ppermute | solution.py:27
  91.2 7.2 %copy-start.4 = (bf16[4,384,512]{2,1,0:T(8,128)(2,1)S(1)}, bf16[4,384,512]{2,1,0:T(8,128)(2,1)}, u32[]{:S(2)}) copy-start(bf16[4,384,512]{2,1,0:T(8,128)(2,1)} %get-tuple-element.35) | copy-start | bytes 4718596
  91.2 5.1 %collective-permute-start.15 = (bf16[4,384,512]{2,1,0:T(8,128)(2,1)}, bf16[4,384,512]{2,1,0:T(8,128)(2,1)S(1)}, u32[]{:S(2)}, u32[]{:S(2)}) collective-permute-start(bf16[4,384,512]{2,1,0:T(8,128)(2,1)} %get-tuple-element.36), channel_id=1, source_target_pairs={{0,1},{1,0},{2,3},{3,2},{4,5},{5,4},{6,7},{7,6},{8,9},{9,8},{10,11... | collective-permute-start | bytes 4718600 | tf_op jit(solution)/shard_map/ppermute | solution.py:27
  91.3 8.1 %collective-permute-start.19 = (bf16[2,384,512]{2,1,0:T(8,128)(2,1)S(1)}, bf16[2,384,512]{2,1,0:T(8,128)(2,1)S(1)}, u32[]{:S(2)}, u32[]{:S(2)}) collective-permute-start(bf16[2,384,512]{2,1,0:T(8,128)(2,1)S(1)} %pad_maximum_fusion.3), channel_id=1, source_target_pairs={{0,1},{1,0},{2,3},{3,2},{4,5},{5,4},{6,7},{7,6},{8,9},{9,8},{10,11... | collective-permute-start | bytes 2359304 | tf_op jit(solution)/shard_map/ppermute | solution.py:27
  91.8 11.6 %collective-permute-start.17 = (bf16[2,384,512]{2,1,0:T(8,128)(2,1)S(1)}, bf16[2,384,512]{2,1,0:T(8,128)(2,1)S(1)}, u32[]{:S(2)}, u32[]{:S(2)}) collective-permute-start(bf16[2,384,512]{2,1,0:T(8,128)(2,1)S(1)} %pad_maximum_fusion.2), channel_id=1, source_target_pairs={{0,1},{1,0},{2,3},{3,2},{4,5},{5,4},{6,7},{7,6},{8,9},{9,8},{10,11... | collective-permute-start | bytes 2359304 | tf_op jit(solution)/shard_map/ppermute | solution.py:27
  91.9 11.5 %collective-permute-start.20 = (bf16[2,384,512]{2,1,0:T(8,128)(2,1)S(1)}, bf16[2,384,512]{2,1,0:T(8,128)(2,1)S(1)}, u32[]{:S(2)}, u32[]{:S(2)}) collective-permute-start(bf16[2,384,512]{2,1,0:T(8,128)(2,1)S(1)} %collective-permute-done.5.refs_9_.refs_12_), channel_id=1, source_target_pairs={{0,1},{1,0},{2,3},{3,2},{4,5},{5,4},{6,7},{7,6},{8,9},{9,8},{10,11... | collective-permute-start | bytes 2359304 | tf_op jit(solution)/shard_map/ppermute | solution.py:27
  92.3 12.9 %collective-permute-start.18 = (bf16[2,384,512]{2,1,0:T(8,128)(2,1)S(1)}, bf16[2,384,512]{2,1,0:T(8,128)(2,1)}, u32[]{:S(2)}, u32[]{:S(2)}) collective-permute-start(bf16[2,384,512]{2,1,0:T(8,128)(2,1)S(1)} %collective-permute-done.3.refs_4_.refs_7_), channel_id=1, source_target_pairs={{0,1},{1,0},{2,3},{3,2},{4,5},{5,4},{6,7},{7,6},{8,9},{9,8},{10,11... | collective-permute-start | bytes 2359304 | tf_op jit(solution)/shard_map/ppermute | solution.py:27
  96.3 45.1 %collective-permute-start.14 = (bf16[2,384,512]{2,1,0:T(8,128)(2,1)}, bf16[2,384,512]{2,1,0:T(8,128)(2,1)}, u32[]{:S(2)}, u32[]{:S(2)}) collective-permute-start(bf16[2,384,512]{2,1,0:T(8,128)(2,1)} %add_convert_fusion.1), channel_id=1, source_target_pairs={{0,2},{1,3},{2,0},{3,1},{4,6},{5,7},{6,4},{7,5},{8,10},{9,11},{10,... | collective-permute-start | bytes 2359304 | tf_op jit(solution)/shard_map/ppermute | solution.py:27
  99.4 3.9 %copy-start.13 = (bf16[2,384,512]{2,1,0:T(8,128)(2,1)}, bf16[2,384,512]{2,1,0:T(8,128)(2,1)S(1)}, u32[]{:S(2)}) copy-start(bf16[2,384,512]{2,1,0:T(8,128)(2,1)S(1)} %collective-permute-done.19.refs_10_.refs_13_) | copy-start | bytes 2359300
  99.4 42.0 %collective-permute-start.16 = (bf16[2,384,512]{2,1,0:T(8,128)(2,1)}, bf16[2,384,512]{2,1,0:T(8,128)(2,1)S(1)}, u32[]{:S(2)}, u32[]{:S(2)}) collective-permute-start(bf16[2,384,512]{2,1,0:T(8,128)(2,1)} %add_convert_fusion), channel_id=1, source_target_pairs={{0,6},{1,7},{2,4},{3,5},{4,2},{5,3},{6,0},{7,1},{8,14},{9,15},{10,... | collective-permute-start | bytes 2359304 | tf_op jit(solution)/shard_map/ppermute | solution.py:27
  103.3 0.9 copy-start.14
  104.3 0.9 copy-start.15
  115.5 14.3 %collective-permute-start.22 = (bf16[2,352,384]{2,1,0:T(8,128)(2,1)}, bf16[2,352,384]{2,1,0:T(8,128)(2,1)}, u32[]{:S(2)}, u32[]{:S(2)}) collective-permute-start(bf16[2,352,384]{2,1,0:T(8,128)(2,1)} %get-tuple-element.39), channel_id=1, source_target_pairs={{0,16},{1,17},{2,18},{3,19},{4,20},{5,21},{6,22},{7,23},{8,24},{9,... | collective-permute-start | bytes 1622024 | tf_op jit(solution)/shard_map/ppermute | solution.py:27
  117.1 24.3 %collective-permute-start.21 = (bf16[2,352,384]{2,1,0:T(8,128)(2,1)S(1)}, bf16[2,352,384]{2,1,0:T(8,128)(2,1)S(1)}, u32[]{:S(2)}, u32[]{:S(2)}) collective-permute-start(bf16[2,352,384]{2,1,0:T(8,128)(2,1)S(1)} %get-tuple-element.38), channel_id=1, source_target_pairs={{0,48},{1,49},{2,50},{3,51},{4,52},{5,53},{6,54},{7,55},{8,56},{9,... | collective-permute-start | bytes 1622024 | tf_op jit(solution)/shard_map/ppermute | solution.py:27
  141.4 5.7 %copy-start.5 = (bf16[2,384,512]{2,1,0:T(8,128)(2,1)}, bf16[2,384,512]{2,1,0:T(8,128)(2,1)S(1)}, u32[]{:S(2)}) copy-start(bf16[2,384,512]{2,1,0:T(8,128)(2,1)S(1)} %collective-permute-done.16) | copy-start | bytes 2359300
  142.6 9.0 %collective-permute-start.30 = (bf16[352,384]{1,0:T(8,128)(2,1)S(1)}, bf16[352,384]{1,0:T(8,128)(2,1)S(1)}, u32[]{:S(2)}, u32[]{:S(2)}) collective-permute-start(bf16[352,384]{1,0:T(8,128)(2,1)S(1)} %fusion.6), channel_id=1, source_target_pairs={{0,48},{1,49},{2,50},{3,51},{4,52},{5,53},{6,54},{7,55},{8,56},{9,... | collective-permute-start | bytes 811016 | tf_op jit(solution)/shard_map/ppermute | solution.py:27
  145.7 2.9 %copy-start.17 = (bf16[2,352,512]{2,1,0:T(8,128)(2,1)S(1)}, bf16[2,352,512]{2,1,0:T(8,128)(2,1)}, u32[]{:S(2)}) copy-start(bf16[2,352,512]{2,1,0:T(8,128)(2,1)} %get-tuple-element.51) | copy-start | bytes 2162692
  145.7 5.9 %copy-start.16 = (bf16[2,352,512]{2,1,0:T(8,128)(2,1)S(1)}, bf16[2,352,512]{2,1,0:T(8,128)(2,1)}, u32[]{:S(2)}) copy-start(bf16[2,352,512]{2,1,0:T(8,128)(2,1)} %get-tuple-element.55) | copy-start | bytes 2162692
  145.7 13.0 %collective-permute-start.29 = (bf16[352,384]{1,0:T(8,128)(2,1)S(1)}, bf16[352,384]{1,0:T(8,128)(2,1)S(1)}, u32[]{:S(2)}, u32[]{:S(2)}) collective-permute-start(bf16[352,384]{1,0:T(8,128)(2,1)S(1)} %fusion.9), channel_id=1, source_target_pairs={{0,16},{1,17},{2,18},{3,19},{4,20},{5,21},{6,22},{7,23},{8,24},{9,... | collective-permute-start | bytes 811016 | tf_op jit(solution)/shard_map/ppermute | solution.py:27
  147.3 12.5 %collective-permute-start.26 = (bf16[384,512]{1,0:T(8,128)(2,1)S(1)}, bf16[384,512]{1,0:T(8,128)(2,1)S(1)}, u32[]{:S(2)}, u32[]{:S(2)}) collective-permute-start(bf16[384,512]{1,0:T(8,128)(2,1)S(1)} %fusion.13), channel_id=1, source_target_pairs={{0,2},{1,3},{2,0},{3,1},{4,6},{5,7},{6,4},{7,5},{8,10},{9,11},{10,... | collective-permute-start | bytes 1179656 | tf_op jit(solution)/shard_map/ppermute | solution.py:27
  147.4 19.5 %collective-permute-start.23 = (bf16[384,512]{1,0:T(8,128)(2,1)S(1)}, bf16[384,512]{1,0:T(8,128)(2,1)S(1)}, u32[]{:S(2)}, u32[]{:S(2)}) collective-permute-start(bf16[384,512]{1,0:T(8,128)(2,1)S(1)} %fusion.12), channel_id=1, source_target_pairs={{0,6},{1,7},{2,4},{3,5},{4,2},{5,3},{6,0},{7,1},{8,14},{9,15},{10,... | collective-permute-start | bytes 1179656 | tf_op jit(solution)/shard_map/ppermute | solution.py:27
  148.7 20.7 %collective-permute-start.31 = (bf16[2,352,512]{2,1,0:T(8,128)(2,1)S(1)}, bf16[2,352,512]{2,1,0:T(8,128)(2,1)S(1)}, u32[]{:S(2)}, u32[]{:S(2)}) collective-permute-start(bf16[2,352,512]{2,1,0:T(8,128)(2,1)S(1)} %copy-done.17), channel_id=1, source_target_pairs={{0,192},{1,193},{2,194},{3,195},{4,196},{5,197},{6,198},{7,199},{8... | collective-permute-start | bytes 2162696 | tf_op jit(solution)/shard_map/ppermute | solution.py:27
  151.6 27.4 %collective-permute-start.33 = (bf16[2,352,512]{2,1,0:T(8,128)(2,1)S(1)}, bf16[2,352,512]{2,1,0:T(8,128)(2,1)S(1)}, u32[]{:S(2)}, u32[]{:S(2)}) collective-permute-start(bf16[2,352,512]{2,1,0:T(8,128)(2,1)S(1)} %copy-done.16), channel_id=1, source_target_pairs={{0,64},{1,65},{2,66},{3,67},{4,68},{5,69},{6,70},{7,71},{8,72},{9,... | collective-permute-start | bytes 2162696 | tf_op jit(solution)/shard_map/ppermute | solution.py:27
  151.7 8.1 %copy-start.6 = (bf16[2,384,512]{2,1,0:T(8,128)(2,1)S(1)}, bf16[2,384,512]{2,1,0:T(8,128)(2,1)}, u32[]{:S(2)}) copy-start(bf16[2,384,512]{2,1,0:T(8,128)(2,1)} %copy-done.5) | copy-start | bytes 2359300
  159.9 19.3 %collective-permute-start.28 = (bf16[384,512]{1,0:T(8,128)(2,1)S(1)}, bf16[384,512]{1,0:T(8,128)(2,1)S(1)}, u32[]{:S(2)}, u32[]{:S(2)}) collective-permute-start(bf16[384,512]{1,0:T(8,128)(2,1)S(1)} %fusion), channel_id=1, source_target_pairs={{0,44},{1,60},{2,40},{3,56},{12,36},{13,52},{14,32},{15,48},{20,61... | collective-permute-start | bytes 1179656 | tf_op jit(solution)/shard_map/ppermute | solution.py:27
  166.2 13.3 %collective-permute-start.27 = (bf16[384,512]{1,0:T(8,128)(2,1)S(1)}, bf16[384,512]{1,0:T(8,128)(2,1)S(1)}, u32[]{:S(2)}, u32[]{:S(2)}) collective-permute-start(bf16[384,512]{1,0:T(8,128)(2,1)S(1)} %fusion), channel_id=1, source_target_pairs={{4,32},{5,48},{6,36},{7,52},{8,40},{9,56},{10,44},{11,60},{16,49},... | collective-permute-start | bytes 1179656 | tf_op jit(solution)/shard_map/ppermute | solution.py:27
  168.1 16.7 %collective-permute-start.25 = (bf16[384,512]{1,0:T(8,128)(2,1)S(1)}, bf16[384,512]{1,0:T(8,128)(2,1)S(1)}, u32[]{:S(2)}, u32[]{:S(2)}) collective-permute-start(bf16[384,512]{1,0:T(8,128)(2,1)S(1)} %fusion.1), channel_id=1, source_target_pairs={{4,12},{5,28},{6,8},{7,24},{8,4},{9,20},{10,0},{11,16},{16,29},{17... | collective-permute-start | bytes 1179656 | tf_op jit(solution)/shard_map/ppermute | solution.py:27
  169.4 16.5 %collective-permute-start.24 = (bf16[384,512]{1,0:T(8,128)(2,1)S(1)}, bf16[384,512]{1,0:T(8,128)(2,1)S(1)}, u32[]{:S(2)}, u32[]{:S(2)}) collective-permute-start(bf16[384,512]{1,0:T(8,128)(2,1)S(1)} %fusion.1), channel_id=1, source_target_pairs={{0,0},{1,16},{2,4},{3,20},{12,8},{13,24},{14,12},{15,28},{20,17},{... | collective-permute-start | bytes 1179656 | tf_op jit(solution)/shard_map/ppermute | solution.py:27
  179.0 7.9 %copy-start.8 = (f32[352,512]{1,0:T(8,128)S(1)}, f32[352,512]{1,0:T(8,128)}, u32[]{:S(2)}) copy-start(f32[352,512]{1,0:T(8,128)} %get-tuple-element.50) | copy-start | bytes 2162692
  179.0 7.9 %collective-permute-start.32 = (bf16[352,512]{1,0:T(8,128)(2,1)S(1)}, bf16[352,512]{1,0:T(8,128)(2,1)S(1)}, u32[]{:S(2)}, u32[]{:S(2)}) collective-permute-start(bf16[352,512]{1,0:T(8,128)(2,1)S(1)} %fusion.4), channel_id=1, source_target_pairs={{0,64},{1,65},{2,66},{3,67},{4,68},{5,69},{6,70},{7,71},{8,72},{9,... | collective-permute-start | bytes 1081352 | tf_op jit(solution)/shard_map/ppermute | solution.py:27
  179.2 10.4 %collective-permute-start.34 = (bf16[352,512]{1,0:T(8,128)(2,1)S(1)}, bf16[352,512]{1,0:T(8,128)(2,1)S(1)}, u32[]{:S(2)}, u32[]{:S(2)}) collective-permute-start(bf16[352,512]{1,0:T(8,128)(2,1)S(1)} %fusion.2), channel_id=1, source_target_pairs={{0,192},{1,193},{2,194},{3,195},{4,196},{5,197},{6,198},{7,199},{8... | collective-permute-start | bytes 1081352 | tf_op jit(solution)/shard_map/ppermute | solution.py:27
  186.9 2.7 %copy-start.7 = (f32[352,512]{1,0:T(8,128)S(1)}, f32[352,512]{1,0:T(8,128)}, u32[]{:S(2)}) copy-start(f32[352,512]{1,0:T(8,128)} %get-tuple-element.53) | copy-start | bytes 2162692

commit v3 on v2

--- a/solution.py
+++ b/solution.py
@@ -46,27 +46,16 @@
         column = zh * 8 + x * 2 + c
         plane, p, q = column % 4, column // 8, column // 4 % 2
         r = plane ^ zl
-        return (y, plane, p ^ kind, 2 * (r // 2 ^ plane % 2 ^ plane // 2 ^ p) + (q ^ kind), r % 2)
-
-    return target
-
-
-def from_plane(kind, part):
-    back = inverse(to_plane(kind))
-
-    def target(y, zl, zh, x, c):
-        if x // 2 ^ zl % 2 ^ zl // 2 ^ zh ^ kind != part:
-            return None
-        return back(y, zl, zh, x, c)
+        return (y, plane, p ^ 1 - kind, 2 * (r // 2 ^ plane % 2 ^ plane // 2 ^ p) + (q ^ 1 - kind), r % 2)
 
     return target
 
 
 def place_of(kind, other, s):
     y, zl, zh, x, c = (lax.axis_index(name) for name in AXES)
-    x, p = x ^ s, zh ^ kind
+    x, p = x ^ s, zh ^ 1 - kind
     r = 2 * ((x // 2) ^ (zl % 2) ^ (zl // 2) ^ p) + (c ^ other)
-    return r, y ^ (2 * p + ((x % 2) ^ kind))
+    return r, y ^ (2 * p + ((x % 2) ^ 1 - kind))
 
 
 def step_for(part, k):
@@ -234,9 +223,11 @@
     return lax.optimization_barrier((value, *others))[0]
 
 
-def finish(parts, axis, order, first):
+def finish(parts, axis, order, first, mids, *before):
     mine, mid, _ = parts
     mid = (mid.astype(f32) + first[1].astype(f32)).astype(bf16)
+    mid = after(mid, *before)
+    mids.append(mid)
     second = permute(mid, partner(axis, order[1]))
     return mine + first[0].astype(f32) + second.astype(f32)
 
@@ -291,17 +282,19 @@
         share = (keep[2:].astype(f32) + got[2:].astype(f32)).astype(bf16)
         return share, permute(share, partner("x", ORDERS[part][0]))
 
-    def take(part, keep, got, first, *before):
+    def pass_on(part, keep, got, first):
         mid = (keep[1].astype(f32) + got[1].astype(f32) + first[1].astype(f32)).astype(bf16)
-        second = permute(after(mid, *before), partner("x", ORDERS[part][1]))
-        total = keep[0].astype(f32) + got[0].astype(f32) + first[0].astype(f32) + second.astype(f32)
-        return second, [permute(total.astype(bf16), from_plane(kind, part)) for kind in (0, 1)]
+        return mid, permute(mid, partner("x", ORDERS[part][1]))
+
+    def total(keep, got, first, second):
+        parts = (keep[0], got[0], first[0], second)
+        return sum(v.astype(f32) for v in parts).astype(bf16)
 
     send0, keep0 = mixed_terms(0, *u_rest)
     got0 = permute(send0, partner("c", 1))
     share0, first0 = give(0, keep0, got0)
     send1, keep1 = mixed_terms(1, send0)
-    got1 = permute(send1, partner("c", 1))
+    got1 = permute(after(send1, got0), partner("c", 1))
     share1, first1 = give(1, keep1, got1)
     orders = ORDERS[::-1]
     backs = call(
@@ -321,9 +314,11 @@
         "hidden_terms",
     )
     sent = [permute(backs[3 * i + 2], partner("zl", orders[i][0])) for i in range(2)]
+    mid0, second0 = pass_on(0, keep0, got0, first0)
+    mid1, second1 = pass_on(1, keep1, got1, first1)
     grads = call(
         functools.partial(weight_kernel, factor, orders),
-        [after(hiddens[0], backs[2], share1), *hiddens[1:], *cots],
+        [after(hiddens[0], backs[2], mid0, mid1), *hiddens[1:], *cots],
         [shape((half, d), f32), shape((half, d), bf16), shape((2, half, d), bf16)] * 2,
         [
             pltpu.VMEM((f, 4 * t), bf16),
@@ -337,17 +332,24 @@
         flops,
         "weight_terms",
     )
-    first0, first1, *sent = lax.optimization_barrier((first0, first1, *sent, grads[2]))[:4]
-    second0, ends = take(0, keep0, got0, first0)
-    back = [finish(backs[3 * i : 3 * i + 3], "zl", orders[i], sent[i]) for i in range(2)]
-    second1, more = take(1, keep1, got1, first1)
-    ends += more
-    grad = []
-    for i in range(2):
-        send = after(grads[3 * i + 2], first0, first1, *sent)
-        first = permute(send, partner("y", orders[i][0]))
-        grad.append(finish(grads[3 * i : 3 * i + 3], "y", orders[i], first))
-    mixed = sum(v.astype(f32) for v in ends).astype(bf16)
+    second0, second1 = lax.optimization_barrier((second0, second1, grads[2]))[:2]
+    others = [
+        permute(after(grads[3 * i + 2], second0, second1), partner("y", orders[i][0])) for i in range(2)
+    ]
+    totals = [total(keep0, got0, first0, second0), total(keep1, got1, first1, second1)]
+    zl, zh, x = (lax.axis_index(name) for name in ("zl", "zh", "x"))
+    swap = (x // 2 ^ zl % 2 ^ zl // 2 ^ zh) == 0
+    kinds = (jnp.where(swap, totals[1], totals[0]), jnp.where(swap, totals[0], totals[1]))
+    ends = [permute(v, inverse(to_plane(kind))) for kind, v in enumerate(kinds)]
+    sent = [after(v, *kinds) for v in sent]
+    before = ([], others[:1])
+    mids = []
+    back = [
+        finish(backs[3 * i : 3 * i + 3], "zl", orders[i], sent[i], mids, *before[i]) for i in range(2)
+    ]
+    grad = [finish(grads[3 * i : 3 * i + 3], "y", orders[i], others[i], mids) for i in range(2)]
+    ends = lax.optimization_barrier((*ends, *mids[1:]))[:2]
+    mixed = (ends[0].astype(f32) + ends[1].astype(f32)).astype(bf16)
     hidden_grad = jnp.concatenate(back).astype(bf16).T
     return (mixed, hidden_grad, jnp.concatenate(grad))
 

time: 194 us -> 181 us (0.933)
  the two profiles are of different devices: /device:TPU:1 before, /device:TPU:79 now
where the time goes in v3:
time: 181 us; the launch traced here: 180 us
  waiting for transfers between devices  72.3 us (40%)
  starting transfers between devices  57.7 us (32%)
  Pallas kernels  30.2 us (17%)
  other arithmetic  14.8 us (8%)
  local copies, waits for them, and re-layouts  4.51 us (2%)
    ppermute x33, waiting for transfers between devices, permute(): return lax.ppermute(array, AXES, pairs)  72.3 us
    ppermute x33, starting transfers between devices, permute(): return lax.ppermute(array, AXES, pairs)  57.7 us
    pallas_call x4, Pallas kernels, call(): pl.pallas_call(kernel, out_shape=outputs, in_specs=[pl.BlockSpec(memory_s...  30.2 us
  transfers between devices with their start and end apart: 33, of which 13 were waited for; matrix products, arithmetic and copies ran while one was open for 9% of the time, Pallas kernels for 14%

profile of v3, /device:TPU:79, one launch (start us, length us, event | category | flops | bytes accessed | tf_op | source)
XLA Modules:
  0.0 180.5 jit_solution(14386386364494242568)
XLA Ops:
  0.6 4.7 %collective-permute-start = (bf16[384,512]{1,0:T(8,128)(2,1)}, bf16[384,512]{1,0:T(8,128)(2,1)S(1)}, u32[]{:S(2)}, u32[]{:S(2)}) collective-permute-start(bf16[384,512]{1,0:T(8,128)(2,1)} %param.7), channel_id=1, source_target_pairs={{0,10},{1,31},{2,42},{3,63},{4,8},{5,29},{6,40},{7,61},{8,6},{9,19... | collective-permute-start | bytes 1179656 | tf_op jit(solution)/shard_map/ppermute | solution.py:27
  5.3 0.9 copy.7
  6.2 0.9 broadcast_in_dim.3
  7.1 0.1 copy.8
  7.2 1.0 copy-done.19
  8.2 0.3 multiply_convert_fusion
  8.6 0.3 collective-permute-start.10
  8.8 1.3 collective-permute-start.11
  10.1 4.6 %collective-permute-start.1 = (bf16[384,512]{1,0:T(8,128)(2,1)S(1)}, bf16[384,512]{1,0:T(8,128)(2,1)S(1)}, u32[]{:S(2)}, u32[]{:S(2)}) collective-permute-start(bf16[384,512]{1,0:T(8,128)(2,1)S(1)} %copy-done.23), channel_id=1, source_target_pairs={{0,0},{1,21},{2,32},{3,53},{4,2},{5,23},{6,34},{7,55},{8,12},{9,25... | collective-permute-start | bytes 1179656 | tf_op jit(solution)/shard_map/ppermute | solution.py:27
  14.7 11.7 %collective-permute-done.refs_2_.refs_5_ = bf16[384,512]{1,0:T(8,128)(2,1)S(1)} collective-permute-done((bf16[384,512]{1,0:T(8,128)(2,1)}, bf16[384,512]{1,0:T(8,128)(2,1)S(1)}, u32[]{:S(2)}, u32[]{:S(2)}) %collective-permute-start) | collective-permute-done | bytes 393248 | tf_op jit(solution)/shard_map/ppermute | solution.py:27
  26.5 1.4 collective-permute-start.12
  27.9 7.8 %collective-permute-start.4 = (bf16[384,512]{1,0:T(8,128)(2,1)S(1)}, bf16[384,512]{1,0:T(8,128)(2,1)S(1)}, u32[]{:S(2)}, u32[]{:S(2)}) collective-permute-start(bf16[384,512]{1,0:T(8,128)(2,1)S(1)} %collective-permute-done.1.refs_7_.refs_10_), channel_id=1, source_target_pairs={{0,6},{1,7},{2,4},{3,5},{4,2},{5,3},{6,0},{7,1},{8,14},{9,15},{10,... | collective-permute-start | bytes 1179656 | tf_op jit(solution)/shard_map/ppermute | solution.py:27
  35.9 1.7 collective-permute-start.8
  37.6 1.8 %collective-permute-done.2.refs_3_.refs_6_ = bf16[384,512]{1,0:T(8,128)(2,1)S(1)} collective-permute-done((bf16[384,512]{1,0:T(8,128)(2,1)S(1)}, bf16[384,512]{1,0:T(8,128)(2,1)S(1)}, u32[]{:S(2)}, u32[]{:S(2)}) %collective-permute-start.2) | collective-permute-done | bytes 393248 | tf_op jit(solution)/shard_map/ppermute | solution.py:27
  39.5 4.9 %collective-permute-start.3 = (bf16[2,384,512]{2,1,0:T(8,128)(2,1)S(1)}, bf16[2,384,512]{2,1,0:T(8,128)(2,1)}, u32[]{:S(2)}, u32[]{:S(2)}) collective-permute-start(bf16[2,384,512]{2,1,0:T(8,128)(2,1)S(1)} %pad_maximum_fusion.2), channel_id=1, source_target_pairs={{0,6},{1,7},{2,4},{3,5},{4,2},{5,3},{6,0},{7,1},{8,14},{9,15},{10,... | collective-permute-start | bytes 2359304 | tf_op jit(solution)/shard_map/ppermute | solution.py:27
  44.4 1.0 pad_maximum_fusion.3
  45.5 0.7 collective-permute-start.7
  46.2 4.7 %collective-permute-start.9 = (bf16[2,352,384]{2,1,0:T(8,128)(2,1)S(1)}, bf16[2,352,384]{2,1,0:T(8,128)(2,1)S(1)}, u32[]{:S(2)}, u32[]{:S(2)}) collective-permute-start(bf16[2,352,384]{2,1,0:T(8,128)(2,1)S(1)} %pad_maximum_fusion.5), channel_id=1, source_target_pairs={{0,16},{1,17},{2,18},{3,19},{4,20},{5,21},{6,22},{7,23},{8,24},{9,... | collective-permute-start | bytes 1622024 | tf_op jit(solution)/shard_map/ppermute | solution.py:27
  50.9 9.9 %collective-permute-done.3.refs_4_.refs_7_ = bf16[2,384,512]{2,1,0:T(8,128)(2,1)} collective-permute-done((bf16[2,384,512]{2,1,0:T(8,128)(2,1)S(1)}, bf16[2,384,512]{2,1,0:T(8,128)(2,1)}, u32[]{:S(2)}, u32[]{:S(2)}) %collective-permute-start.3) | collective-permute-done | bytes 786464 | tf_op jit(solution)/shard_map/ppermute | solution.py:27
  60.8 1.1 collective-permute-done.5.refs_9_.refs_12_
  61.9 11.6 %collective-permute-done.7.refs_2_ = bf16[2,352,384]{2,1,0:T(8,128)(2,1)S(1)} collective-permute-done((bf16[2,352,384]{2,1,0:T(8,128)(2,1)S(1)}, bf16[2,352,384]{2,1,0:T(8,128)(2,1)S(1)}, u32[]{:S(2)}, u32[]{:S(2)}) %collective-permute-start.7) | collective-permute-done | bytes 540704 | tf_op jit(solution)/shard_map/ppermute | solution.py:27
  73.5 1.1 copy-done.20
  74.6 5.4 %mixed_terms.2 = (bf16[4,384,512]{2,1,0:T(8,128)(2,1)}, bf16[4,384,512]{2,1,0:T(8,128)(2,1)}) custom-call(bf16[704,384]{1,0:T(8,128)(2,1)S(1)} %bitcast.67, bf16[352,384]{1,0:T(8,128)(2,1)S(1)} %collective-permute-done.6.refs_1_, bf16[2,352,384]{2,1,0:T(8,128)(2,1)S(1)} %collective-permute-done.7.refs_2_, ...), custom_call_target="tpu_custom_call" | custom-call | flops 2214592512 | bytes 8192000 | tf_op jit(solution)/shard_map/mixed_terms/pallas_call | solution.py:210
  80.0 0.8 collective-permute-start.13
  80.9 5.5 %mixed_terms.3 = (bf16[4,384,512]{2,1,0:T(8,128)(2,1)}, bf16[4,384,512]{2,1,0:T(8,128)(2,1)}) custom-call(bf16[704,384]{1,0:T(8,128)(2,1)S(1)} %bitcast.68, bf16[352,384]{1,0:T(8,128)(2,1)S(1)} %collective-permute-done.6.refs_1_, bf16[2,352,384]{2,1,0:T(8,128)(2,1)S(1)} %collective-permute-done.7.refs_2_, ...), custom_call_target="tpu_custom_call" | custom-call | flops 2214592512 | bytes 8192000 | tf_op jit(solution)/shard_map/mixed_terms/pallas_call | solution.py:210
  86.4 0.1 collective-permute-start.14
  86.5 0.5 collective-permute-start.19
  87.0 0.1 collective-permute-start.21
  87.1 0.4 collective-permute-start.20
  87.5 0.1 collective-permute-start.22
  87.6 1.1 add_convert_fusion
  88.7 2.6 %collective-permute-done.14 = bf16[4,384,512]{2,1,0:T(8,128)(2,1)S(1)} collective-permute-done((bf16[4,384,512]{2,1,0:T(8,128)(2,1)}, bf16[4,384,512]{2,1,0:T(8,128)(2,1)S(1)}, u32[]{:S(2)}, u32[]{:S(2)}) %collective-permute-start.14) | collective-permute-done | bytes 1572896 | tf_op jit(solution)/shard_map/ppermute | solution.py:27
  91.4 1.0 collective-permute-start.16
  92.4 1.1 add_convert_fusion.1
  93.5 2.6 %collective-permute-start.15 = (bf16[2,384,512]{2,1,0:T(8,128)(2,1)}, bf16[2,384,512]{2,1,0:T(8,128)(2,1)}, u32[]{:S(2)}, u32[]{:S(2)}) collective-permute-start(bf16[2,384,512]{2,1,0:T(8,128)(2,1)} %add_convert_fusion.1), channel_id=1, source_target_pairs={{0,6},{1,7},{2,4},{3,5},{4,2},{5,3},{6,0},{7,1},{8,14},{9,15},{10,... | collective-permute-start | bytes 2359304 | tf_op jit(solution)/shard_map/ppermute | solution.py:27
  96.1 10.5 %hidden_terms.1 = (f32[352,384]{1,0:T(8,128)S(1)}, bf16[352,384]{1,0:T(8,128)(2,1)S(1)}, bf16[2,352,384]{2,1,0:T(8,128)(2,1)S(1)}, f32[352,384]{1,0:T(8,128)S(1)...) custom-call(bf16[2,704,512]{2,1,0:T(8,128)(2,1)} %bitcast.65, bf16[2,704,512]{2,1,0:T(8,128)(2,1)} %copy-done.20, ...), custom_call_target="tpu_custom_call" | custom-call | flops 4429185024 | bytes 11878400 | tf_op jit(solution)/shard_map/hidden_terms/pallas_call | solution.py:210
  106.7 0.2 collective-permute-start.28
  106.9 1.6 collective-permute-start.25
  108.5 2.2 %collective-permute-done.16 = bf16[2,384,512]{2,1,0:T(8,128)(2,1)S(1)} collective-permute-done((bf16[2,384,512]{2,1,0:T(8,128)(2,1)}, bf16[2,384,512]{2,1,0:T(8,128)(2,1)S(1)}, u32[]{:S(2)}, u32[]{:S(2)}) %collective-permute-start.16) | collective-permute-done | bytes 786464 | tf_op jit(solution)/shard_map/ppermute | solution.py:27
  110.7 0.1 fusion.12
  110.8 2.1 %collective-permute-start.17 = (bf16[384,512]{1,0:T(8,128)(2,1)S(1)}, bf16[384,512]{1,0:T(8,128)(2,1)S(1)}, u32[]{:S(2)}, u32[]{:S(2)}) collective-permute-start(bf16[384,512]{1,0:T(8,128)(2,1)S(1)} %fusion.12), channel_id=1, source_target_pairs={{0,6},{1,7},{2,4},{3,5},{4,2},{5,3},{6,0},{7,1},{8,14},{9,15},{10,... | collective-permute-start | bytes 1179656 | tf_op jit(solution)/shard_map/ppermute | solution.py:27
  113.0 0.8 collective-permute-done.15
  113.8 1.9 %fusion.13 = bf16[384,512]{1,0:T(8,128)(2,1)} fusion(bf16[2,384,512]{2,1,0:T(8,128)(2,1)} %collective-permute-done.15, bf16[4,384,512]{2,1,0:T(8,128)(2,1)S(1)} %copy-done.16, bf16[4,384,512]{2,1,0:T(8,128)(2,1)S(1)} %copy-done.14), kind=kLoop, calls=%fused_computation.36 | loop fusion | flops 1179648 | bytes 1572864 | tf_op jit(solution)/shard_map/convert_element_type | solution.py:286
  115.7 8.7 %weight_terms.1 = (f32[352,512]{1,0:T(8,128)}, bf16[352,512]{1,0:T(8,128)(2,1)S(1)}, bf16[2,352,512]{2,1,0:T(8,128)(2,1)}, f32[352,512]{1,0:T(8,128)}, bf16[352,...) custom-call(bf16[704,384]{1,0:T(8,128)(2,1)S(1)} %bitcast.69, bf16[352,384]{1,0:T(8,128)(2,1)S(1)} %copy-done.3, ...), custom_call_target="tpu_custom_call" | custom-call | flops 4429185024 | bytes 12058624 | tf_op jit(solution)/shard_map/weight_terms/pallas_call | solution.py:210
  124.5 0.9 collective-permute-done.18
  125.4 3.2 %collective-permute-start.26 = (bf16[2,352,512]{2,1,0:T(8,128)(2,1)}, bf16[2,352,512]{2,1,0:T(8,128)(2,1)S(1)}, u32[]{:S(2)}, u32[]{:S(2)}) collective-permute-start(bf16[2,352,512]{2,1,0:T(8,128)(2,1)} %get-tuple-element.51), channel_id=1, source_target_pairs={{0,192},{1,193},{2,194},{3,195},{4,196},{5,197},{6,198},{7,199},{8... | collective-permute-start | bytes 2162696 | tf_op jit(solution)/shard_map/ppermute | solution.py:27
  128.5 1.4 broadcast_select_fusion
  130.0 2.1 %collective-permute-done.28 = bf16[2,352,384]{2,1,0:T(8,128)(2,1)} collective-permute-done((bf16[2,352,384]{2,1,0:T(8,128)(2,1)S(1)}, bf16[2,352,384]{2,1,0:T(8,128)(2,1)}, u32[]{:S(2)}, u32[]{:S(2)}) %collective-permute-start.28) | collective-permute-done | bytes 540704 | tf_op jit(solution)/shard_map/ppermute | solution.py:27
  132.1 1.0 fusion.8
  133.3 8.2 %collective-permute-start.23 = (bf16[384,512]{1,0:T(8,128)(2,1)S(1)}, bf16[384,512]{1,0:T(8,128)(2,1)S(1)}, u32[]{:S(2)}, u32[]{:S(2)}) collective-permute-start(bf16[384,512]{1,0:T(8,128)(2,1)S(1)} %broadcast_select_fusion.1), channel_id=1, source_target_pairs={{0,44},{1,60},{2,40},{3,56},{4,12},{5,28},{6,8},{7,24},{8,4},{9,20... | collective-permute-start | bytes 1179656 | tf_op jit(solution)/shard_map/ppermute | solution.py:27
  141.5 2.8 %collective-permute-start.24 = (bf16[384,512]{1,0:T(8,128)(2,1)S(1)}, bf16[384,512]{1,0:T(8,128)(2,1)S(1)}, u32[]{:S(2)}, u32[]{:S(2)}) collective-permute-start(bf16[384,512]{1,0:T(8,128)(2,1)S(1)} %get-tuple-element.65), channel_id=1, source_target_pairs={{0,0},{1,16},{2,4},{3,20},{4,32},{5,48},{6,36},{7,52},{8,40},{9,56... | collective-permute-start | bytes 1179656 | tf_op jit(solution)/shard_map/ppermute | solution.py:27
  144.4 1.0 fusion.11
  145.5 1.0 fusion.10
  146.6 1.5 collective-permute-start.31
  148.2 14.4 %collective-permute-done.27 = bf16[2,352,512]{2,1,0:T(8,128)(2,1)S(1)} collective-permute-done((bf16[2,352,512]{2,1,0:T(8,128)(2,1)S(1)}, bf16[2,352,512]{2,1,0:T(8,128)(2,1)S(1)}, u32[]{:S(2)}, u32[]{:S(2)}) %collective-permute-start.27) | collective-permute-done | bytes 720928 | tf_op jit(solution)/shard_map/ppermute | solution.py:27
  162.8 1.1 collective-permute-done.24
  163.8 0.8 add_convert_fusion.2
  164.7 12.1 %collective-permute-done.30 = bf16[352,384]{1,0:T(8,128)(2,1)S(1)} collective-permute-done((bf16[352,384]{1,0:T(8,128)(2,1)S(1)}, bf16[352,384]{1,0:T(8,128)(2,1)S(1)}, u32[]{:S(2)}, u32[]{:S(2)}) %collective-permute-start.30) | collective-permute-done | bytes 270368 | tf_op jit(solution)/shard_map/ppermute | solution.py:27
  176.7 1.0 fusion.7
  177.8 0.9 maximum_bitcast_fusion
  178.7 0.1 fusion.3
  178.8 0.3 copy-done.17
  179.1 0.1 fusion.2
  179.2 1.2 pad_maximum_fusion.1
  (82 shorter events, 1.2 us)
Async XLA Ops:
  0.6 25.7 %collective-permute-start = (bf16[384,512]{1,0:T(8,128)(2,1)}, bf16[384,512]{1,0:T(8,128)(2,1)S(1)}, u32[]{:S(2)}, u32[]{:S(2)}) collective-permute-start(bf16[384,512]{1,0:T(8,128)(2,1)} %param.7), channel_id=1, source_target_pairs={{0,10},{1,31},{2,42},{3,63},{4,8},{5,29},{6,40},{7,61},{8,6},{9,19... | collective-permute-start | bytes 1179656 | tf_op jit(solution)/shard_map/ppermute | solution.py:27
  7.1 1.1 copy-start.19
  8.2 1.9 %copy-start.23 = (bf16[384,512]{1,0:T(8,128)(2,1)S(1)}, bf16[384,512]{1,0:T(8,128)(2,1)}, u32[]{:S(2)}) copy-start(bf16[384,512]{1,0:T(8,128)(2,1)} %param.7) | copy-start | bytes 1179652
  8.5 27.2 %copy-start.1 = (bf16[384,704]{0,1:T(8,128)(2,1)S(1)}, bf16[384,704]{0,1:T(8,128)(2,1)}, u32[]{:S(2)}) copy-start(bf16[384,704]{0,1:T(8,128)(2,1)} %param.4) | copy-start | bytes 1622020
  8.6 17.8 %collective-permute-start.10 = (bf16[352,512]{1,0:T(8,128)(2,1)S(1)}, bf16[352,512]{1,0:T(8,128)(2,1)S(1)}, u32[]{:S(2)}, u32[]{:S(2)}) collective-permute-start(bf16[352,512]{1,0:T(8,128)(2,1)S(1)} %get-tuple-element.68), channel_id=1, source_target_pairs={{0,64},{1,65},{2,66},{3,67},{4,68},{5,69},{6,70},{7,71},{8,72},{9,... | collective-permute-start | bytes 1081352 | tf_op jit(solution)/shard_map/ppermute | solution.py:27
  8.8 17.6 %collective-permute-start.11 = (bf16[352,512]{1,0:T(8,128)(2,1)S(1)}, bf16[352,512]{1,0:T(8,128)(2,1)S(1)}, u32[]{:S(2)}, u32[]{:S(2)}) collective-permute-start(bf16[352,512]{1,0:T(8,128)(2,1)S(1)} %get-tuple-element.69), channel_id=1, source_target_pairs={{0,64},{1,65},{2,66},{3,67},{4,68},{5,69},{6,70},{7,71},{8,72},{9,... | collective-permute-start | bytes 1081352 | tf_op jit(solution)/shard_map/ppermute | solution.py:27
  10.1 17.8 %collective-permute-start.1 = (bf16[384,512]{1,0:T(8,128)(2,1)S(1)}, bf16[384,512]{1,0:T(8,128)(2,1)S(1)}, u32[]{:S(2)}, u32[]{:S(2)}) collective-permute-start(bf16[384,512]{1,0:T(8,128)(2,1)S(1)} %copy-done.23), channel_id=1, source_target_pairs={{0,0},{1,21},{2,32},{3,53},{4,2},{5,23},{6,34},{7,55},{8,12},{9,25... | collective-permute-start | bytes 1179656 | tf_op jit(solution)/shard_map/ppermute | solution.py:27
  26.4 13.0 %collective-permute-start.2 = (bf16[384,512]{1,0:T(8,128)(2,1)S(1)}, bf16[384,512]{1,0:T(8,128)(2,1)S(1)}, u32[]{:S(2)}, u32[]{:S(2)}) collective-permute-start(bf16[384,512]{1,0:T(8,128)(2,1)S(1)} %collective-permute-done.refs_2_.refs_5_), channel_id=1, source_target_pairs={{0,2},{1,3},{2,0},{3,1},{4,6},{5,7},{6,4},{7,5},{8,10},{9,11},{10,... | collective-permute-start | bytes 1179656 | tf_op jit(solution)/shard_map/ppermute | solution.py:27
  26.5 54.4 %copy-start = (bf16[1408,512]{1,0:T(8,128)(2,1)}, bf16[1408,512]{1,0:T(8,128)(2,1)S(1)}, u32[]{:S(2)}) copy-start(bf16[1408,512]{1,0:T(8,128)(2,1)S(1)} %pad_maximum_fusion) | copy-start | bytes 4325380
  26.5 46.9 %collective-permute-start.12 = (bf16[2,704,512]{2,1,0:T(8,128)(2,1)S(1)}, bf16[2,704,512]{2,1,0:T(8,128)(2,1)S(1)}, u32[]{:S(2)}, u32[]{:S(2)}) collective-permute-start(bf16[2,704,512]{2,1,0:T(8,128)(2,1)S(1)} %bitcast.62), channel_id=1, source_target_pairs={{0,192},{1,193},{2,194},{3,195},{4,196},{5,197},{6,198},{7,199},{8... | collective-permute-start | bytes 4325384 | tf_op jit(solution)/shard_map/ppermute | solution.py:27
  27.9 16.5 %collective-permute-start.4 = (bf16[384,512]{1,0:T(8,128)(2,1)S(1)}, bf16[384,512]{1,0:T(8,128)(2,1)S(1)}, u32[]{:S(2)}, u32[]{:S(2)}) collective-permute-start(bf16[384,512]{1,0:T(8,128)(2,1)S(1)} %collective-permute-done.1.refs_7_.refs_10_), channel_id=1, source_target_pairs={{0,6},{1,7},{2,4},{3,5},{4,2},{5,3},{6,0},{7,1},{8,14},{9,15},{10,... | collective-permute-start | bytes 1179656 | tf_op jit(solution)/shard_map/ppermute | solution.py:27
  35.8 9.6 %collective-permute-start.6 = (bf16[352,384]{1,0:T(8,128)(2,1)S(1)}, bf16[352,384]{1,0:T(8,128)(2,1)S(1)}, u32[]{:S(2)}, u32[]{:S(2)}) collective-permute-start(bf16[352,384]{1,0:T(8,128)(2,1)S(1)} %get-tuple-element.73), channel_id=1, source_target_pairs={{0,16},{1,17},{2,18},{3,19},{4,20},{5,21},{6,22},{7,23},{8,24},{9,... | collective-permute-start | bytes 811016 | tf_op jit(solution)/shard_map/ppermute | solution.py:27
  35.9 10.3 %collective-permute-start.8 = (bf16[352,384]{1,0:T(8,128)(2,1)S(1)}, bf16[352,384]{1,0:T(8,128)(2,1)S(1)}, u32[]{:S(2)}, u32[]{:S(2)}) collective-permute-start(bf16[352,384]{1,0:T(8,128)(2,1)S(1)} %get-tuple-element.72), channel_id=1, source_target_pairs={{0,48},{1,49},{2,50},{3,51},{4,52},{5,53},{6,54},{7,55},{8,56},{9,... | collective-permute-start | bytes 811016 | tf_op jit(solution)/shard_map/ppermute | solution.py:27
  39.5 21.3 %collective-permute-start.3 = (bf16[2,384,512]{2,1,0:T(8,128)(2,1)S(1)}, bf16[2,384,512]{2,1,0:T(8,128)(2,1)}, u32[]{:S(2)}, u32[]{:S(2)}) collective-permute-start(bf16[2,384,512]{2,1,0:T(8,128)(2,1)S(1)} %pad_maximum_fusion.2), channel_id=1, source_target_pairs={{0,6},{1,7},{2,4},{3,5},{4,2},{5,3},{6,0},{7,1},{8,14},{9,15},{10,... | collective-permute-start | bytes 2359304 | tf_op jit(solution)/shard_map/ppermute | solution.py:27
  45.4 16.5 %collective-permute-start.5 = (bf16[2,384,512]{2,1,0:T(8,128)(2,1)}, bf16[2,384,512]{2,1,0:T(8,128)(2,1)}, u32[]{:S(2)}, u32[]{:S(2)}) collective-permute-start(bf16[2,384,512]{2,1,0:T(8,128)(2,1)} %pad_maximum_fusion.3), channel_id=1, source_target_pairs={{0,2},{1,3},{2,0},{3,1},{4,6},{5,7},{6,4},{7,5},{8,10},{9,11},{10,... | collective-permute-start | bytes 2359304 | tf_op jit(solution)/shard_map/ppermute | solution.py:27
  45.4 35.5 %copy-start.2 = (bf16[352,384]{1,0:T(8,128)(2,1)}, bf16[352,384]{1,0:T(8,128)(2,1)S(1)}, u32[]{:S(2)}) copy-start(bf16[352,384]{1,0:T(8,128)(2,1)S(1)} %collective-permute-done.6.refs_1_) | copy-start | bytes 811012
  45.5 28.0 %collective-permute-start.7 = (bf16[2,352,384]{2,1,0:T(8,128)(2,1)S(1)}, bf16[2,352,384]{2,1,0:T(8,128)(2,1)S(1)}, u32[]{:S(2)}, u32[]{:S(2)}) collective-permute-start(bf16[2,352,384]{2,1,0:T(8,128)(2,1)S(1)} %pad_maximum_fusion.4), channel_id=1, source_target_pairs={{0,48},{1,49},{2,50},{3,51},{4,52},{5,53},{6,54},{7,55},{8,56},{9,... | collective-permute-start | bytes 1622024 | tf_op jit(solution)/shard_map/ppermute | solution.py:27
  46.2 34.7 %copy-start.4 = (bf16[352,384]{1,0:T(8,128)(2,1)}, bf16[352,384]{1,0:T(8,128)(2,1)S(1)}, u32[]{:S(2)}) copy-start(bf16[352,384]{1,0:T(8,128)(2,1)S(1)} %collective-permute-done.8.refs_3_) | copy-start | bytes 811012
  46.2 27.2 %collective-permute-start.9 = (bf16[2,352,384]{2,1,0:T(8,128)(2,1)S(1)}, bf16[2,352,384]{2,1,0:T(8,128)(2,1)S(1)}, u32[]{:S(2)}, u32[]{:S(2)}) collective-permute-start(bf16[2,352,384]{2,1,0:T(8,128)(2,1)S(1)} %pad_maximum_fusion.5), channel_id=1, source_target_pairs={{0,16},{1,17},{2,18},{3,19},{4,20},{5,21},{6,22},{7,23},{8,24},{9,... | collective-permute-start | bytes 1622024 | tf_op jit(solution)/shard_map/ppermute | solution.py:27
  73.4 7.5 %copy-start.6 = (bf16[2,352,384]{2,1,0:T(8,128)(2,1)}, bf16[2,352,384]{2,1,0:T(8,128)(2,1)S(1)}, u32[]{:S(2)}) copy-start(bf16[2,352,384]{2,1,0:T(8,128)(2,1)S(1)} %collective-permute-done.7.refs_2_) | copy-start | bytes 1622020
  73.4 7.5 %copy-start.8 = (bf16[2,352,384]{2,1,0:T(8,128)(2,1)}, bf16[2,352,384]{2,1,0:T(8,128)(2,1)S(1)}, u32[]{:S(2)}) copy-start(bf16[2,352,384]{2,1,0:T(8,128)(2,1)S(1)} %collective-permute-done.9.refs_4_) | copy-start | bytes 1622020
  73.5 1.1 copy-start.20
  80.0 7.6 %copy-start.9 = (bf16[4,384,512]{2,1,0:T(8,128)(2,1)S(1)}, bf16[4,384,512]{2,1,0:T(8,128)(2,1)}, u32[]{:S(2)}) copy-start(bf16[4,384,512]{2,1,0:T(8,128)(2,1)} %get-tuple-element.41) | copy-start | bytes 4718596
  80.0 6.4 %collective-permute-start.13 = (bf16[4,384,512]{2,1,0:T(8,128)(2,1)}, bf16[4,384,512]{2,1,0:T(8,128)(2,1)S(1)}, u32[]{:S(2)}, u32[]{:S(2)}) collective-permute-start(bf16[4,384,512]{2,1,0:T(8,128)(2,1)} %get-tuple-element.36), channel_id=1, source_target_pairs={{0,1},{1,0},{2,3},{3,2},{4,5},{5,4},{6,7},{7,6},{8,9},{9,8},{10,11... | collective-permute-start | bytes 4718600 | tf_op jit(solution)/shard_map/ppermute | solution.py:27
  86.4 6.0 %copy-start.13 = (bf16[4,384,512]{2,1,0:T(8,128)(2,1)S(1)}, bf16[4,384,512]{2,1,0:T(8,128)(2,1)}, u32[]{:S(2)}) copy-start(bf16[4,384,512]{2,1,0:T(8,128)(2,1)} %get-tuple-element.38) | copy-start | bytes 4718596
  86.4 7.1 %copy-start.11 = (bf16[4,384,512]{2,1,0:T(8,128)(2,1)}, bf16[4,384,512]{2,1,0:T(8,128)(2,1)S(1)}, u32[]{:S(2)}) copy-start(bf16[4,384,512]{2,1,0:T(8,128)(2,1)S(1)} %collective-permute-done.13) | copy-start | bytes 4718596
  86.4 5.0 %collective-permute-start.14 = (bf16[4,384,512]{2,1,0:T(8,128)(2,1)}, bf16[4,384,512]{2,1,0:T(8,128)(2,1)S(1)}, u32[]{:S(2)}, u32[]{:S(2)}) collective-permute-start(bf16[4,384,512]{2,1,0:T(8,128)(2,1)} %get-tuple-element.40), channel_id=1, source_target_pairs={{0,1},{1,0},{2,3},{3,2},{4,5},{5,4},{6,7},{7,6},{8,9},{9,8},{10,11... | collective-permute-start | bytes 4718600 | tf_op jit(solution)/shard_map/ppermute | solution.py:27
  86.5 7.0 %collective-permute-start.19 = (bf16[2,384,512]{2,1,0:T(8,128)(2,1)S(1)}, bf16[2,384,512]{2,1,0:T(8,128)(2,1)S(1)}, u32[]{:S(2)}, u32[]{:S(2)}) collective-permute-start(bf16[2,384,512]{2,1,0:T(8,128)(2,1)S(1)} %pad_maximum_fusion.2), channel_id=1, source_target_pairs={{0,1},{1,0},{2,3},{3,2},{4,5},{5,4},{6,7},{7,6},{8,9},{9,8},{10,11... | collective-permute-start | bytes 2359304 | tf_op jit(solution)/shard_map/ppermute | solution.py:27
  87.0 9.1 %collective-permute-start.21 = (bf16[2,384,512]{2,1,0:T(8,128)(2,1)}, bf16[2,384,512]{2,1,0:T(8,128)(2,1)}, u32[]{:S(2)}, u32[]{:S(2)}) collective-permute-start(bf16[2,384,512]{2,1,0:T(8,128)(2,1)} %pad_maximum_fusion.3), channel_id=1, source_target_pairs={{0,1},{1,0},{2,3},{3,2},{4,5},{5,4},{6,7},{7,6},{8,9},{9,8},{10,11... | collective-permute-start | bytes 2359304 | tf_op jit(solution)/shard_map/ppermute | solution.py:27
  87.1 9.0 %collective-permute-start.20 = (bf16[2,384,512]{2,1,0:T(8,128)(2,1)}, bf16[2,384,512]{2,1,0:T(8,128)(2,1)}, u32[]{:S(2)}, u32[]{:S(2)}) collective-permute-start(bf16[2,384,512]{2,1,0:T(8,128)(2,1)} %collective-permute-done.3.refs_4_.refs_7_), channel_id=1, source_target_pairs={{0,1},{1,0},{2,3},{3,2},{4,5},{5,4},{6,7},{7,6},{8,9},{9,8},{10,11... | collective-permute-start | bytes 2359304 | tf_op jit(solution)/shard_map/ppermute | solution.py:27
  87.5 8.6 %collective-permute-start.22 = (bf16[2,384,512]{2,1,0:T(8,128)(2,1)}, bf16[2,384,512]{2,1,0:T(8,128)(2,1)}, u32[]{:S(2)}, u32[]{:S(2)}) collective-permute-start(bf16[2,384,512]{2,1,0:T(8,128)(2,1)} %collective-permute-done.5.refs_9_.refs_12_), channel_id=1, source_target_pairs={{0,1},{1,0},{2,3},{3,2},{4,5},{5,4},{6,7},{7,6},{8,9},{9,8},{10,11... | collective-permute-start | bytes 2359304 | tf_op jit(solution)/shard_map/ppermute | solution.py:27
  91.4 2.1 %copy-start.15 = (bf16[4,384,512]{2,1,0:T(8,128)(2,1)}, bf16[4,384,512]{2,1,0:T(8,128)(2,1)S(1)}, u32[]{:S(2)}) copy-start(bf16[4,384,512]{2,1,0:T(8,128)(2,1)S(1)} %collective-permute-done.14) | copy-start | bytes 4718596
  91.4 19.3 %collective-permute-start.16 = (bf16[2,384,512]{2,1,0:T(8,128)(2,1)}, bf16[2,384,512]{2,1,0:T(8,128)(2,1)S(1)}, u32[]{:S(2)}, u32[]{:S(2)}) collective-permute-start(bf16[2,384,512]{2,1,0:T(8,128)(2,1)} %add_convert_fusion), channel_id=1, source_target_pairs={{0,2},{1,3},{2,0},{3,1},{4,6},{5,7},{6,4},{7,5},{8,10},{9,11},{10,... | collective-permute-start | bytes 2359304 | tf_op jit(solution)/shard_map/ppermute | solution.py:27
  93.5 2.6 %copy-start.21 = (bf16[2,384,512]{2,1,0:T(8,128)(2,1)}, bf16[2,384,512]{2,1,0:T(8,128)(2,1)S(1)}, u32[]{:S(2)}) copy-start(bf16[2,384,512]{2,1,0:T(8,128)(2,1)S(1)} %collective-permute-done.19.refs_5_.refs_8_) | copy-start | bytes 2359300
  93.5 20.3 %collective-permute-start.15 = (bf16[2,384,512]{2,1,0:T(8,128)(2,1)}, bf16[2,384,512]{2,1,0:T(8,128)(2,1)}, u32[]{:S(2)}, u32[]{:S(2)}) collective-permute-start(bf16[2,384,512]{2,1,0:T(8,128)(2,1)} %add_convert_fusion.1), channel_id=1, source_target_pairs={{0,6},{1,7},{2,4},{3,5},{4,2},{5,3},{6,0},{7,1},{8,14},{9,15},{10,... | collective-permute-start | bytes 2359304 | tf_op jit(solution)/shard_map/ppermute | solution.py:27
  96.1 14.6 %copy-start.10 = (bf16[4,384,512]{2,1,0:T(8,128)(2,1)S(1)}, bf16[4,384,512]{2,1,0:T(8,128)(2,1)}, u32[]{:S(2)}) copy-start(bf16[4,384,512]{2,1,0:T(8,128)(2,1)} %get-tuple-element.41) | copy-start | bytes 4718596
  96.1 14.6 %copy-start.12 = (bf16[4,384,512]{2,1,0:T(8,128)(2,1)S(1)}, bf16[4,384,512]{2,1,0:T(8,128)(2,1)}, u32[]{:S(2)}) copy-start(bf16[4,384,512]{2,1,0:T(8,128)(2,1)} %copy-done.11) | copy-start | bytes 4718596
  96.1 17.7 %copy-start.16 = (bf16[4,384,512]{2,1,0:T(8,128)(2,1)S(1)}, bf16[4,384,512]{2,1,0:T(8,128)(2,1)}, u32[]{:S(2)}) copy-start(bf16[4,384,512]{2,1,0:T(8,128)(2,1)} %copy-done.15) | copy-start | bytes 4718596
  106.7 7.1 %copy-start.14 = (bf16[4,384,512]{2,1,0:T(8,128)(2,1)S(1)}, bf16[4,384,512]{2,1,0:T(8,128)(2,1)}, u32[]{:S(2)}) copy-start(bf16[4,384,512]{2,1,0:T(8,128)(2,1)} %get-tuple-element.38) | copy-start | bytes 4718596
  106.7 25.4 %collective-permute-start.28 = (bf16[2,352,384]{2,1,0:T(8,128)(2,1)S(1)}, bf16[2,352,384]{2,1,0:T(8,128)(2,1)}, u32[]{:S(2)}, u32[]{:S(2)}) collective-permute-start(bf16[2,352,384]{2,1,0:T(8,128)(2,1)S(1)} %get-tuple-element.43), channel_id=1, source_target_pairs={{0,48},{1,49},{2,50},{3,51},{4,52},{5,53},{6,54},{7,55},{8,56},{9,... | collective-permute-start | bytes 1622024 | tf_op jit(solution)/shard_map/ppermute | solution.py:27
  106.9 8.8 %copy-start.3 = (bf16[352,384]{1,0:T(8,128)(2,1)S(1)}, bf16[352,384]{1,0:T(8,128)(2,1)}, u32[]{:S(2)}) copy-start(bf16[352,384]{1,0:T(8,128)(2,1)} %copy-done.2) | copy-start | bytes 811012
  106.9 8.8 %copy-start.5 = (bf16[352,384]{1,0:T(8,128)(2,1)S(1)}, bf16[352,384]{1,0:T(8,128)(2,1)}, u32[]{:S(2)}) copy-start(bf16[352,384]{1,0:T(8,128)(2,1)} %copy-done.4) | copy-start | bytes 811012
  106.9 8.8 %copy-start.7 = (bf16[2,352,384]{2,1,0:T(8,128)(2,1)S(1)}, bf16[2,352,384]{2,1,0:T(8,128)(2,1)}, u32[]{:S(2)}) copy-start(bf16[2,352,384]{2,1,0:T(8,128)(2,1)} %copy-done.6) | copy-start | bytes 1622020
  106.9 37.4 %collective-permute-start.25 = (bf16[2,352,384]{2,1,0:T(8,128)(2,1)}, bf16[2,352,384]{2,1,0:T(8,128)(2,1)}, u32[]{:S(2)}, u32[]{:S(2)}) collective-permute-start(bf16[2,352,384]{2,1,0:T(8,128)(2,1)} %get-tuple-element.49), channel_id=1, source_target_pairs={{0,16},{1,17},{2,18},{3,19},{4,20},{5,21},{6,22},{7,23},{8,24},{9,... | collective-permute-start | bytes 1622024 | tf_op jit(solution)/shard_map/ppermute | solution.py:27
  110.8 13.6 %collective-permute-start.17 = (bf16[384,512]{1,0:T(8,128)(2,1)S(1)}, bf16[384,512]{1,0:T(8,128)(2,1)S(1)}, u32[]{:S(2)}, u32[]{:S(2)}) collective-permute-start(bf16[384,512]{1,0:T(8,128)(2,1)S(1)} %fusion.12), channel_id=1, source_target_pairs={{0,6},{1,7},{2,4},{3,5},{4,2},{5,3},{6,0},{7,1},{8,14},{9,15},{10,... | collective-permute-start | bytes 1179656 | tf_op jit(solution)/shard_map/ppermute | solution.py:27
  115.7 9.7 %collective-permute-start.18 = (bf16[384,512]{1,0:T(8,128)(2,1)}, bf16[384,512]{1,0:T(8,128)(2,1)S(1)}, u32[]{:S(2)}, u32[]{:S(2)}) collective-permute-start(bf16[384,512]{1,0:T(8,128)(2,1)} %fusion.13), channel_id=1, source_target_pairs={{0,2},{1,3},{2,0},{3,1},{4,6},{5,7},{6,4},{7,5},{8,10},{9,11},{10,... | collective-permute-start | bytes 1179656 | tf_op jit(solution)/shard_map/ppermute | solution.py:27
  125.4 21.2 %collective-permute-start.26 = (bf16[2,352,512]{2,1,0:T(8,128)(2,1)}, bf16[2,352,512]{2,1,0:T(8,128)(2,1)S(1)}, u32[]{:S(2)}, u32[]{:S(2)}) collective-permute-start(bf16[2,352,512]{2,1,0:T(8,128)(2,1)} %get-tuple-element.51), channel_id=1, source_target_pairs={{0,192},{1,193},{2,194},{3,195},{4,196},{5,197},{6,198},{7,199},{8... | collective-permute-start | bytes 2162696 | tf_op jit(solution)/shard_map/ppermute | solution.py:27
  129.9 14.4 %copy-start.22 = (bf16[2,352,512]{2,1,0:T(8,128)(2,1)S(1)}, bf16[2,352,512]{2,1,0:T(8,128)(2,1)}, u32[]{:S(2)}) copy-start(bf16[2,352,512]{2,1,0:T(8,128)(2,1)} %get-tuple-element.56) | copy-start | bytes 2162692
  133.2 12.3 %collective-permute-start.29 = (bf16[352,384]{1,0:T(8,128)(2,1)S(1)}, bf16[352,384]{1,0:T(8,128)(2,1)S(1)}, u32[]{:S(2)}, u32[]{:S(2)}) collective-permute-start(bf16[352,384]{1,0:T(8,128)(2,1)S(1)} %fusion.8), channel_id=1, source_target_pairs={{0,16},{1,17},{2,18},{3,19},{4,20},{5,21},{6,22},{7,23},{8,24},{9,... | collective-permute-start | bytes 811016 | tf_op jit(solution)/shard_map/ppermute | solution.py:27
  133.3 29.5 %collective-permute-start.23 = (bf16[384,512]{1,0:T(8,128)(2,1)S(1)}, bf16[384,512]{1,0:T(8,128)(2,1)S(1)}, u32[]{:S(2)}, u32[]{:S(2)}) collective-permute-start(bf16[384,512]{1,0:T(8,128)(2,1)S(1)} %broadcast_select_fusion.1), channel_id=1, source_target_pairs={{0,44},{1,60},{2,40},{3,56},{4,12},{5,28},{6,8},{7,24},{8,4},{9,20... | collective-permute-start | bytes 1179656 | tf_op jit(solution)/shard_map/ppermute | solution.py:27
  141.5 22.4 %collective-permute-start.24 = (bf16[384,512]{1,0:T(8,128)(2,1)S(1)}, bf16[384,512]{1,0:T(8,128)(2,1)S(1)}, u32[]{:S(2)}, u32[]{:S(2)}) collective-permute-start(bf16[384,512]{1,0:T(8,128)(2,1)S(1)} %get-tuple-element.65), channel_id=1, source_target_pairs={{0,0},{1,16},{2,4},{3,20},{4,32},{5,48},{6,36},{7,52},{8,40},{9,56... | collective-permute-start | bytes 1179656 | tf_op jit(solution)/shard_map/ppermute | solution.py:27
  144.3 18.2 %collective-permute-start.27 = (bf16[2,352,512]{2,1,0:T(8,128)(2,1)S(1)}, bf16[2,352,512]{2,1,0:T(8,128)(2,1)S(1)}, u32[]{:S(2)}, u32[]{:S(2)}) collective-permute-start(bf16[2,352,512]{2,1,0:T(8,128)(2,1)S(1)} %copy-done.22), channel_id=1, source_target_pairs={{0,64},{1,65},{2,66},{3,67},{4,68},{5,69},{6,70},{7,71},{8,72},{9,... | collective-permute-start | bytes 2162696 | tf_op jit(solution)/shard_map/ppermute | solution.py:27
  146.6 32.0 %collective-permute-start.31 = (bf16[352,512]{1,0:T(8,128)(2,1)S(1)}, bf16[352,512]{1,0:T(8,128)(2,1)S(1)}, u32[]{:S(2)}, u32[]{:S(2)}) collective-permute-start(bf16[352,512]{1,0:T(8,128)(2,1)S(1)} %fusion.5), channel_id=1, source_target_pairs={{0,64},{1,65},{2,66},{3,67},{4,68},{5,69},{6,70},{7,71},{8,72},{9,... | collective-permute-start | bytes 1081352 | tf_op jit(solution)/shard_map/ppermute | solution.py:27
  148.2 28.6 %collective-permute-start.30 = (bf16[352,384]{1,0:T(8,128)(2,1)S(1)}, bf16[352,384]{1,0:T(8,128)(2,1)S(1)}, u32[]{:S(2)}, u32[]{:S(2)}) collective-permute-start(bf16[352,384]{1,0:T(8,128)(2,1)S(1)} %fusion.11), channel_id=1, source_target_pairs={{0,48},{1,49},{2,50},{3,51},{4,52},{5,53},{6,54},{7,55},{8,56},{9,... | collective-permute-start | bytes 811016 | tf_op jit(solution)/shard_map/ppermute | solution.py:27
  162.6 16.0 %copy-start.18 = (f32[352,512]{1,0:T(8,128)S(1)}, f32[352,512]{1,0:T(8,128)}, u32[]{:S(2)}) copy-start(f32[352,512]{1,0:T(8,128)} %get-tuple-element.63) | copy-start | bytes 2162692
  162.7 16.1 %collective-permute-start.32 = (bf16[352,512]{1,0:T(8,128)(2,1)S(1)}, bf16[352,512]{1,0:T(8,128)(2,1)S(1)}, u32[]{:S(2)}, u32[]{:S(2)}) collective-permute-start(bf16[352,512]{1,0:T(8,128)(2,1)S(1)} %fusion.4), channel_id=1, source_target_pairs={{0,192},{1,193},{2,194},{3,195},{4,196},{5,197},{6,198},{7,199},{8... | collective-permute-start | bytes 1081352 | tf_op jit(solution)/shard_map/ppermute | solution.py:27
  177.8 1.3 copy-start.17

commit v4 on v3

--- a/solution.py
+++ b/solution.py
@@ -12,7 +12,7 @@
 BLOCK = 256
 AXES = ("y", "zl", "zh", "x", "c")
 DIMS = (4, 4, 2, 4, 2)
-VMEM_LIMIT = 50 * 1024 * 1024
+VMEM_LIMIT = 60 * 1024 * 1024
 bf16, f32 = jnp.bfloat16, jnp.float32
 
 ORDERS = ((1, 3), (3, 1))

time: 181 us -> 183 us (1.011)
  the two profiles are of different devices: /device:TPU:79 before, /device:TPU:1 now
where the time goes in v4:
time: 183 us; the launch traced here: 181 us
  waiting for transfers between devices  76 us (42%)
  starting transfers between devices  49.8 us (27%)
  Pallas kernels  33.4 us (18%)
  other arithmetic  14.6 us (8%)
  local copies, waits for them, and re-layouts  6.4 us (3%)
    ppermute x33, waiting for transfers between devices, permute(): return lax.ppermute(array, AXES, pairs)  76 us
    ppermute x33, starting transfers between devices, permute(): return lax.ppermute(array, AXES, pairs)  49.8 us
    pallas_call x4, Pallas kernels, call(): pl.pallas_call(kernel, out_shape=outputs, in_specs=[pl.BlockSpec(memory_s...  33.4 us
    unnamed x62, local copies, waits for them, and re-layouts  5.35 us
    convert_element_type x2, other arithmetic, pass_on(): (keep[1].astype(f32) + got[1].astype(f32) + first[1].astype(f32)).astype(...  4.04 us
  transfers between devices with their start and end apart: 33, of which 13 were waited for; matrix products, arithmetic and copies ran while one was open for 8% of the time, Pallas kernels for 15%

profile of v4, /device:TPU:1, one launch (start us, length us, event | category | flops | bytes accessed | tf_op | source)
XLA Modules:
  0.0 181.4 jit_solution(7308796522890058984)
XLA Ops:
  0.6 9.6 %collective-permute-start = (bf16[384,512]{1,0:T(8,128)(2,1)}, bf16[384,512]{1,0:T(8,128)(2,1)S(1)}, u32[]{:S(2)}, u32[]{:S(2)}) collective-permute-start(bf16[384,512]{1,0:T(8,128)(2,1)} %param.7), channel_id=1, source_target_pairs={{0,10},{1,31},{2,42},{3,63},{4,8},{5,29},{6,40},{7,61},{8,6},{9,19... | collective-permute-start | bytes 1179656 | tf_op jit(solution)/shard_map/ppermute | solution.py:27
  10.2 0.9 copy.7
  11.1 0.9 broadcast_in_dim.3
  12.0 0.1 copy.8
  12.1 1.0 copy-done.8
  13.1 0.2 multiply_convert_fusion
  13.4 1.4 collective-permute-start.10
  14.8 0.2 collective-permute-start.11
  15.0 3.9 %collective-permute-start.1 = (bf16[384,512]{1,0:T(8,128)(2,1)S(1)}, bf16[384,512]{1,0:T(8,128)(2,1)S(1)}, u32[]{:S(2)}, u32[]{:S(2)}) collective-permute-start(bf16[384,512]{1,0:T(8,128)(2,1)S(1)} %copy-done.29), channel_id=1, source_target_pairs={{0,0},{1,21},{2,32},{3,53},{4,2},{5,23},{6,34},{7,55},{8,12},{9,25... | collective-permute-start | bytes 1179656 | tf_op jit(solution)/shard_map/ppermute | solution.py:27
  18.9 17.9 %collective-permute-done.refs_2_.refs_5_ = bf16[384,512]{1,0:T(8,128)(2,1)S(1)} collective-permute-done((bf16[384,512]{1,0:T(8,128)(2,1)}, bf16[384,512]{1,0:T(8,128)(2,1)S(1)}, u32[]{:S(2)}, u32[]{:S(2)}) %collective-permute-start) | collective-permute-done | bytes 393248 | tf_op jit(solution)/shard_map/ppermute | solution.py:27
  37.0 2.8 %collective-permute-start.12 = (bf16[2,704,512]{2,1,0:T(8,128)(2,1)S(1)}, bf16[2,704,512]{2,1,0:T(8,128)(2,1)S(1)}, u32[]{:S(2)}, u32[]{:S(2)}) collective-permute-start(bf16[2,704,512]{2,1,0:T(8,128)(2,1)S(1)} %bitcast.64), channel_id=1, source_target_pairs={{0,192},{1,193},{2,194},{3,195},{4,196},{5,197},{6,198},{7,199},{8... | collective-permute-start | bytes 4325384 | tf_op jit(solution)/shard_map/ppermute | solution.py:27
  40.0 1.7 collective-permute-start.8
  41.7 4.6 %collective-permute-done.2.refs_3_.refs_6_ = bf16[384,512]{1,0:T(8,128)(2,1)S(1)} collective-permute-done((bf16[384,512]{1,0:T(8,128)(2,1)S(1)}, bf16[384,512]{1,0:T(8,128)(2,1)S(1)}, u32[]{:S(2)}, u32[]{:S(2)}) %collective-permute-start.2) | collective-permute-done | bytes 393248 | tf_op jit(solution)/shard_map/ppermute | solution.py:27
  46.3 0.1 collective-permute-start.3
  46.5 5.1 %collective-permute-done.4.refs_8_.refs_11_ = bf16[384,512]{1,0:T(8,128)(2,1)S(1)} collective-permute-done((bf16[384,512]{1,0:T(8,128)(2,1)S(1)}, bf16[384,512]{1,0:T(8,128)(2,1)S(1)}, u32[]{:S(2)}, u32[]{:S(2)}) %collective-permute-start.4) | collective-permute-done | bytes 393248 | tf_op jit(solution)/shard_map/ppermute | solution.py:27
  52.1 0.3 copy-done.15
  52.3 0.3 copy-done.4
  52.6 15.8 %collective-permute-done.3.refs_4_.refs_7_ = bf16[2,384,512]{2,1,0:T(8,128)(2,1)S(1)} collective-permute-done((bf16[2,384,512]{2,1,0:T(8,128)(2,1)S(1)}, bf16[2,384,512]{2,1,0:T(8,128)(2,1)S(1)}, u32[]{:S(2)}, u32[]{:S(2)}) %collective-permute-start.3) | collective-permute-done | bytes 786464 | tf_op jit(solution)/shard_map/ppermute | solution.py:27
  68.4 0.9 collective-permute-done.5.refs_9_.refs_12_
  69.3 7.8 %collective-permute-done.9.refs_4_ = bf16[2,352,384]{2,1,0:T(8,128)(2,1)S(1)} collective-permute-done((bf16[2,352,384]{2,1,0:T(8,128)(2,1)S(1)}, bf16[2,352,384]{2,1,0:T(8,128)(2,1)S(1)}, u32[]{:S(2)}, u32[]{:S(2)}) %collective-permute-start.9) | collective-permute-done | bytes 540704 | tf_op jit(solution)/shard_map/ppermute | solution.py:27
  77.2 0.8 copy-done.28
  77.9 1.1 copy-done.22
  79.0 6.0 %mixed_terms.2 = (bf16[4,384,512]{2,1,0:T(8,128)(2,1)}, bf16[4,384,512]{2,1,0:T(8,128)(2,1)}) custom-call(bf16[704,384]{1,0:T(8,128)(2,1)} %bitcast.68, bf16[352,384]{1,0:T(8,128)(2,1)} %copy-done.20, bf16[2,352,384]{2,1,0:T(8,128)(2,1)} %copy-done.27, bf16[352,384]{1,0:T(8,128)(2,1)} %copy-done.21, bf16[2,352,384]{2,1,0:T(8,128)(2,1)} %copy-done.28, ...), custom_call_target="tpu_custom_call" | custom-call | flops 2214592512 | bytes 8192000 | tf_op jit(solution)/shard_map/mixed_terms/pallas_call | solution.py:210
  85.0 2.0 %collective-permute-start.13 = (bf16[4,384,512]{2,1,0:T(8,128)(2,1)}, bf16[4,384,512]{2,1,0:T(8,128)(2,1)S(1)}, u32[]{:S(2)}, u32[]{:S(2)}) collective-permute-start(bf16[4,384,512]{2,1,0:T(8,128)(2,1)} %get-tuple-element.36), channel_id=1, source_target_pairs={{0,1},{1,0},{2,3},{3,2},{4,5},{5,4},{6,7},{7,6},{8,9},{9,8},{10,11... | collective-permute-start | bytes 4718600 | tf_op jit(solution)/shard_map/ppermute | solution.py:27
  87.0 6.0 %mixed_terms.3 = (bf16[4,384,512]{2,1,0:T(8,128)(2,1)}, bf16[4,384,512]{2,1,0:T(8,128)(2,1)}) custom-call(bf16[704,384]{1,0:T(8,128)(2,1)} %bitcast.69, bf16[352,384]{1,0:T(8,128)(2,1)} %copy-done.20, bf16[2,352,384]{2,1,0:T(8,128)(2,1)} %copy-done.27, bf16[352,384]{1,0:T(8,128)(2,1)} %copy-done.21, bf16[2,352,384]{2,1,0:T(8,128)(2,1)} %copy-done.28, ...), custom_call_target="tpu_custom_call" | custom-call | flops 2214592512 | bytes 8192000 | tf_op jit(solution)/shard_map/mixed_terms/pallas_call | solution.py:210
  93.0 0.3 collective-permute-start.14
  93.3 0.3 collective-permute-start.19
  93.6 0.2 collective-permute-start.21
  93.8 0.3 collective-permute-start.20
  94.1 0.2 collective-permute-start.22
  94.3 1.1 add_convert_fusion
  95.4 1.3 collective-permute-done.14
  96.7 1.9 %collective-permute-start.16 = (bf16[2,384,512]{2,1,0:T(8,128)(2,1)}, bf16[2,384,512]{2,1,0:T(8,128)(2,1)}, u32[]{:S(2)}, u32[]{:S(2)}) collective-permute-start(bf16[2,384,512]{2,1,0:T(8,128)(2,1)} %add_convert_fusion), channel_id=1, source_target_pairs={{0,2},{1,3},{2,0},{3,1},{4,6},{5,7},{6,4},{7,5},{8,10},{9,11},{10,... | collective-permute-start | bytes 2359304 | tf_op jit(solution)/shard_map/ppermute | solution.py:27
  98.6 1.1 add_convert_fusion.1
  99.7 0.9 copy-done.25
  100.6 1.9 %collective-permute-start.15 = (bf16[2,384,512]{2,1,0:T(8,128)(2,1)}, bf16[2,384,512]{2,1,0:T(8,128)(2,1)}, u32[]{:S(2)}, u32[]{:S(2)}) collective-permute-start(bf16[2,384,512]{2,1,0:T(8,128)(2,1)} %add_convert_fusion.1), channel_id=1, source_target_pairs={{0,6},{1,7},{2,4},{3,5},{4,2},{5,3},{6,0},{7,1},{8,14},{9,15},{10,... | collective-permute-start | bytes 2359304 | tf_op jit(solution)/shard_map/ppermute | solution.py:27
  102.5 11.6 %hidden_terms.1 = (f32[352,384]{1,0:T(8,128)}, bf16[352,384]{1,0:T(8,128)(2,1)}, bf16[2,352,384]{2,1,0:T(8,128)(2,1)}, f32[352,384]{1,0:T(8,128)}, bf16[352,384]...) custom-call(bf16[2,704,512]{2,1,0:T(8,128)(2,1)} %bitcast.67, bf16[2,704,512]{2,1,0:T(8,128)(2,1)} %copy-done.22, ...), custom_call_target="tpu_custom_call" | custom-call | flops 4429185024 | bytes 11878400 | tf_op jit(solution)/shard_map/hidden_terms/pallas_call | solution.py:210
  114.2 1.0 collective-permute-start.28
  115.2 1.6 collective-permute-done.16
  116.8 1.9 %fusion.12 = bf16[384,512]{1,0:T(8,128)(2,1)} fusion(bf16[2,384,512]{2,1,0:T(8,128)(2,1)} %collective-permute-done.16, bf16[4,384,512]{2,1,0:T(8,128)(2,1)S(1)} %collective-permute-done.13, bf16[4,384,512]{2,1,0:T(8,128)(2,1)S(1)} %copy-done), kind=kLoop, calls=%fused_computation.35 | loop fusion | flops 1179648 | bytes 1572864 | tf_op jit(solution)/shard_map/convert_element_type | solution.py:286
  118.7 1.8 %collective-permute-start.17 = (bf16[384,512]{1,0:T(8,128)(2,1)}, bf16[384,512]{1,0:T(8,128)(2,1)S(1)}, u32[]{:S(2)}, u32[]{:S(2)}) collective-permute-start(bf16[384,512]{1,0:T(8,128)(2,1)} %fusion.12), channel_id=1, source_target_pairs={{0,6},{1,7},{2,4},{3,5},{4,2},{5,3},{6,0},{7,1},{8,14},{9,15},{10,... | collective-permute-start | bytes 1179656 | tf_op jit(solution)/shard_map/ppermute | solution.py:27
  120.5 0.3 collective-permute-done.15
  120.8 2.2 %fusion.13 = bf16[384,512]{1,0:T(8,128)(2,1)} fusion(bf16[2,384,512]{2,1,0:T(8,128)(2,1)} %collective-permute-done.15, bf16[4,384,512]{2,1,0:T(8,128)(2,1)} %copy-done.2, bf16[4,384,512]{2,1,0:T(8,128)(2,1)} %get-tuple-element.38), kind=kLoop, calls=%fused_computation.36 | loop fusion | flops 1179648 | bytes 1572864 | tf_op jit(solution)/shard_map/convert_element_type | solution.py:286
  123.0 0.3 collective-permute-start.18
  123.3 9.8 %weight_terms.1 = (f32[352,512]{1,0:T(8,128)}, bf16[352,512]{1,0:T(8,128)(2,1)}, bf16[2,352,512]{2,1,0:T(8,128)(2,1)}, f32[352,512]{1,0:T(8,128)}, bf16[352,512]...) custom-call(bf16[704,384]{1,0:T(8,128)(2,1)} %bitcast.70, bf16[352,384]{1,0:T(8,128)(2,1)} %copy-done.20, ...), custom_call_target="tpu_custom_call" | custom-call | flops 4429185024 | bytes 12058624 | tf_op jit(solution)/shard_map/weight_terms/pallas_call | solution.py:210
  133.1 1.2 collective-permute-start.26
  134.3 1.9 %broadcast_select_fusion = (bf16[384,512]{1,0:T(8,128)(2,1)S(1)}, bf16[384,512]{1,0:T(8,128)(2,1)S(1)}, bf16[384,512]{1,0:T(8,128)(2,1)S(1)}) fusion(pred[]{:T(512)S(6)} %eq.5, bf16[384,512]{1,0:T(8,128)(2,1)S(1)} %collective-permute-done.17, bf16[2,384,512]{2,1,0:T(8,128)(2,1)} %collective-permute-done.16, ...), kind=kLoop, calls=%fused_computation.37 | loop fusion | flops 3342336 | bytes 4325377 | tf_op jit(solution)/shard_map/jit(_where)/select_n | solution.py:342
  136.3 1.1 fusion.8
  137.4 3.9 %collective-permute-start.29 = (bf16[352,384]{1,0:T(8,128)(2,1)S(1)}, bf16[352,384]{1,0:T(8,128)(2,1)S(1)}, u32[]{:S(2)}, u32[]{:S(2)}) collective-permute-start(bf16[352,384]{1,0:T(8,128)(2,1)S(1)} %fusion.8), channel_id=1, source_target_pairs={{0,16},{1,17},{2,18},{3,19},{4,20},{5,21},{6,22},{7,23},{8,24},{9,... | collective-permute-start | bytes 811016 | tf_op jit(solution)/shard_map/ppermute | solution.py:27
  141.3 8.0 %collective-permute-start.23 = (bf16[384,512]{1,0:T(8,128)(2,1)S(1)}, bf16[384,512]{1,0:T(8,128)(2,1)S(1)}, u32[]{:S(2)}, u32[]{:S(2)}) collective-permute-start(bf16[384,512]{1,0:T(8,128)(2,1)S(1)} %broadcast_select_fusion.1), channel_id=1, source_target_pairs={{0,44},{1,60},{2,40},{3,56},{4,12},{5,28},{6,8},{7,24},{8,4},{9,20... | collective-permute-start | bytes 1179656 | tf_op jit(solution)/shard_map/ppermute | solution.py:27
  149.3 2.1 %collective-permute-start.24 = (bf16[384,512]{1,0:T(8,128)(2,1)S(1)}, bf16[384,512]{1,0:T(8,128)(2,1)S(1)}, u32[]{:S(2)}, u32[]{:S(2)}) collective-permute-start(bf16[384,512]{1,0:T(8,128)(2,1)S(1)} %get-tuple-element.65), channel_id=1, source_target_pairs={{0,0},{1,16},{2,4},{3,20},{4,32},{5,48},{6,36},{7,52},{8,40},{9,56... | collective-permute-start | bytes 1179656 | tf_op jit(solution)/shard_map/ppermute | solution.py:27
  151.7 1.1 fusion.10
  152.9 1.6 collective-permute-start.31
  154.5 2.7 %collective-permute-start.30 = (bf16[352,384]{1,0:T(8,128)(2,1)S(1)}, bf16[352,384]{1,0:T(8,128)(2,1)S(1)}, u32[]{:S(2)}, u32[]{:S(2)}) collective-permute-start(bf16[352,384]{1,0:T(8,128)(2,1)S(1)} %fusion.11), channel_id=1, source_target_pairs={{0,48},{1,49},{2,50},{3,51},{4,52},{5,53},{6,54},{7,55},{8,56},{9,... | collective-permute-start | bytes 811016 | tf_op jit(solution)/shard_map/ppermute | solution.py:27
  157.2 12.6 %collective-permute-done.27 = bf16[2,352,512]{2,1,0:T(8,128)(2,1)S(1)} collective-permute-done((bf16[2,352,512]{2,1,0:T(8,128)(2,1)S(1)}, bf16[2,352,512]{2,1,0:T(8,128)(2,1)S(1)}, u32[]{:S(2)}, u32[]{:S(2)}) %collective-permute-start.27) | collective-permute-done | bytes 720928 | tf_op jit(solution)/shard_map/ppermute | solution.py:27
  170.0 1.1 collective-permute-done.24
  171.1 0.8 add_convert_fusion.2
  171.9 0.1 fusion.7
  172.0 0.9 maximum_bitcast_fusion
  172.9 3.5 %collective-permute-done.31 = bf16[352,512]{1,0:T(8,128)(2,1)S(1)} collective-permute-done((bf16[352,512]{1,0:T(8,128)(2,1)S(1)}, bf16[352,512]{1,0:T(8,128)(2,1)S(1)}, u32[]{:S(2)}, u32[]{:S(2)}) %collective-permute-start.31) | collective-permute-done | bytes 360480 | tf_op jit(solution)/shard_map/ppermute | solution.py:27
  176.4 0.2 fusion.3
  176.6 3.4 %collective-permute-done.32 = bf16[352,512]{1,0:T(8,128)(2,1)S(1)} collective-permute-done((bf16[352,512]{1,0:T(8,128)(2,1)S(1)}, bf16[352,512]{1,0:T(8,128)(2,1)S(1)}, u32[]{:S(2)}, u32[]{:S(2)}) %collective-permute-start.32) | collective-permute-done | bytes 360480 | tf_op jit(solution)/shard_map/ppermute | solution.py:27
  180.0 0.2 fusion.2
  180.2 1.2 pad_maximum_fusion.1
  (94 shorter events, 1.5 us)
Async XLA Ops:
  0.6 36.2 %collective-permute-start = (bf16[384,512]{1,0:T(8,128)(2,1)}, bf16[384,512]{1,0:T(8,128)(2,1)S(1)}, u32[]{:S(2)}, u32[]{:S(2)}) collective-permute-start(bf16[384,512]{1,0:T(8,128)(2,1)} %param.7), channel_id=1, source_target_pairs={{0,10},{1,31},{2,42},{3,63},{4,8},{5,29},{6,40},{7,61},{8,6},{9,19... | collective-permute-start | bytes 1179656 | tf_op jit(solution)/shard_map/ppermute | solution.py:27
  12.0 1.1 copy-start.8
  13.1 1.9 %copy-start.29 = (bf16[384,512]{1,0:T(8,128)(2,1)S(1)}, bf16[384,512]{1,0:T(8,128)(2,1)}, u32[]{:S(2)}) copy-start(bf16[384,512]{1,0:T(8,128)(2,1)} %param.7) | copy-start | bytes 1179652
  13.4 26.4 %copy-start.9 = (bf16[384,704]{0,1:T(8,128)(2,1)S(1)}, bf16[384,704]{0,1:T(8,128)(2,1)}, u32[]{:S(2)}) copy-start(bf16[384,704]{0,1:T(8,128)(2,1)} %param.4) | copy-start | bytes 1622020
  13.4 23.4 %collective-permute-start.10 = (bf16[352,512]{1,0:T(8,128)(2,1)S(1)}, bf16[352,512]{1,0:T(8,128)(2,1)S(1)}, u32[]{:S(2)}, u32[]{:S(2)}) collective-permute-start(bf16[352,512]{1,0:T(8,128)(2,1)S(1)} %get-tuple-element.68), channel_id=1, source_target_pairs={{0,64},{1,65},{2,66},{3,67},{4,68},{5,69},{6,70},{7,71},{8,72},{9,... | collective-permute-start | bytes 1081352 | tf_op jit(solution)/shard_map/ppermute | solution.py:27
  14.8 22.0 %collective-permute-start.11 = (bf16[352,512]{1,0:T(8,128)(2,1)S(1)}, bf16[352,512]{1,0:T(8,128)(2,1)S(1)}, u32[]{:S(2)}, u32[]{:S(2)}) collective-permute-start(bf16[352,512]{1,0:T(8,128)(2,1)S(1)} %get-tuple-element.69), channel_id=1, source_target_pairs={{0,64},{1,65},{2,66},{3,67},{4,68},{5,69},{6,70},{7,71},{8,72},{9,... | collective-permute-start | bytes 1081352 | tf_op jit(solution)/shard_map/ppermute | solution.py:27
  15.0 24.8 %collective-permute-start.1 = (bf16[384,512]{1,0:T(8,128)(2,1)S(1)}, bf16[384,512]{1,0:T(8,128)(2,1)S(1)}, u32[]{:S(2)}, u32[]{:S(2)}) collective-permute-start(bf16[384,512]{1,0:T(8,128)(2,1)S(1)} %copy-done.29), channel_id=1, source_target_pairs={{0,0},{1,21},{2,32},{3,53},{4,2},{5,23},{6,34},{7,55},{8,12},{9,25... | collective-permute-start | bytes 1179656 | tf_op jit(solution)/shard_map/ppermute | solution.py:27
  36.8 9.4 %copy-start.12 = (bf16[384,512]{1,0:T(8,128)(2,1)}, bf16[384,512]{1,0:T(8,128)(2,1)S(1)}, u32[]{:S(2)}) copy-start(bf16[384,512]{1,0:T(8,128)(2,1)S(1)} %collective-permute-done.refs_2_.refs_5_) | copy-start | bytes 1179652
  36.8 9.4 %collective-permute-start.2 = (bf16[384,512]{1,0:T(8,128)(2,1)S(1)}, bf16[384,512]{1,0:T(8,128)(2,1)S(1)}, u32[]{:S(2)}, u32[]{:S(2)}) collective-permute-start(bf16[384,512]{1,0:T(8,128)(2,1)S(1)} %collective-permute-done.refs_2_.refs_5_), channel_id=1, source_target_pairs={{0,2},{1,3},{2,0},{3,1},{4,6},{5,7},{6,4},{7,5},{8,10},{9,11},{10,... | collective-permute-start | bytes 1179656 | tf_op jit(solution)/shard_map/ppermute | solution.py:27
  37.0 9.4 %copy-start.3 = (bf16[1408,512]{1,0:T(8,128)(2,1)}, bf16[1408,512]{1,0:T(8,128)(2,1)S(1)}, u32[]{:S(2)}) copy-start(bf16[1408,512]{1,0:T(8,128)(2,1)S(1)} %pad_maximum_fusion) | copy-start | bytes 4325380
  37.0 40.2 %collective-permute-start.12 = (bf16[2,704,512]{2,1,0:T(8,128)(2,1)S(1)}, bf16[2,704,512]{2,1,0:T(8,128)(2,1)S(1)}, u32[]{:S(2)}, u32[]{:S(2)}) collective-permute-start(bf16[2,704,512]{2,1,0:T(8,128)(2,1)S(1)} %bitcast.64), channel_id=1, source_target_pairs={{0,192},{1,193},{2,194},{3,195},{4,196},{5,197},{6,198},{7,199},{8... | collective-permute-start | bytes 4325384 | tf_op jit(solution)/shard_map/ppermute | solution.py:27
  39.8 11.8 %copy-start.13 = (bf16[384,512]{1,0:T(8,128)(2,1)}, bf16[384,512]{1,0:T(8,128)(2,1)S(1)}, u32[]{:S(2)}) copy-start(bf16[384,512]{1,0:T(8,128)(2,1)S(1)} %collective-permute-done.1.refs_7_.refs_10_) | copy-start | bytes 1179652
  39.8 11.8 %collective-permute-start.4 = (bf16[384,512]{1,0:T(8,128)(2,1)S(1)}, bf16[384,512]{1,0:T(8,128)(2,1)S(1)}, u32[]{:S(2)}, u32[]{:S(2)}) collective-permute-start(bf16[384,512]{1,0:T(8,128)(2,1)S(1)} %collective-permute-done.1.refs_7_.refs_10_), channel_id=1, source_target_pairs={{0,6},{1,7},{2,4},{3,5},{4,2},{5,3},{6,0},{7,1},{8,14},{9,15},{10,... | collective-permute-start | bytes 1179656 | tf_op jit(solution)/shard_map/ppermute | solution.py:27
  39.9 11.9 %collective-permute-start.6 = (bf16[352,384]{1,0:T(8,128)(2,1)S(1)}, bf16[352,384]{1,0:T(8,128)(2,1)S(1)}, u32[]{:S(2)}, u32[]{:S(2)}) collective-permute-start(bf16[352,384]{1,0:T(8,128)(2,1)S(1)} %get-tuple-element.73), channel_id=1, source_target_pairs={{0,16},{1,17},{2,18},{3,19},{4,20},{5,21},{6,22},{7,23},{8,24},{9,... | collective-permute-start | bytes 811016 | tf_op jit(solution)/shard_map/ppermute | solution.py:27
  40.0 12.0 %collective-permute-start.8 = (bf16[352,384]{1,0:T(8,128)(2,1)S(1)}, bf16[352,384]{1,0:T(8,128)(2,1)S(1)}, u32[]{:S(2)}, u32[]{:S(2)}) collective-permute-start(bf16[352,384]{1,0:T(8,128)(2,1)S(1)} %get-tuple-element.72), channel_id=1, source_target_pairs={{0,48},{1,49},{2,50},{3,51},{4,52},{5,53},{6,54},{7,55},{8,56},{9,... | collective-permute-start | bytes 811016 | tf_op jit(solution)/shard_map/ppermute | solution.py:27
  46.2 5.4 %copy-start.14 = (bf16[384,512]{1,0:T(8,128)(2,1)}, bf16[384,512]{1,0:T(8,128)(2,1)S(1)}, u32[]{:S(2)}) copy-start(bf16[384,512]{1,0:T(8,128)(2,1)S(1)} %collective-permute-done.2.refs_3_.refs_6_) | copy-start | bytes 1179652
  46.3 5.7 %copy-start.5 = (bf16[2,384,512]{2,1,0:T(8,128)(2,1)}, bf16[2,384,512]{2,1,0:T(8,128)(2,1)S(1)}, u32[]{:S(2)}) copy-start(bf16[2,384,512]{2,1,0:T(8,128)(2,1)S(1)} %pad_maximum_fusion.2) | copy-start | bytes 2359300
  46.3 22.1 %collective-permute-start.3 = (bf16[2,384,512]{2,1,0:T(8,128)(2,1)S(1)}, bf16[2,384,512]{2,1,0:T(8,128)(2,1)S(1)}, u32[]{:S(2)}, u32[]{:S(2)}) collective-permute-start(bf16[2,384,512]{2,1,0:T(8,128)(2,1)S(1)} %pad_maximum_fusion.2), channel_id=1, source_target_pairs={{0,6},{1,7},{2,4},{3,5},{4,2},{5,3},{6,0},{7,1},{8,14},{9,15},{10,... | collective-permute-start | bytes 2359304 | tf_op jit(solution)/shard_map/ppermute | solution.py:27
  51.6 0.8 copy-start.15
  51.7 0.9 copy-start.4
  51.7 17.6 %collective-permute-start.5 = (bf16[2,384,512]{2,1,0:T(8,128)(2,1)S(1)}, bf16[2,384,512]{2,1,0:T(8,128)(2,1)S(1)}, u32[]{:S(2)}, u32[]{:S(2)}) collective-permute-start(bf16[2,384,512]{2,1,0:T(8,128)(2,1)S(1)} %pad_maximum_fusion.3), channel_id=1, source_target_pairs={{0,2},{1,3},{2,0},{3,1},{4,6},{5,7},{6,4},{7,5},{8,10},{9,11},{10,... | collective-permute-start | bytes 2359304 | tf_op jit(solution)/shard_map/ppermute | solution.py:27
  51.8 25.3 %copy-start.20 = (bf16[352,384]{1,0:T(8,128)(2,1)}, bf16[352,384]{1,0:T(8,128)(2,1)S(1)}, u32[]{:S(2)}) copy-start(bf16[352,384]{1,0:T(8,128)(2,1)S(1)} %collective-permute-done.6.refs_1_) | copy-start | bytes 811012
  51.9 17.4 %collective-permute-start.7 = (bf16[2,352,384]{2,1,0:T(8,128)(2,1)S(1)}, bf16[2,352,384]{2,1,0:T(8,128)(2,1)S(1)}, u32[]{:S(2)}, u32[]{:S(2)}) collective-permute-start(bf16[2,352,384]{2,1,0:T(8,128)(2,1)S(1)} %pad_maximum_fusion.4), channel_id=1, source_target_pairs={{0,48},{1,49},{2,50},{3,51},{4,52},{5,53},{6,54},{7,55},{8,56},{9,... | collective-permute-start | bytes 1622024 | tf_op jit(solution)/shard_map/ppermute | solution.py:27
  52.0 25.2 %copy-start.21 = (bf16[352,384]{1,0:T(8,128)(2,1)}, bf16[352,384]{1,0:T(8,128)(2,1)S(1)}, u32[]{:S(2)}) copy-start(bf16[352,384]{1,0:T(8,128)(2,1)S(1)} %collective-permute-done.8.refs_3_) | copy-start | bytes 811012
  52.6 24.5 %collective-permute-start.9 = (bf16[2,352,384]{2,1,0:T(8,128)(2,1)S(1)}, bf16[2,352,384]{2,1,0:T(8,128)(2,1)S(1)}, u32[]{:S(2)}, u32[]{:S(2)}) collective-permute-start(bf16[2,352,384]{2,1,0:T(8,128)(2,1)S(1)} %pad_maximum_fusion.5), channel_id=1, source_target_pairs={{0,16},{1,17},{2,18},{3,19},{4,20},{5,21},{6,22},{7,23},{8,24},{9,... | collective-permute-start | bytes 1622024 | tf_op jit(solution)/shard_map/ppermute | solution.py:27
  68.4 8.7 %copy-start.23 = (bf16[2,384,512]{2,1,0:T(8,128)(2,1)}, bf16[2,384,512]{2,1,0:T(8,128)(2,1)S(1)}, u32[]{:S(2)}) copy-start(bf16[2,384,512]{2,1,0:T(8,128)(2,1)S(1)} %collective-permute-done.3.refs_4_.refs_7_) | copy-start | bytes 2359300
  69.3 7.8 %copy-start.24 = (bf16[2,384,512]{2,1,0:T(8,128)(2,1)}, bf16[2,384,512]{2,1,0:T(8,128)(2,1)S(1)}, u32[]{:S(2)}) copy-start(bf16[2,384,512]{2,1,0:T(8,128)(2,1)S(1)} %collective-permute-done.5.refs_9_.refs_12_) | copy-start | bytes 2359300
  69.3 7.8 %copy-start.27 = (bf16[2,352,384]{2,1,0:T(8,128)(2,1)}, bf16[2,352,384]{2,1,0:T(8,128)(2,1)S(1)}, u32[]{:S(2)}) copy-start(bf16[2,352,384]{2,1,0:T(8,128)(2,1)S(1)} %collective-permute-done.7.refs_2_) | copy-start | bytes 1622020
  77.1 0.8 copy-start.28
  77.9 1.1 copy-start.22
  85.0 9.3 %copy-start = (bf16[4,384,512]{2,1,0:T(8,128)(2,1)S(1)}, bf16[4,384,512]{2,1,0:T(8,128)(2,1)}, u32[]{:S(2)}) copy-start(bf16[4,384,512]{2,1,0:T(8,128)(2,1)} %get-tuple-element.41) | copy-start | bytes 4718596
  85.0 8.0 %collective-permute-start.13 = (bf16[4,384,512]{2,1,0:T(8,128)(2,1)}, bf16[4,384,512]{2,1,0:T(8,128)(2,1)S(1)}, u32[]{:S(2)}, u32[]{:S(2)}) collective-permute-start(bf16[4,384,512]{2,1,0:T(8,128)(2,1)} %get-tuple-element.36), channel_id=1, source_target_pairs={{0,1},{1,0},{2,3},{3,2},{4,5},{5,4},{6,7},{7,6},{8,9},{9,8},{10,11... | collective-permute-start | bytes 4718600 | tf_op jit(solution)/shard_map/ppermute | solution.py:27
  93.0 5.6 %copy-start.1 = (bf16[4,384,512]{2,1,0:T(8,128)(2,1)S(1)}, bf16[4,384,512]{2,1,0:T(8,128)(2,1)}, u32[]{:S(2)}) copy-start(bf16[4,384,512]{2,1,0:T(8,128)(2,1)} %get-tuple-element.38) | copy-start | bytes 4718596
  93.0 3.7 %collective-permute-start.14 = (bf16[4,384,512]{2,1,0:T(8,128)(2,1)}, bf16[4,384,512]{2,1,0:T(8,128)(2,1)S(1)}, u32[]{:S(2)}, u32[]{:S(2)}) collective-permute-start(bf16[4,384,512]{2,1,0:T(8,128)(2,1)} %get-tuple-element.40), channel_id=1, source_target_pairs={{0,1},{1,0},{2,3},{3,2},{4,5},{5,4},{6,7},{7,6},{8,9},{9,8},{10,11... | collective-permute-start | bytes 4718600 | tf_op jit(solution)/shard_map/ppermute | solution.py:27
  93.3 6.5 %collective-permute-start.19 = (bf16[2,384,512]{2,1,0:T(8,128)(2,1)}, bf16[2,384,512]{2,1,0:T(8,128)(2,1)S(1)}, u32[]{:S(2)}, u32[]{:S(2)}) collective-permute-start(bf16[2,384,512]{2,1,0:T(8,128)(2,1)} %copy-done.5), channel_id=1, source_target_pairs={{0,1},{1,0},{2,3},{3,2},{4,5},{5,4},{6,7},{7,6},{8,9},{9,8},{10,11... | collective-permute-start | bytes 2359304 | tf_op jit(solution)/shard_map/ppermute | solution.py:27
  93.6 8.9 %collective-permute-start.21 = (bf16[2,384,512]{2,1,0:T(8,128)(2,1)}, bf16[2,384,512]{2,1,0:T(8,128)(2,1)}, u32[]{:S(2)}, u32[]{:S(2)}) collective-permute-start(bf16[2,384,512]{2,1,0:T(8,128)(2,1)} %copy-done.4), channel_id=1, source_target_pairs={{0,1},{1,0},{2,3},{3,2},{4,5},{5,4},{6,7},{7,6},{8,9},{9,8},{10,11... | collective-permute-start | bytes 2359304 | tf_op jit(solution)/shard_map/ppermute | solution.py:27
  93.8 8.7 %collective-permute-start.20 = (bf16[2,384,512]{2,1,0:T(8,128)(2,1)}, bf16[2,384,512]{2,1,0:T(8,128)(2,1)}, u32[]{:S(2)}, u32[]{:S(2)}) collective-permute-start(bf16[2,384,512]{2,1,0:T(8,128)(2,1)} %copy-done.23), channel_id=1, source_target_pairs={{0,1},{1,0},{2,3},{3,2},{4,5},{5,4},{6,7},{7,6},{8,9},{9,8},{10,11... | collective-permute-start | bytes 2359304 | tf_op jit(solution)/shard_map/ppermute | solution.py:27
  94.1 8.4 %collective-permute-start.22 = (bf16[2,384,512]{2,1,0:T(8,128)(2,1)}, bf16[2,384,512]{2,1,0:T(8,128)(2,1)}, u32[]{:S(2)}, u32[]{:S(2)}) collective-permute-start(bf16[2,384,512]{2,1,0:T(8,128)(2,1)} %copy-done.24), channel_id=1, source_target_pairs={{0,1},{1,0},{2,3},{3,2},{4,5},{5,4},{6,7},{7,6},{8,9},{9,8},{10,11... | collective-permute-start | bytes 2359304 | tf_op jit(solution)/shard_map/ppermute | solution.py:27
  96.7 3.0 %copy-start.2 = (bf16[4,384,512]{2,1,0:T(8,128)(2,1)}, bf16[4,384,512]{2,1,0:T(8,128)(2,1)S(1)}, u32[]{:S(2)}) copy-start(bf16[4,384,512]{2,1,0:T(8,128)(2,1)S(1)} %collective-permute-done.14) | copy-start | bytes 4718596
  96.7 20.1 %collective-permute-start.16 = (bf16[2,384,512]{2,1,0:T(8,128)(2,1)}, bf16[2,384,512]{2,1,0:T(8,128)(2,1)}, u32[]{:S(2)}, u32[]{:S(2)}) collective-permute-start(bf16[2,384,512]{2,1,0:T(8,128)(2,1)} %add_convert_fusion), channel_id=1, source_target_pairs={{0,2},{1,3},{2,0},{3,1},{4,6},{5,7},{6,4},{7,5},{8,10},{9,11},{10,... | collective-permute-start | bytes 2359304 | tf_op jit(solution)/shard_map/ppermute | solution.py:27
  99.7 0.9 copy-start.25
  100.6 20.2 %collective-permute-start.15 = (bf16[2,384,512]{2,1,0:T(8,128)(2,1)}, bf16[2,384,512]{2,1,0:T(8,128)(2,1)}, u32[]{:S(2)}, u32[]{:S(2)}) collective-permute-start(bf16[2,384,512]{2,1,0:T(8,128)(2,1)} %add_convert_fusion.1), channel_id=1, source_target_pairs={{0,6},{1,7},{2,4},{3,5},{4,2},{5,3},{6,0},{7,1},{8,14},{9,15},{10,... | collective-permute-start | bytes 2359304 | tf_op jit(solution)/shard_map/ppermute | solution.py:27
  114.2 22.1 %collective-permute-start.28 = (bf16[2,352,384]{2,1,0:T(8,128)(2,1)}, bf16[2,352,384]{2,1,0:T(8,128)(2,1)}, u32[]{:S(2)}, u32[]{:S(2)}) collective-permute-start(bf16[2,352,384]{2,1,0:T(8,128)(2,1)} %get-tuple-element.43), channel_id=1, source_target_pairs={{0,48},{1,49},{2,50},{3,51},{4,52},{5,53},{6,54},{7,55},{8,56},{9,... | collective-permute-start | bytes 1622024 | tf_op jit(solution)/shard_map/ppermute | solution.py:27
  115.2 36.3 %collective-permute-start.25 = (bf16[2,352,384]{2,1,0:T(8,128)(2,1)}, bf16[2,352,384]{2,1,0:T(8,128)(2,1)S(1)}, u32[]{:S(2)}, u32[]{:S(2)}) collective-permute-start(bf16[2,352,384]{2,1,0:T(8,128)(2,1)} %get-tuple-element.49), channel_id=1, source_target_pairs={{0,16},{1,17},{2,18},{3,19},{4,20},{5,21},{6,22},{7,23},{8,24},{9,... | collective-permute-start | bytes 1622024 | tf_op jit(solution)/shard_map/ppermute | solution.py:27
  118.7 14.4 %collective-permute-start.17 = (bf16[384,512]{1,0:T(8,128)(2,1)}, bf16[384,512]{1,0:T(8,128)(2,1)S(1)}, u32[]{:S(2)}, u32[]{:S(2)}) collective-permute-start(bf16[384,512]{1,0:T(8,128)(2,1)} %fusion.12), channel_id=1, source_target_pairs={{0,6},{1,7},{2,4},{3,5},{4,2},{5,3},{6,0},{7,1},{8,14},{9,15},{10,... | collective-permute-start | bytes 1179656 | tf_op jit(solution)/shard_map/ppermute | solution.py:27
  123.0 10.1 %collective-permute-start.18 = (bf16[384,512]{1,0:T(8,128)(2,1)}, bf16[384,512]{1,0:T(8,128)(2,1)}, u32[]{:S(2)}, u32[]{:S(2)}) collective-permute-start(bf16[384,512]{1,0:T(8,128)(2,1)} %fusion.13), channel_id=1, source_target_pairs={{0,2},{1,3},{2,0},{3,1},{4,6},{5,7},{6,4},{7,5},{8,10},{9,11},{10,... | collective-permute-start | bytes 1179656 | tf_op jit(solution)/shard_map/ppermute | solution.py:27
  133.1 3.2 %copy-start.19 = (bf16[352,384]{1,0:T(8,128)(2,1)S(1)}, bf16[352,384]{1,0:T(8,128)(2,1)}, u32[]{:S(2)}) copy-start(bf16[352,384]{1,0:T(8,128)(2,1)} %get-tuple-element.61) | copy-start | bytes 811012
  133.1 19.7 %collective-permute-start.26 = (bf16[2,352,512]{2,1,0:T(8,128)(2,1)}, bf16[2,352,512]{2,1,0:T(8,128)(2,1)S(1)}, u32[]{:S(2)}, u32[]{:S(2)}) collective-permute-start(bf16[2,352,512]{2,1,0:T(8,128)(2,1)} %get-tuple-element.51), channel_id=1, source_target_pairs={{0,192},{1,193},{2,194},{3,195},{4,196},{5,197},{6,198},{7,199},{8... | collective-permute-start | bytes 2162696 | tf_op jit(solution)/shard_map/ppermute | solution.py:27
  136.2 15.3 %copy-start.26 = (bf16[2,352,512]{2,1,0:T(8,128)(2,1)S(1)}, bf16[2,352,512]{2,1,0:T(8,128)(2,1)}, u32[]{:S(2)}) copy-start(bf16[2,352,512]{2,1,0:T(8,128)(2,1)} %get-tuple-element.56) | copy-start | bytes 2162692
  136.2 15.4 %copy-start.18 = (bf16[352,384]{1,0:T(8,128)(2,1)S(1)}, bf16[352,384]{1,0:T(8,128)(2,1)}, u32[]{:S(2)}) copy-start(bf16[352,384]{1,0:T(8,128)(2,1)} %get-tuple-element.48) | copy-start | bytes 811012
  136.2 15.5 %copy-start.11 = (f32[352,384]{1,0:T(8,128)S(1)}, f32[352,384]{1,0:T(8,128)}, u32[]{:S(2)}) copy-start(f32[352,384]{1,0:T(8,128)} %get-tuple-element.59) | copy-start | bytes 1622020
  136.3 16.5 %copy-start.17 = (bf16[352,512]{1,0:T(8,128)(2,1)S(1)}, bf16[352,512]{1,0:T(8,128)(2,1)}, u32[]{:S(2)}) copy-start(bf16[352,512]{1,0:T(8,128)(2,1)} %get-tuple-element.53) | copy-start | bytes 1081348
  137.4 14.3 %collective-permute-start.29 = (bf16[352,384]{1,0:T(8,128)(2,1)S(1)}, bf16[352,384]{1,0:T(8,128)(2,1)S(1)}, u32[]{:S(2)}, u32[]{:S(2)}) collective-permute-start(bf16[352,384]{1,0:T(8,128)(2,1)S(1)} %fusion.8), channel_id=1, source_target_pairs={{0,16},{1,17},{2,18},{3,19},{4,20},{5,21},{6,22},{7,23},{8,24},{9,... | collective-permute-start | bytes 811016 | tf_op jit(solution)/shard_map/ppermute | solution.py:27
  141.3 28.7 %collective-permute-start.23 = (bf16[384,512]{1,0:T(8,128)(2,1)S(1)}, bf16[384,512]{1,0:T(8,128)(2,1)S(1)}, u32[]{:S(2)}, u32[]{:S(2)}) collective-permute-start(bf16[384,512]{1,0:T(8,128)(2,1)S(1)} %broadcast_select_fusion.1), channel_id=1, source_target_pairs={{0,44},{1,60},{2,40},{3,56},{4,12},{5,28},{6,8},{7,24},{8,4},{9,20... | collective-permute-start | bytes 1179656 | tf_op jit(solution)/shard_map/ppermute | solution.py:27
  149.3 21.7 %collective-permute-start.24 = (bf16[384,512]{1,0:T(8,128)(2,1)S(1)}, bf16[384,512]{1,0:T(8,128)(2,1)S(1)}, u32[]{:S(2)}, u32[]{:S(2)}) collective-permute-start(bf16[384,512]{1,0:T(8,128)(2,1)S(1)} %get-tuple-element.65), channel_id=1, source_target_pairs={{0,0},{1,16},{2,4},{3,20},{4,32},{5,48},{6,36},{7,52},{8,40},{9,56... | collective-permute-start | bytes 1179656 | tf_op jit(solution)/shard_map/ppermute | solution.py:27
  151.5 18.3 %collective-permute-start.27 = (bf16[2,352,512]{2,1,0:T(8,128)(2,1)S(1)}, bf16[2,352,512]{2,1,0:T(8,128)(2,1)S(1)}, u32[]{:S(2)}, u32[]{:S(2)}) collective-permute-start(bf16[2,352,512]{2,1,0:T(8,128)(2,1)S(1)} %copy-done.26), channel_id=1, source_target_pairs={{0,64},{1,65},{2,66},{3,67},{4,68},{5,69},{6,70},{7,71},{8,72},{9,... | collective-permute-start | bytes 2162696 | tf_op jit(solution)/shard_map/ppermute | solution.py:27
  151.6 18.1 %copy-start.16 = (bf16[352,512]{1,0:T(8,128)(2,1)S(1)}, bf16[352,512]{1,0:T(8,128)(2,1)}, u32[]{:S(2)}) copy-start(bf16[352,512]{1,0:T(8,128)(2,1)} %get-tuple-element.54) | copy-start | bytes 1081348
  152.8 19.1 %copy-start.10 = (f32[352,384]{1,0:T(8,128)S(1)}, f32[352,384]{1,0:T(8,128)}, u32[]{:S(2)}) copy-start(f32[352,384]{1,0:T(8,128)} %get-tuple-element.62) | copy-start | bytes 1622020
  152.9 23.5 %collective-permute-start.31 = (bf16[352,512]{1,0:T(8,128)(2,1)S(1)}, bf16[352,512]{1,0:T(8,128)(2,1)S(1)}, u32[]{:S(2)}, u32[]{:S(2)}) collective-permute-start(bf16[352,512]{1,0:T(8,128)(2,1)S(1)} %fusion.5), channel_id=1, source_target_pairs={{0,64},{1,65},{2,66},{3,67},{4,68},{5,69},{6,70},{7,71},{8,72},{9,... | collective-permute-start | bytes 1081352 | tf_op jit(solution)/shard_map/ppermute | solution.py:27
  154.5 17.5 %collective-permute-start.30 = (bf16[352,384]{1,0:T(8,128)(2,1)S(1)}, bf16[352,384]{1,0:T(8,128)(2,1)S(1)}, u32[]{:S(2)}, u32[]{:S(2)}) collective-permute-start(bf16[352,384]{1,0:T(8,128)(2,1)S(1)} %fusion.11), channel_id=1, source_target_pairs={{0,48},{1,49},{2,50},{3,51},{4,52},{5,53},{6,54},{7,55},{8,56},{9,... | collective-permute-start | bytes 811016 | tf_op jit(solution)/shard_map/ppermute | solution.py:27
  169.9 6.5 %copy-start.7 = (f32[352,512]{1,0:T(8,128)S(1)}, f32[352,512]{1,0:T(8,128)}, u32[]{:S(2)}) copy-start(f32[352,512]{1,0:T(8,128)} %get-tuple-element.63) | copy-start | bytes 2162692
  169.9 10.1 %collective-permute-start.32 = (bf16[352,512]{1,0:T(8,128)(2,1)S(1)}, bf16[352,512]{1,0:T(8,128)(2,1)S(1)}, u32[]{:S(2)}, u32[]{:S(2)}) collective-permute-start(bf16[352,512]{1,0:T(8,128)(2,1)S(1)} %fusion.4), channel_id=1, source_target_pairs={{0,192},{1,193},{2,194},{3,195},{4,196},{5,197},{6,198},{7,199},{8... | collective-permute-start | bytes 1081352 | tf_op jit(solution)/shard_map/ppermute | solution.py:27
  172.0 8.0 %copy-start.6 = (f32[352,512]{1,0:T(8,128)S(1)}, f32[352,512]{1,0:T(8,128)}, u32[]{:S(2)}) copy-start(f32[352,512]{1,0:T(8,128)} %get-tuple-element.64) | copy-start | bytes 2162692
